TPU v7x, 32 devices: a whole 2x2x4 slice. The times are simulated.
32 devices in a mesh: row: 4 (over z), col: 8 (over y, x, core).
Axes of the slice: x: 2, y: 2, z: 4, core: 2. Of those that a mesh axis runs over, the one named last changes fastest.
Arguments:
- activations: bfloat16 [96, 48, 3072], P('row', None, 'col'), may hold values from -30 to 30
- cotangent: bfloat16 [96, 48, 3072], P('row', None, 'col'), may hold values from -6 to 6
- kernel: float32 [7, 7, 3072], P(None, None, 'col'), may hold values from -0.875 to 0.875
- ln_gain: float32 [3072], replicated, may hold values from 0.25 to 1.75
- ln_bias: float32 [3072], replicated, may hold values from -3 to 3
- w_expand: bfloat16 [3072, 12288], P('row', 'col'), may hold values from -0.5 to 0.5
- b_expand: float32 [12288], P('col'), may hold values from -3 to 3
- w_reduce: bfloat16 [12288, 3072], P('col', 'row'), may hold values from -0.078125 to 0.078125
- b_reduce: float32 [3072], P('col'), may hold values from -3 to 3
- layer_scale: float32 [3072], P('col'), may hold values from 0.3 to 1.5
Outputs:
- block_out: bfloat16 [96, 48, 3072], P('row', None, 'col')
- grad_input: bfloat16 [96, 48, 3072], P('row', None, 'col')
All inputs are finite; a program needn't handle non-finite values.
Results may differ from a plain program's by a relative error of at most 0.015.
Values may be sent and summed in bfloat16 or wider, within the bound.
A program may use at most 128 MiB of HBM per device.

v0:
```python
import jax
import jax.numpy as jnp
from jax import lax
from jax.sharding import PartitionSpec as P

H = 48


epsilon = 1e-06
root_half = 0.7071067811865476
density_scale = 0.3989422804014327


def spatial_mix(padded, weights, height):
    row_count = padded.shape[0] - 6
    col_count = padded.shape[1] - 6
    out_rows = jnp.arange(row_count, dtype=jnp.int32)
    running = jnp.zeros((row_count, col_count, padded.shape[2]), jnp.float32)
    for row_off in range(7):
        source = out_rows + (row_off - 3)
        inside = source // height == out_rows // height
        band = jnp.zeros_like(running)
        for col_off in range(7):
            band = (
                band
                + weights[row_off, col_off]
                * padded[row_off : row_off + row_count, col_off : col_off + col_count]
            )
        running = running + jnp.where(inside[:, None, None], band, jnp.zeros_like(band))
    return running


def gelu_slope(preact):
    cumulative = 0.5 * (1.0 + jax.scipy.special.erf(preact * root_half))
    return cumulative + preact * jnp.exp(-0.5 * preact * preact) * density_scale


def channel_sums(first_sum, second_sum):
    return lax.psum((first_sum, second_sum), "col")


def body(
    activations,
    cotangent,
    kernel,
    ln_gain,
    ln_bias,
    w_expand,
    b_expand,
    w_reduce,
    b_reduce,
    layer_scale,
):
    row_count, grid_width, narrow = activations.shape
    channels = narrow * lax.axis_size("col")
    col_start = lax.axis_index("col") * narrow
    tokens = row_count * grid_width
    flipped = kernel[::-1, ::-1]

    def mixing(source_field, weights):
        gathered = lax.all_to_all(source_field, "row", split_axis=2, concat_axis=0, tiled=True)
        per_device = gathered.shape[2]
        subset = lax.dynamic_slice_in_dim(
            weights, lax.axis_index("row") * per_device, per_device, 2
        )
        padded = jnp.pad(gathered, ((3, 3), (3, 3), (0, 0))).astype(jnp.float32)
        mixed_out = spatial_mix(padded, subset, H).astype(jnp.bfloat16)
        return lax.all_to_all(mixed_out, "row", split_axis=0, concat_axis=2, tiled=True)

    mixed_bf = mixing(activations, kernel)
    mixed_flat = lax.optimization_barrier(mixed_bf).reshape(tokens, narrow)
    expand_full, reduce_full = (
        lax.all_gather(w_expand, "row", axis=0, tiled=True),
        lax.all_gather(w_reduce, "row", axis=1, tiled=True),
    )
    local_mixed = mixed_flat.astype(jnp.float32)
    row_sum, square_sum = channel_sums(
        jnp.sum(local_mixed, 1), jnp.sum(local_mixed * local_mixed, 1)
    )
    row_mean = row_sum[:, None] / channels
    square = square_sum[:, None] / channels
    inv_std = lax.rsqrt(square - row_mean * row_mean + epsilon)
    normal_local = (local_mixed - row_mean) * inv_std
    local_gain = lax.dynamic_slice_in_dim(ln_gain, col_start, narrow)
    local_shift = lax.dynamic_slice_in_dim(ln_bias, col_start, narrow)
    normed = (normal_local * local_gain + local_shift).astype(jnp.bfloat16)
    panel = expand_full
    preact = jnp.dot(
        lax.all_gather(normed, "col", axis=1, tiled=True), panel, preferred_element_type=jnp.float32
    )
    preact = preact + b_expand
    hidden = jax.nn.gelu(preact, approximate=False).astype(jnp.bfloat16)
    panel = reduce_full
    branch_turned = lax.psum_scatter(
        lax.dot_general(
            panel, hidden, (((0,), (1,)), ((), ())), preferred_element_type=jnp.float32
        ).astype(jnp.bfloat16),
        "col",
        scatter_dimension=0,
        tiled=True,
    ).astype(jnp.float32)
    branch_out = branch_turned.T + b_reduce
    act_f = activations.astype(jnp.float32)
    block_out = (act_f + layer_scale * branch_out.reshape(row_count, grid_width, narrow)).astype(
        jnp.bfloat16
    )
    cot_f = cotangent.astype(jnp.float32)
    grad_branch = (layer_scale * cot_f).reshape(tokens, narrow).astype(jnp.bfloat16)
    panel = reduce_full
    grad_hidden = lax.dot_general(
        lax.all_gather(grad_branch, "col", axis=1, tiled=True),
        panel,
        (((1,), (1,)), ((), ())),
        preferred_element_type=jnp.float32,
    )
    grad_preact = (grad_hidden * gelu_slope(preact)).astype(jnp.bfloat16)
    panel = expand_full
    grad_turned = lax.psum_scatter(
        lax.dot_general(
            panel, grad_preact, (((1,), (1,)), ((), ())), preferred_element_type=jnp.float32
        ).astype(jnp.bfloat16),
        "col",
        scatter_dimension=0,
        tiled=True,
    ).astype(jnp.float32)
    grad_gain = grad_turned.T * local_gain
    grad_total, grad_cross = channel_sums(
        jnp.sum(grad_gain, 1), jnp.sum(grad_gain * normal_local, 1)
    )
    grad_mixed = inv_std * (
        grad_gain - grad_total[:, None] / channels - normal_local * grad_cross[:, None] / channels
    )
    grad_mixed = grad_mixed.astype(jnp.bfloat16).reshape(row_count, grid_width, narrow)
    grad_spatial = mixing(grad_mixed, flipped)
    grad_input = (cot_f + lax.optimization_barrier(grad_spatial).astype(jnp.float32)).astype(
        jnp.bfloat16
    )
    return (block_out, grad_input)


def solution(mesh):
    return jax.shard_map(
        body,
        mesh=mesh,
        in_specs=(
            P("row", None, "col"),
            P("row", None, "col"),
            P(None, None, "col"),
            P(),
            P(),
            P("row", "col"),
            P("col"),
            P("col", "row"),
            P("col"),
            P("col"),
        ),
        out_specs=(P("row", None, "col"), P("row", None, "col")),
        check_vma=False,
    )
```

profile of v0, /device:TPU:0, one launch (start us, length us, event | category | flops | bytes accessed | tf_op | source)
XLA Modules:
  0.0 832.6 jit_solution(8400221531538594373)
XLA Ops:
  7.2 0.7 all-gather.7.cloned.1.call-update
  7.9 0.4 copy-done.2
  8.3 1.4 copy.16
  9.8 4.6 reshape.134
  14.4 6.3 all-to-all-start
  20.7 0.6 fusion.178
  21.3 0.6 fusion.206
  21.9 0.6 fusion.208
  22.4 2.2 fusion.181
  24.6 46.9 %all-to-all-done = bf16[4,2,55296]{2,1,0:T(2,128)(2,1)S(1)} async-done(((bf16[4,2,55296]{2,1,0:T(2,128)(2,1)}), bf16[4,2,55296]{2,1,0:T(2,128)(2,1)S(1)}, u32[]{:S(2)}, u32[]{:S(2)}) %all-to-all-start) | async-done | bytes 884768 | tf_op jit(solution)/shard_map/all_to_all | solution.py:61
  71.5 2.4 reshape.135
  73.9 2.1 copy.24
  76.0 0.2 copy.18
  76.6 0.4 pad_convert_fusion.1
  77.4 20.2 %fusion.115 = bf16[96,48,96]{2,1,0:T(8,128)(2,1)} fusion(f32[102,54,96]{2,1,0:T(8,128)S(1)} %pad_convert_fusion.1, f32[96]{0:T(128)} %get-tuple-element.105, f32[96]{0:T(128)S(1)} %get-tuple-element.58, f32[96]{0:T(128)S(1)} %get-tuple-element.59, f32[96]{0:T(128)S(1)} %get-tuple-element.60, f32[96]{0:T(128)S(1)} %copy-done.55, f32[96]{0:T(128)S(1)} %copy-done.56, ...), kind=kLoop, calls=%fused_computation.178 | loop fusion | flops 46006272 | bytes 87608256 | tf_op jit(solution)/shard_map/convert_element_type | solution.py:67
  97.6 3.5 all-to-all-start.1
  101.2 0.8 dynamic_slice.13
  102.0 0.8 dynamic_slice.14
  102.8 54.6 %all-to-all-done.1 = bf16[96,48,96]{2,1,0:T(8,128)(2,1)S(1)} async-done(((bf16[96,48,96]{2,1,0:T(8,128)(2,1)}), bf16[96,48,96]{2,1,0:T(8,128)(2,1)S(1)}, u32[]{:S(2)}, u32[]{:S(2)}) %all-to-all-start.1) | async-done | bytes 884768 | tf_op jit(solution)/shard_map/all_to_all | solution.py:68
  157.3 0.9 copy.19
  158.2 0.8 all_to_all.59
  159.0 0.4 convert_reduce_fusion
  159.4 0.1 reduce_sum.41
  159.6 23.9 %all-reduce.3 = (f32[1152]{0:T(1024)S(1)}, f32[1152]{0:T(1024)S(1)}) all-reduce(f32[1152]{0:T(1024)S(1)} %reduce_sum.43, f32[1152]{0:T(1024)S(1)} %reduce_sum.41), channel_id=1, replica_groups=mesh['row'=4,'col'=8] {'col'}, use_global_device_ids=true, to_apply=%region_3.4 | all-reduce | flops 2304 | bytes 18432 | tf_op jit(solution)/shard_map/psum | solution.py:39
  183.5 0.6 copy-done.7
  184.1 1.3 add_convert_fusion.1
  185.5 0.7 all-gather.9.cloned.1.call-update
  186.2 0.2 reduce-scatter.7.cloned.1.call-start
  186.5 34.0 %all-gather.7.cloned.1.call-done = bf16[3072,1536]{1,0:T(8,128)(2,1)} async-done(((bf16[768,1536]{1,0:T(8,128)(2,1)}), bf16[3072,1536]{1,0:T(8,128)(2,1)}) %all-gather.7.cloned.1.call-update) | async-done | bytes 9437200 | tf_op jit(solution)/shard_map/all_gather | solution.py:73
  220.5 51.8 %all-gather.5.cloned.1.call-done = bf16[1152,3072]{1,0:T(8,128)(2,1)} async-done(((bf16[1152,384]{1,0:T(8,128)(2,1)}), bf16[1152,3072]{1,0:T(8,128)(2,1)}) %all-gather.5.cloned.1.call-update) | async-done | bytes 7077904 | tf_op jit(solution)/shard_map/all_gather | solution.py:89
  272.3 17.0 %convolution_add_fusion = f32[1152,1536]{1,0:T(8,128)} fusion(bf16[1152,3072]{1,0:T(8,128)(2,1)} %all-gather.5.cloned.1.call-done, bf16[3072,1536]{1,0:T(8,128)(2,1)} %all-gather.7.cloned.1.call-done, f32[1536]{0:T(1024)S(1)} %copy-done.95), kind=kOutput, calls=%fused_computation.7 | convolution fusion | flops 10873405440 | bytes 23599104 | tf_op jit(solution)/shard_map/dot_general | solution.py:88
  289.2 151.4 %all-gather.9.cloned.1.call-done = bf16[1536,3072]{1,0:T(8,128)(2,1)} async-done(((bf16[1536,768]{1,0:T(8,128)(2,1)}), bf16[1536,3072]{1,0:T(8,128)(2,1)}) %all-gather.9.cloned.1.call-update) | async-done | bytes 9437200 | tf_op jit(solution)/shard_map/all_gather | solution.py:74
  440.7 31.1 %fusion = bf16[3072,1152]{0,1:T(8,128)(2,1)} fusion(bf16[1536,3072]{1,0:T(8,128)(2,1)} %all-gather.9.cloned.1.call-done, f32[1152,1536]{1,0:T(8,128)} %convolution_add_fusion), kind=kOutput, calls=%fused_computation.5 | convolution fusion | flops 10990190592 | bytes 23592960 | tf_op jit(solution)/shard_map/dot_general | solution.py:95
  471.7 9.8 %copy.26 = bf16[3072,1152]{1,0:T(8,128)(2,1)} copy(bf16[3072,1152]{0,1:T(8,128)(2,1)} %fusion) | data formatting | bytes 14155776
  481.7 63.8 %reduce-scatter.7.cloned.1.call-done = bf16[384,1152]{1,0:T(8,128)(2,1)} async-done(((bf16[3072,1152]{1,0:T(8,128)(2,1)}), bf16[384,1152]{1,0:T(8,128)(2,1)}) %reduce-scatter.7.cloned.1.call-update) | async-done | bytes 884752
  545.4 1.7 copy.27
  547.2 0.1 convert_add_fusion.1
  547.3 1.7 fusion.167
  549.0 0.3 reduce-scatter.9.cloned.1.call-start
  549.3 50.0 %all-gather.11.cloned.1.call-done = bf16[1152,3072]{1,0:T(8,128)(2,1)} async-done(((bf16[1152,384]{1,0:T(8,128)(2,1)}), bf16[1152,3072]{1,0:T(8,128)(2,1)}) %all-gather.11.cloned.1.call-update) | async-done | bytes 7077904 | tf_op jit(solution)/shard_map/all_gather | solution.py:111
  599.3 18.6 %fusion.2.clone.4 = bf16[1152,1536]{1,0:T(8,128)(2,1)S(1)} fusion(bf16[1152,3072]{1,0:T(8,128)(2,1)} %all-gather.11.cloned.1.call-done, bf16[1536,3072]{1,0:T(8,128)(2,1)} %all-gather.9.cloned.1.call-done, f32[1152,1536]{1,0:T(8,128)} %convolution_add_fusion), kind=kOutput, calls=%fused_computation.8.clone.clone.clone.1 | convolution fusion | flops 10889330688 | bytes 27131904 | tf_op jit(solution)/shard_map/dot_general | solution.py:110
  618.0 15.6 %fusion.1 = bf16[3072,1152]{0,1:T(8,128)(2,1)} fusion(bf16[3072,1536]{1,0:T(8,128)(2,1)} %all-gather.7.cloned.1.call-done, bf16[1152,1536]{1,0:T(8,128)(2,1)S(1)} %fusion.2.clone.4), kind=kOutput, calls=%fused_computation.6 | convolution fusion | flops 10875174912 | bytes 20054016 | tf_op jit(solution)/shard_map/dot_general | solution.py:119
  633.6 10.3 %copy.28 = bf16[3072,1152]{1,0:T(8,128)(2,1)} copy(bf16[3072,1152]{0,1:T(8,128)(2,1)} %fusion.1) | data formatting | bytes 14155776
  644.0 65.7 %reduce-scatter.9.cloned.1.call-done = bf16[384,1152]{1,0:T(8,128)(2,1)} async-done(((bf16[3072,1152]{1,0:T(8,128)(2,1)}), bf16[384,1152]{1,0:T(8,128)(2,1)}) %reduce-scatter.9.cloned.1.call-update) | async-done | bytes 884752
  709.6 1.7 copy.29
  711.4 0.3 fusion.174
  711.7 0.7 fusion.172
  712.4 23.5 %all-reduce.2 = (f32[1152]{0:T(1024)S(1)}, f32[1152]{0:T(1024)S(1)}) all-reduce(f32[1152]{0:T(1024)S(1)} %fusion.172, f32[1152]{0:T(1024)S(1)} %fusion.174), channel_id=1, replica_groups=mesh['row'=4,'col'=8] {'col'}, use_global_device_ids=true, to_apply=%region_9.10 | all-reduce | flops 2304 | bytes 18432 | tf_op jit(solution)/shard_map/psum | solution.py:39
  735.9 1.0 fusion.171
  736.9 1.4 copy.20
  738.3 4.6 reshape.136
  743.0 4.6 all-to-all-start.2
  747.6 0.1 rev.3
  747.7 1.0 fusion.180
  748.7 18.6 %all-to-all-done.2 = bf16[4,2,55296]{2,1,0:T(2,128)(2,1)S(1)} async-done(((bf16[4,2,55296]{2,1,0:T(2,128)(2,1)}), bf16[4,2,55296]{2,1,0:T(2,128)(2,1)S(1)}, u32[]{:S(2)}, u32[]{:S(2)}) %all-to-all-start.2) | async-done | bytes 884768 | tf_op jit(solution)/shard_map/all_to_all | solution.py:61
  767.2 2.4 reshape.137
  769.6 2.1 copy.25
  771.8 0.2 copy.22
  772.3 0.4 pad_convert_fusion
  773.1 19.4 %fusion.60 = bf16[96,48,96]{2,1,0:T(8,128)(2,1)S(1)} fusion(f32[102,54,96]{2,1,0:T(8,128)S(1)} %pad_convert_fusion, f32[96]{0:T(128)} %get-tuple-element.56, f32[96]{0:T(128)S(1)} %get-tuple-element.9, f32[96]{0:T(128)S(1)} %get-tuple-element.10, f32[96]{0:T(128)S(1)} %get-tuple-element.11, f32[96]{0:T(128)S(1)} %copy-done.15, f32[96]{0:T(128)S(1)} %copy-done.16, ...), kind=kLoop, calls=%fused_computation.74 | loop fusion | flops 46006272 | bytes 87608256 | tf_op jit(solution)/shard_map/convert_element_type | solution.py:67
  792.6 29.9 %all_to_all.72 = bf16[96,48,96]{2,1,0:T(8,128)(2,1)S(1)} all-to-all(bf16[96,48,96]{2,1,0:T(8,128)(2,1)S(1)} %fusion.60), channel_id=1, replica_groups=mesh['row'=4,'col'=8] {'row'}, dimensions={0} | all-to-all | bytes 1769472 | tf_op jit(solution)/shard_map/all_to_all | solution.py:68
  822.4 0.9 copy.23
  823.4 0.8 all_to_all.67
  824.1 1.1 fusion.168
  (201 shorter events, 0.7 us)
Async XLA Ops:
  7.2 1.2 copy-start.2
  7.2 213.3 %all-gather.7.cloned.1.call-start = ((), (), s32[]{:S(2)}) async-start(), calls=%async_computation.7 | async-start | bytes 11796480 | tf_op jit(solution)/shard_map/all_gather | solution.py:73
  14.4 57.1 %all-to-all-start = ((bf16[4,2,55296]{2,1,0:T(2,128)(2,1)}), bf16[4,2,55296]{2,1,0:T(2,128)(2,1)S(1)}, u32[]{:S(2)}, u32[]{:S(2)}) async-start(bf16[4,2,55296]{2,1,0:T(2,128)(2,1)} %reshape.134), calls=%async_computation | async-start | bytes 1769472 | tf_op jit(solution)/shard_map/all_to_all | solution.py:61
  76.2 0.8 copy-start.55
  76.2 0.8 copy-start.56
  76.2 0.8 copy-start.57
  76.2 0.8 copy-start.58
  76.2 0.8 copy-start.59
  76.3 0.8 copy-start.60
  76.3 0.8 copy-start.61
  76.3 0.8 copy-start.62
  76.3 0.8 copy-start.63
  76.3 0.8 copy-start.64
  76.3 0.8 copy-start.65
  76.3 0.8 copy-start.66
  76.3 0.8 copy-start.67
  76.3 0.8 copy-start.68
  76.3 0.8 copy-start.69
  76.4 0.8 copy-start.70
  76.4 0.8 copy-start.71
  76.4 0.8 copy-start.72
  76.4 0.8 copy-start.73
  76.4 0.8 copy-start.74
  76.4 0.8 copy-start.75
  76.4 0.8 copy-start.76
  76.4 0.8 copy-start.77
  76.4 0.8 copy-start.78
  76.4 0.8 copy-start.79
  76.5 0.8 copy-start.80
  76.5 0.8 copy-start.81
  76.5 0.8 copy-start.82
  76.5 0.8 copy-start.83
  76.5 0.8 copy-start.84
  76.5 0.8 copy-start.85
  76.5 0.8 copy-start.86
  76.5 0.8 copy-start.87
  76.5 0.8 copy-start.88
  76.5 0.8 copy-start.89
  76.6 0.8 copy-start.90
  76.6 0.8 copy-start.91
  76.6 0.8 copy-start.92
  76.6 0.8 copy-start.93
  76.6 0.8 copy-start.94
  97.6 59.7 %all-to-all-start.1 = ((bf16[96,48,96]{2,1,0:T(8,128)(2,1)}), bf16[96,48,96]{2,1,0:T(8,128)(2,1)S(1)}, u32[]{:S(2)}, u32[]{:S(2)}) async-start(bf16[96,48,96]{2,1,0:T(8,128)(2,1)} %fusion.115), calls=%async_computation.1 | async-start | bytes 2359296 | tf_op jit(solution)/shard_map/all_to_all | solution.py:68
  101.1 171.1 %all-gather.5.cloned.1.call-start = ((), (), s32[]{:S(2)}) async-start(), calls=%async_computation.6 | async-start | bytes 7962624 | tf_op jit(solution)/shard_map/all_gather | solution.py:89
  102.0 81.6 %copy-start.11 = (f32[384]{0:T(512)}, f32[384]{0:T(512)S(1)}, u32[]{:S(2)}) copy-start(f32[384]{0:T(512)S(1)} %dynamic_slice.13) | copy-start | bytes 4612
  159.0 27.2 %copy-start = (bf16[24,48,384]{2,1,0:T(8,128)(2,1)}, bf16[24,48,384]{2,1,0:T(8,128)(2,1)S(1)}, u32[]{:S(2)}) copy-start(bf16[24,48,384]{2,1,0:T(8,128)(2,1)S(1)} %all_to_all.59) | copy-start | bytes 2654212
  184.1 88.1 %copy-start.95 = (f32[1536]{0:T(1024)S(1)}, f32[1536]{0:T(1024)}, u32[]{:S(2)}) copy-start(f32[1536]{0:T(1024)} %param.16) | copy-start | bytes 18436
  185.5 255.2 %all-gather.9.cloned.1.call-start = ((), (), s32[]{:S(2)}) async-start(), calls=%async_computation.8 | async-start | bytes 11796480 | tf_op jit(solution)/shard_map/all_gather | solution.py:74
  186.2 359.2 %reduce-scatter.7.cloned.1.call-start = ((), (), s32[]{:S(2)}) async-start(), calls=%async_computation.10 | async-start | bytes 7962624
  481.5 65.6 %copy-start.14 = (f32[384]{0:T(512)S(1)}, f32[384]{0:T(512)}, u32[]{:S(2)}) copy-start(f32[384]{0:T(512)} %param.18) | copy-start | bytes 4612
  481.6 65.7 %copy-start.3 = (bf16[24,48,384]{2,1,0:T(8,128)(2,1)S(1)}, bf16[24,48,384]{2,1,0:T(8,128)(2,1)}, u32[]{:S(2)}) copy-start(bf16[24,48,384]{2,1,0:T(8,128)(2,1)} %param.10) | copy-start | bytes 2654212
  481.6 65.7 %copy-start.4 = (bf16[24,48,384]{2,1,0:T(8,128)(2,1)S(1)}, bf16[24,48,384]{2,1,0:T(8,128)(2,1)}, u32[]{:S(2)}) copy-start(bf16[24,48,384]{2,1,0:T(8,128)(2,1)} %param.11) | copy-start | bytes 2654212
  481.6 65.7 %copy-start.13 = (f32[384]{0:T(512)S(1)}, f32[384]{0:T(512)}, u32[]{:S(2)}) copy-start(f32[384]{0:T(512)} %param.19) | copy-start | bytes 4612
  481.6 117.7 %all-gather.11.cloned.1.call-start = ((), (), s32[]{:S(2)}) async-start(), calls=%async_computation.9 | async-start | bytes 7962624 | tf_op jit(solution)/shard_map/all_gather | solution.py:111
  549.0 160.6 %reduce-scatter.9.cloned.1.call-start = ((), (), s32[]{:S(2)}) async-start(), calls=%async_computation.11 | async-start | bytes 7962624
  643.9 67.5 %copy-start.12 = (f32[384]{0:T(512)S(1)}, f32[384]{0:T(512)}, u32[]{:S(2)}) copy-start(f32[384]{0:T(512)} %copy-done.11) | copy-start | bytes 4612
  643.9 67.7 %copy-start.1 = (bf16[24,48,384]{2,1,0:T(8,128)(2,1)S(1)}, bf16[24,48,384]{2,1,0:T(8,128)(2,1)}, u32[]{:S(2)}) copy-start(bf16[24,48,384]{2,1,0:T(8,128)(2,1)} %copy-done) | copy-start | bytes 2654212
  643.9 67.7 %copy-start.8 = (f32[1152]{0:T(1024)S(1)}, f32[1152]{0:T(1024)}, u32[]{:S(2)}) copy-start(f32[1152]{0:T(1024)} %copy-done.7) | copy-start | bytes 13828
  643.9 67.7 %copy-start.10 = (f32[1152]{0:T(1024)S(1)}, f32[1152]{0:T(1024)}, u32[]{:S(2)}) copy-start(f32[1152]{0:T(1024)} %copy-done.9) | copy-start | bytes 13828
  738.3 9.2 %copy-start.6 = (f32[7,7,384]{2,1,0:T(8,128)S(1)}, f32[7,7,384]{2,1,0:T(8,128)}, u32[]{:S(2)}) copy-start(f32[7,7,384]{2,1,0:T(8,128)} %param.12) | copy-start | bytes 225796
  743.0 24.3 %all-to-all-start.2 = ((bf16[4,2,55296]{2,1,0:T(2,128)(2,1)}), bf16[4,2,55296]{2,1,0:T(2,128)(2,1)S(1)}, u32[]{:S(2)}, u32[]{:S(2)}) async-start(bf16[4,2,55296]{2,1,0:T(2,128)(2,1)} %reshape.136), calls=%async_computation.2 | async-start | bytes 1769472 | tf_op jit(solution)/shard_map/all_to_all | solution.py:61
  771.9 0.8 copy-start.15
  822.4 1.7 copy-start.5
  (41 other events, 32.5 us)
Sparse Core Ops, SparseCore 0:
  9.6 210.8 all-gather.6
  222.9 49.2 all-gather.4
  273.8 166.7 all-gather.8
  481.7 63.6 reduce-scatter.6
  549.2 50.1 all-gather.10
  644.0 65.5 reduce-scatter.8
where the time goes:
time: 841 us; the launch traced here: 833 us
  waiting for transfers between devices  538 us (64%)
  matrix products  82.3 us (10%)
  blocking collectives  77.3 us (9%)
  local copies, waits for them, and re-layouts  54.9 us (7%)
  other arithmetic  48.8 us (6%)
  between operations  16.2 us (2%)
  starting transfers between devices  15.1 us (2%)
    all_gather x1, waiting for transfers between devices, body(): lax.all_gather(w_reduce, 'row', axis=1, tiled=True)  151 us
    unnamed x8, waiting for transfers between devices  131 us
    all_to_all x2, waiting for transfers between devices, mixing(): lax.all_to_all(source_field, 'row', split_axis=2, concat_axis=0, tiled=True)  65.4 us
    all_to_all x1, waiting for transfers between devices, mixing(): lax.all_to_all(mixed_out, 'row', split_axis=0, concat_axis=2, tiled=True)  54.6 us
    all_gather x1, waiting for transfers between devices, body(): lax.all_gather(normed, 'col', axis=1, tiled=True)  51.8 us
    all_gather x1, waiting for transfers between devices, body(): lax.all_gather(grad_branch, 'col', axis=1, tiled=True)  50 us
    psum x2, blocking collectives, channel_sums(): return lax.psum((first_sum, second_sum), 'col')  47.4 us
    unnamed x201, local copies, waits for them, and re-layouts  40.5 us
  transfers between devices with their start and end apart: 9, of which 9 were waited for; matrix products, arithmetic and copies ran while one was open for 7% of the time, Pallas kernels for 0%

commit v1 on v0

v1 whole, which is shorter than its diff:
```python
import functools

import jax
import jax.numpy as jnp
from jax import lax
from jax.experimental import pallas as pl
from jax.experimental.pallas import tpu as pltpu
from jax.sharding import PartitionSpec as P

H = 48
LANES = 128
CHUNKS = 2

epsilon = 1e-06
root_half = 0.7071067811865476
density_scale = 0.3989422804014327


def conv_kernel(flip, add, x_ref, top_ref, bottom_ref, k_ref, *rest):
    if add:
        add_ref, o_ref, field = rest
    else:
        o_ref, field = rest
    rows, width, lanes = x_ref.shape
    field[...] = jnp.zeros_like(field)
    field[0:3, 8 : 8 + width, :] = top_ref[...].astype(jnp.float32)
    field[3 : 3 + rows, 8 : 8 + width, :] = x_ref[...].astype(jnp.float32)
    field[3 + rows : 6 + rows, 8 : 8 + width, :] = bottom_ref[...].astype(jnp.float32)

    @pl.loop(0, rows)
    def _(r):
        total = jnp.zeros((width, lanes), jnp.float32)
        for a in range(7):
            for b in range(7):
                weight = k_ref[6 - a, 6 - b] if flip else k_ref[a, b]
                total += weight[None, :] * field[r + a, 5 + b : 5 + b + width, :]
        mixed = total.astype(jnp.bfloat16)
        if add:
            mixed = (add_ref[r].astype(jnp.float32) + mixed.astype(jnp.float32)).astype(
                jnp.bfloat16
            )
        o_ref[r] = mixed


def depthwise(field, top, bottom, kernel, flip, add=None):
    rows, width, channels = field.shape
    lanes = LANES if channels % LANES == 0 else channels
    block = lambda n: pl.BlockSpec((n, width, lanes), lambda i: (0, 0, i))
    operands = [field, top, bottom, kernel]
    specs = [block(rows), block(3), block(3), pl.BlockSpec((7, 7, lanes), lambda i: (0, 0, i))]
    if add is not None:
        operands.append(add)
        specs.append(block(rows))
    return pl.pallas_call(
        functools.partial(conv_kernel, flip, add is not None),
        out_shape=jax.ShapeDtypeStruct(field.shape, jnp.bfloat16),
        grid=(channels // lanes,),
        in_specs=specs,
        out_specs=block(rows),
        scratch_shapes=[pltpu.VMEM((rows + 6, width + 16, lanes), jnp.float32)],
        compiler_params=pltpu.CompilerParams(vmem_limit_bytes=32 * 2**20),
        cost_estimate=pl.CostEstimate(
            flops=98 * rows * width * channels,
            bytes_accessed=6 * rows * width * channels,
            transcendentals=0,
        ),
        name="depthwise_flipped" if flip else "depthwise",
    )(*operands)


def halo(field):
    rows = field.shape[0]
    per_image = H // rows
    count = lax.axis_size("row")
    down = [(i, i + 1) for i in range(count - 1) if (i + 1) % per_image]
    up = [(j, i) for i, j in down]
    return lax.ppermute(field[-3:], "row", down), lax.ppermute(field[:3], "row", up)


def swap(value, distance):
    count = lax.axis_size("col")
    return lax.ppermute(value, "col", [(i, i ^ distance) for i in range(count)])


def gather_columns(piece):
    count = lax.axis_size("col")
    me = lax.axis_index("col")
    tokens, narrow = piece.shape
    out = jnp.zeros((tokens, narrow * count), piece.dtype)
    for distance in range(0, count, 2):
        arrived = swap(piece, distance) if distance else piece
        other = swap(arrived, 1)
        out = lax.dynamic_update_slice(out, arrived, (0, (me ^ distance) * narrow))
        out = lax.dynamic_update_slice(out, other, (0, (me ^ distance ^ 1) * narrow))
    return out


def scatter_columns(part):
    count = lax.axis_size("col")
    me = lax.axis_index("col")
    order = list(range(2, count, 2)) + [0]
    arrived = {d: swap(part(me ^ d ^ 1).astype(jnp.bfloat16), 1) for d in order}
    total = None
    pieces = []
    for d in order:
        pair = part(me ^ d) + arrived[d].astype(jnp.float32)
        pieces.append(swap(pair.astype(jnp.bfloat16), d).astype(jnp.float32) if d else pair)
    total = pieces[-1]
    for piece in pieces[:-1]:
        total = total + piece
    return total


def body(
    activations,
    cotangent,
    kernel,
    ln_gain,
    ln_bias,
    w_expand,
    b_expand,
    w_reduce,
    b_reduce,
    layer_scale,
):
    row_count, grid_width, narrow = activations.shape
    channels = narrow * lax.axis_size("col")
    col_start = lax.axis_index("col") * narrow
    tokens = row_count * grid_width
    units = w_expand.shape[1]
    step = units // CHUNKS
    dot = functools.partial(jnp.dot, preferred_element_type=jnp.float32)

    expand_full = lax.all_gather(w_expand, "row", axis=0, tiled=True)
    reduce_full = [
        lax.all_gather(w_reduce[i * step : (i + 1) * step], "row", axis=1, tiled=True)
        for i in range(CHUNKS)
    ]

    top, bottom = halo(activations)
    mixed_bf = depthwise(activations, top, bottom, kernel, False)
    local_mixed = mixed_bf.reshape(tokens, narrow).astype(jnp.float32)
    row_sum, square_sum = lax.psum(
        (jnp.sum(local_mixed, 1), jnp.sum(local_mixed * local_mixed, 1)), "col"
    )
    row_mean = row_sum[:, None] / channels
    square = square_sum[:, None] / channels
    inv_std = lax.rsqrt(square - row_mean * row_mean + epsilon)
    normal_local = (local_mixed - row_mean) * inv_std
    local_gain = lax.dynamic_slice_in_dim(ln_gain, col_start, narrow)
    local_shift = lax.dynamic_slice_in_dim(ln_bias, col_start, narrow)
    normed = (normal_local * local_gain + local_shift).astype(jnp.bfloat16)
    normed_full = gather_columns(normed)

    cot_f = cotangent.astype(jnp.float32)
    grad_branch = (layer_scale * cot_f).reshape(tokens, narrow).astype(jnp.bfloat16)
    grad_full = gather_columns(grad_branch)

    preact = dot(normed_full, expand_full) + b_expand
    cumulative = 0.5 * (1.0 + lax.erf(preact * root_half))
    hidden = (preact * cumulative).astype(jnp.bfloat16)
    slope = cumulative + preact * jnp.exp(-0.5 * preact * preact) * density_scale

    grad_parts = []
    for i in range(CHUNKS):
        grad_hidden = lax.dot_general(
            grad_full, reduce_full[i], (((1,), (1,)), ((), ())), preferred_element_type=jnp.float32
        )
        grad_parts.append(
            (grad_hidden * slope[:, i * step : (i + 1) * step]).astype(jnp.bfloat16)
        )
    grad_preact = jnp.concatenate(grad_parts, 1)

    def grad_part(owner):
        rows = lax.dynamic_slice_in_dim(expand_full, owner * narrow, narrow, 0)
        return lax.dot_general(
            grad_preact, rows, (((1,), (1,)), ((), ())), preferred_element_type=jnp.float32
        )

    def branch_part(owner):
        total = 0.0
        for i in range(CHUNKS):
            block = lax.dynamic_slice_in_dim(reduce_full[i], owner * narrow, narrow, 1)
            total = total + dot(hidden[:, i * step : (i + 1) * step], block)
        return total

    grad_gain = scatter_columns(grad_part) * local_gain
    branch_out = scatter_columns(branch_part) + b_reduce

    grad_sums = jnp.stack([jnp.sum(grad_gain, 1), jnp.sum(grad_gain * normal_local, 1)])
    every_sum = grad_sums
    for distance in range(1, lax.axis_size("col")):
        every_sum = every_sum + swap(grad_sums, distance)
    grad_total, grad_cross = every_sum[0], every_sum[1]
    grad_mixed = inv_std * (
        grad_gain - grad_total[:, None] / channels - normal_local * grad_cross[:, None] / channels
    )
    grad_mixed = grad_mixed.astype(jnp.bfloat16).reshape(row_count, grid_width, narrow)
    top, bottom = halo(grad_mixed)
    grad_input = depthwise(grad_mixed, top, bottom, kernel, True, cotangent)

    act_f = activations.astype(jnp.float32)
    block_out = (act_f + layer_scale * branch_out.reshape(row_count, grid_width, narrow)).astype(
        jnp.bfloat16
    )
    return (block_out, grad_input)


def solution(mesh):
    return jax.shard_map(
        body,
        mesh=mesh,
        in_specs=(
            P("row", None, "col"),
            P("row", None, "col"),
            P(None, None, "col"),
            P(),
            P(),
            P("row", "col"),
            P("col"),
            P("col", "row"),
            P("col"),
            P("col"),
        ),
        out_specs=(P("row", None, "col"), P("row", None, "col")),
        check_vma=False,
    )
```

time: 841 us -> 577 us (0.69)
  waiting for transfers between devices: 538 us -> 368 us
  blocking collectives: 77.3 us -> 24.2 us
  other arithmetic: 48.8 us -> 6.08 us
  local copies, waits for them, and re-layouts: 54.9 us -> 25.2 us
  Pallas kernels: 0 us -> 20.9 us
  starting transfers between devices: 15.1 us -> 33.4 us
    ppermute x0 -> x39, waiting for transfers between devices: none -> 151 us  [the longest x35 142 us: swap(): return lax.ppermute(value, 'col', [(i, i ^ distance) for i in range(count)])]
    unnamed x8 -> x3, waiting for transfers between devices: 131 us -> 0.71 us
    all_to_all x3 -> x0, waiting for transfers between devices: 120 us -> none  [the longest x2 65.4 us: mixing(): lax.all_to_all(source_field, 'row', split_axis=2, concat_axis=0, tiled=True)]
    all_gather x4 -> x3, waiting for transfers between devices: 287 us -> 217 us  [the longest x2 155 us: body(): lax.all_gather(w_reduce[i * step:(i + 1) * step], 'row', axis=1, tiled=True)]
    convert_element_type x6 -> x0, other arithmetic: 42.9 us -> none  [the longest x2 39.6 us: mixing(): mixed_out = spatial_mix(padded, subset, H).astype(jnp.bfloat16)]
    unnamed x201 -> x28, local copies, waits for them, and re-layouts: 40.5 us -> 0.07 us
    ppermute x0 -> x39, starting transfers between devices: none -> 33.3 us  [the longest x35 24.5 us: swap(): return lax.ppermute(value, 'col', [(i, i ^ distance) for i in range(count)])]
    all_to_all x1 -> x0, blocking collectives: 29.9 us -> none  [mixing(): lax.all_to_all(mixed_out, 'row', split_axis=0, concat_axis=2, tiled=True)]
  transfers between devices with their start and end apart: 9 -> 42, of which waited for: 9 -> 19; matrix products, arithmetic and copies ran while one was open for 7% -> 14% of each run, Pallas kernels for 0% -> 2%
where the time goes in v1:
time: 577 us; the launch traced here: 570 us
  waiting for transfers between devices  368 us (64%)
  matrix products  77.8 us (13%)
  starting transfers between devices  33.4 us (6%)
  local copies, waits for them, and re-layouts  25.2 us (4%)
  blocking collectives  24.2 us (4%)
  Pallas kernels  20.9 us (4%)
  between operations  14.5 us (3%)
  other arithmetic  6.08 us (1%)
    all_gather x2, waiting for transfers between devices, body(): lax.all_gather(w_reduce[i * step:(i + 1) * step], 'row', axis=1, tiled=True)  155 us
    ppermute x35, waiting for transfers between devices, swap(): return lax.ppermute(value, 'col', [(i, i ^ distance) for i in range(count)])  142 us
    all_gather x1, waiting for transfers between devices, body(): expand_full = lax.all_gather(w_expand, 'row', axis=0, tiled=True)  62.2 us
    ppermute x35, starting transfers between devices, swap(): return lax.ppermute(value, 'col', [(i, i ^ distance) for i in range(count)])  24.5 us
    dot_general x16, matrix products, branch_part(): total = total + dot(hidden[:, i * step:(i + 1) * step], block)  24.3 us
    psum x1, blocking collectives, body(): lax.psum((jnp.sum(local_mixed, 1), jnp.sum(local_mixed * local_mixed, 1))...  24.2 us
    pallas_call x2, Pallas kernels, depthwise(): pl.pallas_call(functools.partial(conv_kernel, flip, add is not None), out...  20.9 us
    dot_general x1, matrix products, body(): preact = dot(normed_full, expand_full) + b_expand  20 us
  transfers between devices with their start and end apart: 42, of which 19 were waited for; matrix products, arithmetic and copies ran while one was open for 14% of the time, Pallas kernels for 2%

profile of v1, /device:TPU:0, one launch (start us, length us, event | category | flops | bytes accessed | tf_op | source)
XLA Modules:
  0.0 570.5 jit_solution(9409257029238719783)
XLA Ops:
  8.0 3.2 fusion.101
  11.3 4.9 collective-permute-start
  16.3 1.3 collective-permute-start.1
  19.2 3.8 collective-permute-done.1.bottom_ref
  22.9 9.9 %depthwise.1 = bf16[24,48,384]{2,1,0:T(8,128)(2,1)S(1)} custom-call(bf16[24,48,384]{2,1,0:T(8,128)(2,1)S(1)} %copy-done, bf16[3,48,384]{2,1,0:T(8,128)(2,1)S(1)} %collective-permute-done.top_ref, bf16[3,48,384]{2,1,0:T(8,128)(2,1)S(1)} %collective-permute-done.1.bottom_ref, f32[7,7,384]{2,1,0:T(8,128)S(1)} %copy-done.2), custom_call_target="tpu_custom_call" | custom-call | flops 43352064 | bytes 2654208 | tf_op jit(solution)/shard_map/depthwise/pallas_call | solution.py:54
  33.4 24.2 %all-reduce = (f32[1152]{0:T(1024)S(1)}, f32[1152]{0:T(1024)S(1)}) all-reduce(f32[1152]{0:T(1024)S(1)} %reduce_sum.43, f32[1152]{0:T(1024)S(1)} %reduce_sum.41), channel_id=1, replica_groups=mesh['row'=4,'col'=8] {'col'}, use_global_device_ids=true, to_apply=%region_3.0 | all-reduce | flops 2304 | bytes 18432 | tf_op jit(solution)/shard_map/psum | solution.py:143
  57.7 3.7 broadcast.29.clone
  61.4 1.4 constant_dynamic-update-slice_fusion.15
  62.9 1.3 collective-permute-start.5
  64.1 2.2 collective-permute-start.7
  66.4 19.2 %collective-permute-done.3 = bf16[1152,384]{1,0:T(8,128)(2,1)} collective-permute-done((bf16[1152,384]{1,0:T(8,128)(2,1)S(1)}, bf16[1152,384]{1,0:T(8,128)(2,1)}, u32[]{:S(2)}, u32[]{:S(2)}) %collective-permute-start.3) | collective-permute-done | bytes 884768 | tf_op jit(solution)/shard_map/ppermute | solution.py:82
  85.6 17.3 %collective-permute-done.5 = bf16[1152,384]{1,0:T(8,128)(2,1)} collective-permute-done((bf16[1152,384]{1,0:T(8,128)(2,1)S(1)}, bf16[1152,384]{1,0:T(8,128)(2,1)}, u32[]{:S(2)}, u32[]{:S(2)}) %collective-permute-start.5) | collective-permute-done | bytes 884768 | tf_op jit(solution)/shard_map/ppermute | solution.py:82
  103.3 2.2 constant_dynamic-update-slice_fusion.14
  105.6 2.3 constant_dynamic-update-slice_fusion.13
  107.8 2.2 constant_dynamic-update-slice_fusion.12
  110.1 2.3 constant_dynamic-update-slice_fusion.11
  113.4 2.4 constant_dynamic-update-slice_fusion.9
  116.9 62.2 %all-gather.4.cloned.1.call-done = bf16[3072,1536]{1,0:T(8,128)(2,1)} async-done(((bf16[768,1536]{1,0:T(8,128)(2,1)}), bf16[3072,1536]{1,0:T(8,128)(2,1)}) %all-gather.4.cloned.1.call-update) | async-done | bytes 9437200 | tf_op jit(solution)/shard_map/all_gather | solution.py:134
  179.1 20.0 %fusion.3 = (f32[1152,1536]{1,0:T(8,128)}, bf16[1152,1536]{1,0:T(8,128)(2,1)}) fusion(f32[1536]{0:T(1024)S(1)} %copy-done.6, bf16[1152,3072]{1,0:T(8,128)(2,1)} %constant_dynamic-update-slice_fusion.8, bf16[3072,1536]{1,0:T(8,128)(2,1)} %all-gather.4.cloned.1.call-done), kind=kOutput, calls=%fused_computation.5 | convolution fusion | flops 10891100160 | bytes 27138048 | tf_op jit(solution)/shard_map/dot_general | solution.py:159
  199.1 69.2 %all-gather.6.cloned.1.call-done = bf16[768,3072]{1,0:T(8,128)(2,1)} async-done(((bf16[768,768]{1,0:T(8,128)(2,1)}), bf16[768,3072]{1,0:T(8,128)(2,1)}) %all-gather.6.cloned.1.call-update) | async-done | bytes 4718608 | tf_op jit(solution)/shard_map/all_gather | solution.py:136
  268.3 4.0 fusion.30
  272.2 85.5 %all-gather.8.cloned.1.call-done = bf16[768,3072]{1,0:T(8,128)(2,1)} async-done(((bf16[768,768]{1,0:T(8,128)(2,1)}), bf16[768,3072]{1,0:T(8,128)(2,1)}) %all-gather.8.cloned.1.call-update) | async-done | bytes 4718608 | tf_op jit(solution)/shard_map/all_gather | solution.py:136
  357.7 3.4 fusion.9
  361.3 2.3 fusion.38
  363.6 1.1 fusion.8
  366.6 1.1 fusion.7
  368.9 1.1 fusion.6
  372.8 1.1 fusion.51
  373.9 1.1 add_convert_fusion.4
  375.0 2.4 collective-permute-start.15
  377.5 1.1 add_convert_fusion.5
  379.2 1.4 add_convert_fusion.6
  382.3 1.2 convolution_add_fusion.8
  383.5 15.0 %collective-permute-done.15 = bf16[1152,384]{1,0:T(8,128)(2,1)S(1)} collective-permute-done((bf16[1152,384]{1,0:T(8,128)(2,1)S(1)}, bf16[1152,384]{1,0:T(8,128)(2,1)S(1)}, u32[]{:S(2)}, u32[]{:S(2)}) %collective-permute-start.15) | collective-permute-done | bytes 884768 | tf_op jit(solution)/shard_map/ppermute | solution.py:82
  398.5 18.0 %collective-permute-done.13 = bf16[1152,384]{1,0:T(8,128)(2,1)S(1)} collective-permute-done((bf16[1152,384]{1,0:T(8,128)(2,1)S(1)}, bf16[1152,384]{1,0:T(8,128)(2,1)S(1)}, u32[]{:S(2)}, u32[]{:S(2)}) %collective-permute-start.13) | collective-permute-done | bytes 884768 | tf_op jit(solution)/shard_map/ppermute | solution.py:82
  417.2 1.3 multiply_convert_fusion.2
  418.5 1.5 collective-permute-start.17
  420.0 1.4 collective-permute-start.19
  422.0 19.0 %collective-permute-done.17 = bf16[1152,384]{1,0:T(8,128)(2,1)S(1)} collective-permute-done((bf16[1152,384]{1,0:T(8,128)(2,1)S(1)}, bf16[1152,384]{1,0:T(8,128)(2,1)S(1)}, u32[]{:S(2)}, u32[]{:S(2)}) %collective-permute-start.17) | collective-permute-done | bytes 884768 | tf_op jit(solution)/shard_map/ppermute | solution.py:82
  442.2 18.0 %collective-permute-done.19 = bf16[1152,384]{1,0:T(8,128)(2,1)S(1)} collective-permute-done((bf16[1152,384]{1,0:T(8,128)(2,1)S(1)}, bf16[1152,384]{1,0:T(8,128)(2,1)S(1)}, u32[]{:S(2)}, u32[]{:S(2)}) %collective-permute-start.19) | collective-permute-done | bytes 884768 | tf_op jit(solution)/shard_map/ppermute | solution.py:82
  464.1 7.6 %fusion.5 = bf16[1152,768]{1,0:T(8,128)(2,1)S(1)} fusion(f32[1152,1536]{1,0:T(8,128)} %get-tuple-element.11, bf16[1152,3072]{1,0:T(8,128)(2,1)S(1)} %constant_dynamic-update-slice_fusion, bf16[768,3072]{1,0:T(8,128)(2,1)S(1)} %bitcast.31), kind=kOutput, calls=%fused_computation.12 | convolution fusion | flops 5437587456 | bytes 17104896 | tf_op jit(solution)/shard_map/dot_general | solution.py:166
  471.7 9.3 %fusion.4 = bf16[1152,768]{1,0:T(8,128)(2,1)S(1)} fusion(f32[1152,1536]{1,0:T(8,128)} %get-tuple-element.11, bf16[1152,3072]{1,0:T(8,128)(2,1)S(1)} %constant_dynamic-update-slice_fusion, bf16[768,3072]{1,0:T(8,128)(2,1)} %all-gather.6.cloned.1.call-done), kind=kOutput, calls=%fused_computation.11 | convolution fusion | flops 5437587456 | bytes 17104896 | tf_op jit(solution)/shard_map/dot_general | solution.py:166
  481.1 2.0 convolution_convert_fusion
  483.3 2.0 convolution_convert_fusion.1
  485.8 2.0 convolution_convert_fusion.2
  488.1 2.0 convolution_convert_fusion.3
  490.5 2.1 add_convert_fusion
  492.6 1.5 collective-permute-start.29
  494.2 2.1 add_convert_fusion.1
  496.3 2.1 add_convert_fusion.2
  498.4 2.0 collective-permute-start.25
  500.4 2.2 fusion.27
  502.7 13.4 %collective-permute-done.29 = bf16[1152,384]{1,0:T(8,128)(2,1)S(1)} collective-permute-done((bf16[1152,384]{1,0:T(8,128)(2,1)S(1)}, bf16[1152,384]{1,0:T(8,128)(2,1)S(1)}, u32[]{:S(2)}, u32[]{:S(2)}) %collective-permute-start.29) | collective-permute-done | bytes 884768 | tf_op jit(solution)/shard_map/ppermute | solution.py:82
  516.1 18.1 %collective-permute-done.27 = bf16[1152,384]{1,0:T(8,128)(2,1)S(1)} collective-permute-done((bf16[1152,384]{1,0:T(8,128)(2,1)S(1)}, bf16[1152,384]{1,0:T(8,128)(2,1)S(1)}, u32[]{:S(2)}, u32[]{:S(2)}) %collective-permute-start.27) | collective-permute-done | bytes 884768 | tf_op jit(solution)/shard_map/ppermute | solution.py:82
  534.3 1.3 fusion.100
  535.6 1.1 collective-permute-start.36
  536.7 1.4 collective-permute-start.35
  538.2 1.3 collective-permute-start.34
  540.1 1.5 collective-permute-start.31
  541.9 1.2 collective-permute-done.33
  544.9 1.3 collective-permute-start.37
  546.2 1.3 collective-permute-start.38
  548.5 4.3 collective-permute-done.38.bottom_ref
  552.8 10.9 %depthwise_flipped.1 = bf16[24,48,384]{2,1,0:T(8,128)(2,1)} custom-call(bf16[24,48,384]{2,1,0:T(8,128)(2,1)S(1)} %bitcast.21, bf16[3,48,384]{2,1,0:T(8,128)(2,1)S(1)} %collective-permute-done.37.top_ref, bf16[3,48,384]{2,1,0:T(8,128)(2,1)S(1)} %collective-permute-done.38.bottom_ref, f32[7,7,384]{2,1,0:T(8,128)S(1)} %copy-done.2, ...), custom_call_target="tpu_custom_call" | custom-call | flops 43352064 | bytes 2654208 | tf_op jit(solution)/shard_map/depthwise_flipped/pallas_call | solution.py:54
  (120 shorter events, 25.3 us)
Async XLA Ops:
  7.2 171.9 %all-gather.4.cloned.1.call-start = ((), (), s32[]{:S(2)}) async-start(), calls=%async_computation | async-start | bytes 11796480 | tf_op jit(solution)/shard_map/all_gather | solution.py:134
  7.9 3.4 copy-start
  7.9 15.0 %copy-start.2 = (f32[7,7,384]{2,1,0:T(8,128)S(1)}, f32[7,7,384]{2,1,0:T(8,128)}, u32[]{:S(2)}) copy-start(f32[7,7,384]{2,1,0:T(8,128)} %k_ref.3) | copy-start | bytes 225796
  7.9 260.4 %all-gather.6.cloned.1.call-start = ((), (), s32[]{:S(2)}) async-start(), calls=%async_computation.1 | async-start | bytes 5898240 | tf_op jit(solution)/shard_map/all_gather | solution.py:136
  11.2 346.5 %all-gather.8.cloned.1.call-start = ((), (), s32[]{:S(2)}) async-start(), calls=%async_computation.2 | async-start | bytes 5898240 | tf_op jit(solution)/shard_map/all_gather | solution.py:136
  11.3 7.8 %collective-permute-start = (bf16[3,48,384]{2,1,0:T(8,128)(2,1)S(1)}, bf16[3,48,384]{2,1,0:T(8,128)(2,1)S(1)}, u32[]{:S(2)}, u32[]{:S(2)}) collective-permute-start(bf16[3,48,384]{2,1,0:T(8,128)(2,1)S(1)} %get-tuple-element.18), channel_id=1, source_target_pairs={{0,8},{16,24},{1,9},{17,25},{2,10},{18,26},{3,11},{19,27},{4,12},{... | collective-permute-start | bytes 331784 | tf_op jit(solution)/shard_map/ppermute | solution.py:77
  16.3 6.6 %collective-permute-start.1 = (bf16[3,48,384]{2,1,0:T(8,128)(2,1)S(1)}, bf16[3,48,384]{2,1,0:T(8,128)(2,1)S(1)}, u32[]{:S(2)}, u32[]{:S(2)}) collective-permute-start(bf16[3,48,384]{2,1,0:T(8,128)(2,1)S(1)} %get-tuple-element.17), channel_id=1, source_target_pairs={{8,0},{24,16},{9,1},{25,17},{10,2},{26,18},{11,3},{27,19},{12,4},{... | collective-permute-start | bytes 331784 | tf_op jit(solution)/shard_map/ppermute | solution.py:77
  62.9 22.7 %collective-permute-start.3 = (bf16[1152,384]{1,0:T(8,128)(2,1)S(1)}, bf16[1152,384]{1,0:T(8,128)(2,1)}, u32[]{:S(2)}, u32[]{:S(2)}) collective-permute-start(bf16[1152,384]{1,0:T(8,128)(2,1)S(1)} %get-tuple-element.24), channel_id=1, source_target_pairs={{0,2},{1,3},{2,0},{3,1},{4,6},{5,7},{6,4},{7,5},{8,10},{9,11},{10,... | collective-permute-start | bytes 2654216 | tf_op jit(solution)/shard_map/ppermute | solution.py:82
  62.9 39.9 %collective-permute-start.5 = (bf16[1152,384]{1,0:T(8,128)(2,1)S(1)}, bf16[1152,384]{1,0:T(8,128)(2,1)}, u32[]{:S(2)}, u32[]{:S(2)}) collective-permute-start(bf16[1152,384]{1,0:T(8,128)(2,1)S(1)} %get-tuple-element.24), channel_id=1, source_target_pairs={{0,4},{1,5},{2,6},{3,7},{4,0},{5,1},{6,2},{7,3},{8,12},{9,13},{10,... | collective-permute-start | bytes 2654216 | tf_op jit(solution)/shard_map/ppermute | solution.py:82
  64.1 38.7 %collective-permute-start.7 = (bf16[1152,384]{1,0:T(8,128)(2,1)S(1)}, bf16[1152,384]{1,0:T(8,128)(2,1)}, u32[]{:S(2)}, u32[]{:S(2)}) collective-permute-start(bf16[1152,384]{1,0:T(8,128)(2,1)S(1)} %get-tuple-element.24), channel_id=1, source_target_pairs={{0,6},{1,7},{2,4},{3,5},{4,2},{5,3},{6,0},{7,1},{8,14},{9,15},{10,... | collective-permute-start | bytes 2654216 | tf_op jit(solution)/shard_map/ppermute | solution.py:82
  66.3 37.0 %collective-permute-start.2 = (bf16[1152,384]{1,0:T(8,128)(2,1)S(1)}, bf16[1152,384]{1,0:T(8,128)(2,1)}, u32[]{:S(2)}, u32[]{:S(2)}) collective-permute-start(bf16[1152,384]{1,0:T(8,128)(2,1)S(1)} %get-tuple-element.24), channel_id=1, source_target_pairs={{0,1},{1,0},{2,3},{3,2},{4,5},{5,4},{6,7},{7,6},{8,9},{9,8},{10,11... | collective-permute-start | bytes 2654216 | tf_op jit(solution)/shard_map/ppermute | solution.py:82
  85.5 22.3 %collective-permute-start.4 = (bf16[1152,384]{1,0:T(8,128)(2,1)}, bf16[1152,384]{1,0:T(8,128)(2,1)}, u32[]{:S(2)}, u32[]{:S(2)}) collective-permute-start(bf16[1152,384]{1,0:T(8,128)(2,1)} %collective-permute-done.3), channel_id=1, source_target_pairs={{0,1},{1,0},{2,3},{3,2},{4,5},{5,4},{6,7},{7,6},{8,9},{9,8},{10,11... | collective-permute-start | bytes 2654216 | tf_op jit(solution)/shard_map/ppermute | solution.py:82
  102.8 9.5 %collective-permute-start.6 = (bf16[1152,384]{1,0:T(8,128)(2,1)}, bf16[1152,384]{1,0:T(8,128)(2,1)S(1)}, u32[]{:S(2)}, u32[]{:S(2)}) collective-permute-start(bf16[1152,384]{1,0:T(8,128)(2,1)} %collective-permute-done.5), channel_id=1, source_target_pairs={{0,1},{1,0},{2,3},{3,2},{4,5},{5,4},{6,7},{7,6},{8,9},{9,8},{10,11... | collective-permute-start | bytes 2654216 | tf_op jit(solution)/shard_map/ppermute | solution.py:82
  102.8 13.0 %collective-permute-start.8 = (bf16[1152,384]{1,0:T(8,128)(2,1)}, bf16[1152,384]{1,0:T(8,128)(2,1)S(1)}, u32[]{:S(2)}, u32[]{:S(2)}) collective-permute-start(bf16[1152,384]{1,0:T(8,128)(2,1)} %collective-permute-done.7), channel_id=1, source_target_pairs={{0,1},{1,0},{2,3},{3,2},{4,5},{5,4},{6,7},{7,6},{8,9},{9,8},{10,11... | collective-permute-start | bytes 2654216 | tf_op jit(solution)/shard_map/ppermute | solution.py:82
  110.1 69.0 %copy-start.6 = (f32[1536]{0:T(1024)S(1)}, f32[1536]{0:T(1024)}, u32[]{:S(2)}) copy-start(f32[1536]{0:T(1024)} %param.16) | copy-start | bytes 18436
  268.3 97.2 %slice-start.5 = ((s8[4718592]{0:T(1024)(128)(4,1)}), s8[524288]{0:T(1024)(128)(4,1)S(1)}, s32[]{:S(2)}) async-start(s8[4718592]{0:T(1024)(128)(4,1)} %bitcast.34), calls=%async_computation.8 | async-start | bytes 1048576
  357.7 3.5 copy-start.3
  357.7 5.9 %slice-start = ((s8[4718592]{0:T(1024)(128)(4,1)}), s8[4194304]{0:T(1024)(128)(4,1)S(1)}, s32[]{:S(2)}) async-start(s8[4718592]{0:T(1024)(128)(4,1)} %bitcast.30), calls=%async_computation.3 | async-start | bytes 8388608
  361.2 2.5 slice-start.1
  361.2 4.4 slice-start.6
  361.2 12.7 %collective-permute-start.14 = (bf16[1152,384]{1,0:T(8,128)(2,1)S(1)}, bf16[1152,384]{1,0:T(8,128)(2,1)S(1)}, u32[]{:S(2)}, u32[]{:S(2)}) collective-permute-start(bf16[1152,384]{1,0:T(8,128)(2,1)S(1)} %fusion.9), channel_id=1, source_target_pairs={{0,1},{1,0},{2,3},{3,2},{4,5},{5,4},{6,7},{7,6},{8,9},{9,8},{10,11... | collective-permute-start | bytes 2654216 | tf_op jit(solution)/shard_map/ppermute | solution.py:82
  364.7 12.7 %collective-permute-start.12 = (bf16[1152,384]{1,0:T(8,128)(2,1)S(1)}, bf16[1152,384]{1,0:T(8,128)(2,1)S(1)}, u32[]{:S(2)}, u32[]{:S(2)}) collective-permute-start(bf16[1152,384]{1,0:T(8,128)(2,1)S(1)} %fusion.8), channel_id=1, source_target_pairs={{0,1},{1,0},{2,3},{3,2},{4,5},{5,4},{6,7},{7,6},{8,9},{9,8},{10,11... | collective-permute-start | bytes 2654216 | tf_op jit(solution)/shard_map/ppermute | solution.py:82
  367.7 11.5 %collective-permute-start.10 = (bf16[1152,384]{1,0:T(8,128)(2,1)S(1)}, bf16[1152,384]{1,0:T(8,128)(2,1)S(1)}, u32[]{:S(2)}, u32[]{:S(2)}) collective-permute-start(bf16[1152,384]{1,0:T(8,128)(2,1)S(1)} %fusion.7), channel_id=1, source_target_pairs={{0,1},{1,0},{2,3},{3,2},{4,5},{5,4},{6,7},{7,6},{8,9},{9,8},{10,11... | collective-permute-start | bytes 2654216 | tf_op jit(solution)/shard_map/ppermute | solution.py:82
  370.1 13.4 %collective-permute-start.9 = (bf16[1152,384]{1,0:T(8,128)(2,1)S(1)}, bf16[1152,384]{1,0:T(8,128)(2,1)S(1)}, u32[]{:S(2)}, u32[]{:S(2)}) collective-permute-start(bf16[1152,384]{1,0:T(8,128)(2,1)S(1)} %fusion.6), channel_id=1, source_target_pairs={{0,1},{1,0},{2,3},{3,2},{4,5},{5,4},{6,7},{7,6},{8,9},{9,8},{10,11... | collective-permute-start | bytes 2654216 | tf_op jit(solution)/shard_map/ppermute | solution.py:82
  375.0 23.5 %collective-permute-start.15 = (bf16[1152,384]{1,0:T(8,128)(2,1)S(1)}, bf16[1152,384]{1,0:T(8,128)(2,1)S(1)}, u32[]{:S(2)}, u32[]{:S(2)}) collective-permute-start(bf16[1152,384]{1,0:T(8,128)(2,1)S(1)} %add_convert_fusion.4), channel_id=1, source_target_pairs={{0,6},{1,7},{2,4},{3,5},{4,2},{5,3},{6,0},{7,1},{8,14},{9,15},{10,... | collective-permute-start | bytes 2654216 | tf_op jit(solution)/shard_map/ppermute | solution.py:82
  378.6 38.0 %collective-permute-start.13 = (bf16[1152,384]{1,0:T(8,128)(2,1)S(1)}, bf16[1152,384]{1,0:T(8,128)(2,1)S(1)}, u32[]{:S(2)}, u32[]{:S(2)}) collective-permute-start(bf16[1152,384]{1,0:T(8,128)(2,1)S(1)} %add_convert_fusion.5), channel_id=1, source_target_pairs={{0,4},{1,5},{2,6},{3,7},{4,0},{5,1},{6,2},{7,3},{8,12},{9,13},{10,... | collective-permute-start | bytes 2654216 | tf_op jit(solution)/shard_map/ppermute | solution.py:82
  380.6 36.0 %collective-permute-start.11 = (bf16[1152,384]{1,0:T(8,128)(2,1)S(1)}, bf16[1152,384]{1,0:T(8,128)(2,1)S(1)}, u32[]{:S(2)}, u32[]{:S(2)}) collective-permute-start(bf16[1152,384]{1,0:T(8,128)(2,1)S(1)} %add_convert_fusion.6), channel_id=1, source_target_pairs={{0,2},{1,3},{2,0},{3,1},{4,6},{5,7},{6,4},{7,5},{8,10},{9,11},{10,... | collective-permute-start | bytes 2654216 | tf_op jit(solution)/shard_map/ppermute | solution.py:82
  382.3 34.3 %copy-start.5 = (f32[384]{0:T(512)S(1)}, f32[384]{0:T(512)}, u32[]{:S(2)}) copy-start(f32[384]{0:T(512)} %param.18) | copy-start | bytes 4612
  383.5 33.7 %copy-start.1 = (bf16[24,48,384]{2,1,0:T(8,128)(2,1)S(1)}, bf16[24,48,384]{2,1,0:T(8,128)(2,1)}, u32[]{:S(2)}) copy-start(bf16[24,48,384]{2,1,0:T(8,128)(2,1)} %rest_0_.1) | copy-start | bytes 2654212
  383.5 33.7 %copy-start.4 = (f32[384]{0:T(512)S(1)}, f32[384]{0:T(512)}, u32[]{:S(2)}) copy-start(f32[384]{0:T(512)} %param.19) | copy-start | bytes 4612
  418.5 22.5 %collective-permute-start.17 = (bf16[1152,384]{1,0:T(8,128)(2,1)S(1)}, bf16[1152,384]{1,0:T(8,128)(2,1)S(1)}, u32[]{:S(2)}, u32[]{:S(2)}) collective-permute-start(bf16[1152,384]{1,0:T(8,128)(2,1)S(1)} %bitcast.23), channel_id=1, source_target_pairs={{0,2},{1,3},{2,0},{3,1},{4,6},{5,7},{6,4},{7,5},{8,10},{9,11},{10,... | collective-permute-start | bytes 2654216 | tf_op jit(solution)/shard_map/ppermute | solution.py:82
  420.0 40.2 %collective-permute-start.19 = (bf16[1152,384]{1,0:T(8,128)(2,1)S(1)}, bf16[1152,384]{1,0:T(8,128)(2,1)S(1)}, u32[]{:S(2)}, u32[]{:S(2)}) collective-permute-start(bf16[1152,384]{1,0:T(8,128)(2,1)S(1)} %bitcast.24), channel_id=1, source_target_pairs={{0,4},{1,5},{2,6},{3,7},{4,0},{5,1},{6,2},{7,3},{8,12},{9,13},{10,... | collective-permute-start | bytes 2654216 | tf_op jit(solution)/shard_map/ppermute | solution.py:82
  421.4 38.8 %collective-permute-start.21 = (bf16[1152,384]{1,0:T(8,128)(2,1)S(1)}, bf16[1152,384]{1,0:T(8,128)(2,1)S(1)}, u32[]{:S(2)}, u32[]{:S(2)}) collective-permute-start(bf16[1152,384]{1,0:T(8,128)(2,1)S(1)} %bitcast.25), channel_id=1, source_target_pairs={{0,6},{1,7},{2,4},{3,5},{4,2},{5,3},{6,0},{7,1},{8,14},{9,15},{10,... | collective-permute-start | bytes 2654216 | tf_op jit(solution)/shard_map/ppermute | solution.py:82
  422.0 38.7 %collective-permute-start.16 = (bf16[1152,384]{1,0:T(8,128)(2,1)S(1)}, bf16[1152,384]{1,0:T(8,128)(2,1)S(1)}, u32[]{:S(2)}, u32[]{:S(2)}) collective-permute-start(bf16[1152,384]{1,0:T(8,128)(2,1)S(1)} %bitcast.26), channel_id=1, source_target_pairs={{0,1},{1,0},{2,3},{3,2},{4,5},{5,4},{6,7},{7,6},{8,9},{9,8},{10,11... | collective-permute-start | bytes 2654216 | tf_op jit(solution)/shard_map/ppermute | solution.py:82
  441.0 20.2 %collective-permute-start.18 = (bf16[1152,384]{1,0:T(8,128)(2,1)S(1)}, bf16[1152,384]{1,0:T(8,128)(2,1)S(1)}, u32[]{:S(2)}, u32[]{:S(2)}) collective-permute-start(bf16[1152,384]{1,0:T(8,128)(2,1)S(1)} %collective-permute-done.17), channel_id=1, source_target_pairs={{0,1},{1,0},{2,3},{3,2},{4,5},{5,4},{6,7},{7,6},{8,9},{9,8},{10,11... | collective-permute-start | bytes 2654216 | tf_op jit(solution)/shard_map/ppermute | solution.py:82
  460.1 2.4 collective-permute-start.20
  460.2 3.7 collective-permute-start.22
  464.1 17.0 %slice-start.2 = ((s8[9437184]{0:T(1024)(128)(4,1)}), s8[4194304]{0:T(1024)(128)(4,1)S(1)}, s32[]{:S(2)}) async-start(s8[9437184]{0:T(1024)(128)(4,1)} %bitcast.32), calls=%async_computation.5 | async-start | bytes 8388608
  464.1 17.0 %slice-start.3 = ((s8[9437184]{0:T(1024)(128)(4,1)}), s8[4194304]{0:T(1024)(128)(4,1)S(1)}, s32[]{:S(2)}) async-start(s8[9437184]{0:T(1024)(128)(4,1)} %bitcast.32), calls=%async_computation.6 | async-start | bytes 8388608
  471.7 9.3 %slice-start.4 = ((s8[9437184]{0:T(1024)(128)(4,1)}), s8[1048576]{0:T(1024)(128)(4,1)S(1)}, s32[]{:S(2)}) async-start(s8[9437184]{0:T(1024)(128)(4,1)} %bitcast.32), calls=%async_computation.7 | async-start | bytes 2097152
  483.1 7.4 %collective-permute-start.28 = (bf16[1152,384]{1,0:T(8,128)(2,1)S(1)}, bf16[1152,384]{1,0:T(8,128)(2,1)S(1)}, u32[]{:S(2)}, u32[]{:S(2)}) collective-permute-start(bf16[1152,384]{1,0:T(8,128)(2,1)S(1)} %convolution_convert_fusion), channel_id=1, source_target_pairs={{0,1},{1,0},{2,3},{3,2},{4,5},{5,4},{6,7},{7,6},{8,9},{9,8},{10,11... | collective-permute-start | bytes 2654216 | tf_op jit(solution)/shard_map/ppermute | solution.py:82
  485.4 8.8 %collective-permute-start.26 = (bf16[1152,384]{1,0:T(8,128)(2,1)S(1)}, bf16[1152,384]{1,0:T(8,128)(2,1)S(1)}, u32[]{:S(2)}, u32[]{:S(2)}) collective-permute-start(bf16[1152,384]{1,0:T(8,128)(2,1)S(1)} %convolution_convert_fusion.1), channel_id=1, source_target_pairs={{0,1},{1,0},{2,3},{3,2},{4,5},{5,4},{6,7},{7,6},{8,9},{9,8},{10,11... | collective-permute-start | bytes 2654216 | tf_op jit(solution)/shard_map/ppermute | solution.py:82
  487.9 8.5 %collective-permute-start.24 = (bf16[1152,384]{1,0:T(8,128)(2,1)S(1)}, bf16[1152,384]{1,0:T(8,128)(2,1)S(1)}, u32[]{:S(2)}, u32[]{:S(2)}) collective-permute-start(bf16[1152,384]{1,0:T(8,128)(2,1)S(1)} %convolution_convert_fusion.2), channel_id=1, source_target_pairs={{0,1},{1,0},{2,3},{3,2},{4,5},{5,4},{6,7},{7,6},{8,9},{9,8},{10,11... | collective-permute-start | bytes 2654216 | tf_op jit(solution)/shard_map/ppermute | solution.py:82
  490.1 12.6 %collective-permute-start.23 = (bf16[1152,384]{1,0:T(8,128)(2,1)S(1)}, bf16[1152,384]{1,0:T(8,128)(2,1)S(1)}, u32[]{:S(2)}, u32[]{:S(2)}) collective-permute-start(bf16[1152,384]{1,0:T(8,128)(2,1)S(1)} %convolution_convert_fusion.3), channel_id=1, source_target_pairs={{0,1},{1,0},{2,3},{3,2},{4,5},{5,4},{6,7},{7,6},{8,9},{9,8},{10,11... | collective-permute-start | bytes 2654216 | tf_op jit(solution)/shard_map/ppermute | solution.py:82
  492.6 23.5 %collective-permute-start.29 = (bf16[1152,384]{1,0:T(8,128)(2,1)S(1)}, bf16[1152,384]{1,0:T(8,128)(2,1)S(1)}, u32[]{:S(2)}, u32[]{:S(2)}) collective-permute-start(bf16[1152,384]{1,0:T(8,128)(2,1)S(1)} %add_convert_fusion), channel_id=1, source_target_pairs={{0,6},{1,7},{2,4},{3,5},{4,2},{5,3},{6,0},{7,1},{8,14},{9,15},{10,... | collective-permute-start | bytes 2654216 | tf_op jit(solution)/shard_map/ppermute | solution.py:82
  496.2 38.0 %collective-permute-start.27 = (bf16[1152,384]{1,0:T(8,128)(2,1)S(1)}, bf16[1152,384]{1,0:T(8,128)(2,1)S(1)}, u32[]{:S(2)}, u32[]{:S(2)}) collective-permute-start(bf16[1152,384]{1,0:T(8,128)(2,1)S(1)} %add_convert_fusion.1), channel_id=1, source_target_pairs={{0,4},{1,5},{2,6},{3,7},{4,0},{5,1},{6,2},{7,3},{8,12},{9,13},{10,... | collective-permute-start | bytes 2654216 | tf_op jit(solution)/shard_map/ppermute | solution.py:82
  498.4 35.9 %collective-permute-start.25 = (bf16[1152,384]{1,0:T(8,128)(2,1)S(1)}, bf16[1152,384]{1,0:T(8,128)(2,1)S(1)}, u32[]{:S(2)}, u32[]{:S(2)}) collective-permute-start(bf16[1152,384]{1,0:T(8,128)(2,1)S(1)} %add_convert_fusion.2), channel_id=1, source_target_pairs={{0,2},{1,3},{2,0},{3,1},{4,6},{5,7},{6,4},{7,5},{8,10},{9,11},{10,... | collective-permute-start | bytes 2654216 | tf_op jit(solution)/shard_map/ppermute | solution.py:82
  535.6 4.5 collective-permute-start.36
  536.7 4.9 collective-permute-start.35
  538.2 3.8 collective-permute-start.34
  539.5 3.7 collective-permute-start.33
  540.1 3.1 collective-permute-start.32
  540.1 3.7 collective-permute-start.31
  541.7 2.1 collective-permute-start.30
  544.9 3.6 collective-permute-start.37
  546.2 6.6 %collective-permute-start.38 = (bf16[3,48,384]{2,1,0:T(8,128)(2,1)S(1)}, bf16[3,48,384]{2,1,0:T(8,128)(2,1)S(1)}, u32[]{:S(2)}, u32[]{:S(2)}) collective-permute-start(bf16[3,48,384]{2,1,0:T(8,128)(2,1)S(1)} %bitcast.28), channel_id=1, source_target_pairs={{8,0},{24,16},{9,1},{25,17},{10,2},{26,18},{11,3},{27,19},{12,4},{... | collective-permute-start | bytes 331784 | tf_op jit(solution)/shard_map/ppermute | solution.py:77
Sparse Core Ops, SparseCore 0:
  9.6 169.4 all-gather.3
  180.6 87.5 all-gather.5
  269.9 87.8 all-gather.7

commit v2 on v1

--- a/solution.py
+++ b/solution.py
@@ -9,7 +9,6 @@
 
 H = 48
 LANES = 128
-CHUNKS = 2
 
 epsilon = 1e-06
 root_half = 0.7071067811865476
@@ -95,19 +94,22 @@
     return out
 
 
-def scatter_columns(part):
+def pair_sums(part):
     count = lax.axis_size("col")
     me = lax.axis_index("col")
     order = list(range(2, count, 2)) + [0]
     arrived = {d: swap(part(me ^ d ^ 1).astype(jnp.bfloat16), 1) for d in order}
-    total = None
-    pieces = []
+    pairs = []
     for d in order:
         pair = part(me ^ d) + arrived[d].astype(jnp.float32)
-        pieces.append(swap(pair.astype(jnp.bfloat16), d).astype(jnp.float32) if d else pair)
-    total = pieces[-1]
-    for piece in pieces[:-1]:
-        total = total + piece
+        pairs.append(pair.astype(jnp.bfloat16) if d else pair)
+    return pairs
+
+
+def sum_pairs(pairs):
+    total = pairs[-1]
+    for index, pair in enumerate(pairs[:-1]):
+        total = total + swap(pair, 2 * index + 2).astype(jnp.float32)
     return total
 
 
@@ -128,14 +130,22 @@
     col_start = lax.axis_index("col") * narrow
     tokens = row_count * grid_width
     units = w_expand.shape[1]
-    step = units // CHUNKS
+    cut = narrow * 2 // 3
     dot = functools.partial(jnp.dot, preferred_element_type=jnp.float32)
 
+    def turned(left, right):
+        return lax.dot_general(
+            left, right, (((1,), (1,)), ((), ())), preferred_element_type=jnp.float32
+        )
+
+    owners = w_reduce.reshape(units, -1, narrow)
     expand_full = lax.all_gather(w_expand, "row", axis=0, tiled=True)
-    reduce_full = [
-        lax.all_gather(w_reduce[i * step : (i + 1) * step], "row", axis=1, tiled=True)
-        for i in range(CHUNKS)
-    ]
+    reduce_first = lax.all_gather(
+        owners[:, :, :cut].reshape(units, -1), "row", axis=1, tiled=True
+    )
+    reduce_last = lax.all_gather(
+        owners[:, :, cut:].reshape(units, -1), "row", axis=1, tiled=True
+    )
 
     top, bottom = halo(activations)
     mixed_bf = depthwise(activations, top, bottom, kernel, False)
@@ -154,38 +164,41 @@
 
     cot_f = cotangent.astype(jnp.float32)
     grad_branch = (layer_scale * cot_f).reshape(tokens, narrow).astype(jnp.bfloat16)
-    grad_full = gather_columns(grad_branch)
+    grad_first = gather_columns(grad_branch[:, :cut])
+    grad_last = gather_columns(grad_branch[:, cut:])
+    expand_full, grad_first, grad_last = lax.optimization_barrier(
+        (expand_full, grad_first, grad_last)
+    )
 
     preact = dot(normed_full, expand_full) + b_expand
     cumulative = 0.5 * (1.0 + lax.erf(preact * root_half))
     hidden = (preact * cumulative).astype(jnp.bfloat16)
+
+    def branch_part(weights, activated):
+        width = weights.shape[1] // lax.axis_size("col")
+        return lambda owner: dot(
+            activated, lax.dynamic_slice_in_dim(weights, owner * width, width, 1)
+        )
+
+    branch_first = sum_pairs(pair_sums(branch_part(reduce_first, hidden)))
+    grad_hidden = turned(grad_first, reduce_first)
+    reduce_last, branch_first, grad_hidden = lax.optimization_barrier(
+        (reduce_last, branch_first, grad_hidden)
+    )
     slope = cumulative + preact * jnp.exp(-0.5 * preact * preact) * density_scale
-
-    grad_parts = []
-    for i in range(CHUNKS):
-        grad_hidden = lax.dot_general(
-            grad_full, reduce_full[i], (((1,), (1,)), ((), ())), preferred_element_type=jnp.float32
+    grad_hidden = grad_hidden + turned(grad_last, reduce_last)
+    grad_preact = (grad_hidden * slope).astype(jnp.bfloat16)
+
+    def grad_part(owner):
+        return turned(
+            grad_preact, lax.dynamic_slice_in_dim(expand_full, owner * narrow, narrow, 0)
         )
-        grad_parts.append(
-            (grad_hidden * slope[:, i * step : (i + 1) * step]).astype(jnp.bfloat16)
-        )
-    grad_preact = jnp.concatenate(grad_parts, 1)
-
-    def grad_part(owner):
-        rows = lax.dynamic_slice_in_dim(expand_full, owner * narrow, narrow, 0)
-        return lax.dot_general(
-            grad_preact, rows, (((1,), (1,)), ((), ())), preferred_element_type=jnp.float32
-        )
-
-    def branch_part(owner):
-        total = 0.0
-        for i in range(CHUNKS):
-            block = lax.dynamic_slice_in_dim(reduce_full[i], owner * narrow, narrow, 1)
-            total = total + dot(hidden[:, i * step : (i + 1) * step], block)
-        return total
-
-    grad_gain = scatter_columns(grad_part) * local_gain
-    branch_out = scatter_columns(branch_part) + b_reduce
+
+    grad_pairs = pair_sums(grad_part)
+    *grad_pairs, hidden = lax.optimization_barrier((*grad_pairs, hidden))
+    grad_gain = sum_pairs(grad_pairs) * local_gain
+    branch_last = sum_pairs(pair_sums(branch_part(reduce_last, hidden)))
+    branch_out = jnp.concatenate([branch_first, branch_last], 1) + b_reduce
 
     grad_sums = jnp.stack([jnp.sum(grad_gain, 1), jnp.sum(grad_gain * normal_local, 1)])
     every_sum = grad_sums

time: 577 us -> 492 us (0.85)
  waiting for transfers between devices: 368 us -> 236 us
  local copies, waits for them, and re-layouts: 25.2 us -> 47.5 us
  matrix products: 77.8 us -> 90.7 us
  starting transfers between devices: 33.4 us -> 44.3 us
    all_gather x1, waiting for transfers between devices: 62.2 us -> 10.1 us  [body(): expand_full = lax.all_gather(w_expand, 'row', axis=0, tiled=True)]
    all_gather x2, waiting for transfers between devices: 155 us -> 111 us  [the longest x1 89.9 us: body(): lax.all_gather(owners[:, :, :cut].reshape(units, -1), 'row', axis=1, tile...]
    ppermute x35 -> x49, waiting for transfers between devices: 142 us -> 99.3 us  [swap(): return lax.ppermute(value, 'col', [(i, i ^ distance) for i in range(count)])]
    ppermute x35 -> x49, starting transfers between devices: 24.5 us -> 36.6 us  [swap(): return lax.ppermute(value, 'col', [(i, i ^ distance) for i in range(count)])]
    broadcast_in_dim x0 -> x3, local copies, waits for them, and re-layouts: none -> 8.25 us  [gather_columns(): out = jnp.zeros((tokens, narrow * count), piece.dtype)]
    dot_general x1, matrix products: 20 us -> 27.6 us  [body(): preact = dot(normed_full, expand_full) + b_expand]
    dynamic_update_slice x8 -> x12, local copies, waits for them, and re-layouts: 7.62 us -> 13.4 us  [gather_columns(): lax.dynamic_update_slice(out, other, (0, (me ^ distance ^ 1) * narrow))]
    reshape x0 -> x1, local copies, waits for them, and re-layouts: none -> 5.78 us  [body(): owners = w_reduce.reshape(units, -1, narrow)]
  transfers between devices with their start and end apart: 42 -> 56, of which waited for: 19 -> 19; matrix products, arithmetic and copies ran while one was open for 14% -> 25% of each run, Pallas kernels for 2% -> 2%
where the time goes in v2:
time: 492 us; the launch traced here: 484 us
  waiting for transfers between devices  236 us (48%)
  matrix products  90.7 us (18%)
  local copies, waits for them, and re-layouts  47.5 us (10%)
  starting transfers between devices  44.3 us (9%)
  blocking collectives  24.7 us (5%)
  Pallas kernels  19 us (4%)
  between operations  14.5 us (3%)
  other arithmetic  7.14 us (1%)
    ppermute x49, waiting for transfers between devices, swap(): return lax.ppermute(value, 'col', [(i, i ^ distance) for i in range(count)])  99.3 us
    all_gather x1, waiting for transfers between devices, body(): lax.all_gather(owners[:, :, :cut].reshape(units, -1), 'row', axis=1, tile...  89.9 us
    dot_general x10, matrix products, turned(): lax.dot_general(left, right, (((1,), (1,)), ((), ())), preferred_element_...  41.9 us
    ppermute x49, starting transfers between devices, swap(): return lax.ppermute(value, 'col', [(i, i ^ distance) for i in range(count)])  36.6 us
    dot_general x1, matrix products, body(): preact = dot(normed_full, expand_full) + b_expand  27.6 us
    psum x1, blocking collectives, body(): lax.psum((jnp.sum(local_mixed, 1), jnp.sum(local_mixed * local_mixed, 1))...  24.7 us
    all_gather x1, waiting for transfers between devices, body(): lax.all_gather(owners[:, :, cut:].reshape(units, -1), 'row', axis=1, tile...  21.5 us
    dot_general x16, matrix products, branch_part(): dot(activated, lax.dynamic_slice_in_dim(weights, owner * width, width, 1))  21.2 us
  transfers between devices with their start and end apart: 56, of which 19 were waited for; matrix products, arithmetic and copies ran while one was open for 25% of the time, Pallas kernels for 2%

profile of v2, /device:TPU:0, one launch (start us, length us, event | category | flops | bytes accessed | tf_op | source)
XLA Modules:
  0.0 483.8 jit_solution(3580919358351583160)
XLA Ops:
  7.9 5.8 %reshape.56 = bf16[1536,2,384]{2,1,0:T(2,128)(2,1)} reshape(bf16[1536,768]{1,0:T(8,128)(2,1)} %param.17) | data formatting | bytes 4718592 | tf_op jit(solution)/shard_map/reshape | solution.py:141
  13.7 1.4 slice-done
  15.1 1.5 copy.13
  16.9 2.8 broadcast_in_dim.7
  21.4 2.6 collective-permute-start.10
  24.0 1.5 collective-permute-start.12
  26.2 3.5 collective-permute-start
  29.7 1.4 collective-permute-start.1
  32.1 1.7 broadcast_in_dim.8
  35.5 1.4 dynamic_slice.79
  36.9 9.6 %collective-permute-done.1.bottom_ref = bf16[3,48,384]{2,1,0:T(8,128)(2,1)S(1)} collective-permute-done((bf16[3,48,384]{2,1,0:T(8,128)(2,1)}, bf16[3,48,384]{2,1,0:T(8,128)(2,1)S(1)}, u32[]{:S(2)}, u32[]{:S(2)}) %collective-permute-start.1) | collective-permute-done | bytes 110624 | tf_op jit(solution)/shard_map/ppermute | solution.py:76
  46.5 1.5 collective-permute-start.17
  48.0 9.0 %depthwise.1 = bf16[24,48,384]{2,1,0:T(8,128)(2,1)S(1)} custom-call(bf16[24,48,384]{2,1,0:T(8,128)(2,1)S(1)} %copy-done, bf16[3,48,384]{2,1,0:T(8,128)(2,1)S(1)} %collective-permute-done.top_ref, bf16[3,48,384]{2,1,0:T(8,128)(2,1)S(1)} %collective-permute-done.1.bottom_ref, f32[7,7,384]{2,1,0:T(8,128)S(1)} %copy-done.2), custom_call_target="tpu_custom_call" | custom-call | flops 43352064 | bytes 2654208 | tf_op jit(solution)/shard_map/depthwise/pallas_call | solution.py:53
  57.5 24.7 %all-reduce = (f32[1152]{0:T(1024)S(1)}, f32[1152]{0:T(1024)S(1)}) all-reduce(f32[1152]{0:T(1024)S(1)} %reduce_sum.43, f32[1152]{0:T(1024)S(1)} %reduce_sum.41), channel_id=1, replica_groups=mesh['row'=4,'col'=8] {'col'}, use_global_device_ids=true, to_apply=%region_3.0 | all-reduce | flops 2304 | bytes 18432 | tf_op jit(solution)/shard_map/psum | solution.py:153
  82.2 3.7 broadcast_in_dim.6
  86.0 1.4 constant_dynamic-update-slice_fusion.23
  88.0 1.8 constant_dynamic-update-slice_fusion.6
  89.8 1.7 constant_dynamic-update-slice_fusion.5
  91.6 2.0 constant_dynamic-update-slice_fusion.14
  93.5 2.9 collective-permute-start.14
  96.5 2.0 constant_dynamic-update-slice_fusion.13
  98.5 13.9 %collective-permute-done.19 = bf16[1152,128]{1,0:T(8,128)(2,1)S(1)} collective-permute-done((bf16[1152,128]{1,0:T(8,128)(2,1)S(1)}, bf16[1152,128]{1,0:T(8,128)(2,1)S(1)}, u32[]{:S(2)}, u32[]{:S(2)}) %collective-permute-start.19) | collective-permute-done | bytes 294944 | tf_op jit(solution)/shard_map/ppermute | solution.py:81
  115.2 2.0 collective-permute-start.3
  117.9 1.4 collective-permute-start.5
  121.0 1.2 constant_dynamic-update-slice_fusion.22
  122.6 15.0 %collective-permute-done.3 = bf16[1152,384]{1,0:T(8,128)(2,1)S(1)} collective-permute-done((bf16[1152,384]{1,0:T(8,128)(2,1)S(1)}, bf16[1152,384]{1,0:T(8,128)(2,1)S(1)}, u32[]{:S(2)}, u32[]{:S(2)}) %collective-permute-start.3) | collective-permute-done | bytes 884768 | tf_op jit(solution)/shard_map/ppermute | solution.py:81
  138.7 19.6 %collective-permute-done.5 = bf16[1152,384]{1,0:T(8,128)(2,1)S(1)} collective-permute-done((bf16[1152,384]{1,0:T(8,128)(2,1)S(1)}, bf16[1152,384]{1,0:T(8,128)(2,1)S(1)}, u32[]{:S(2)}, u32[]{:S(2)}) %collective-permute-start.5) | collective-permute-done | bytes 884768 | tf_op jit(solution)/shard_map/ppermute | solution.py:81
  169.0 10.1 %all-gather.6.cloned.1.call-done = bf16[3072,1536]{1,0:T(8,128)(2,1)} async-done(((bf16[768,1536]{1,0:T(8,128)(2,1)}), bf16[3072,1536]{1,0:T(8,128)(2,1)}) %all-gather.6.cloned.1.call-update) | async-done | bytes 9437200 | tf_op jit(solution)/shard_map/all_gather | solution.py:142
  179.1 27.6 %multiply_convert_fusion = (bf16[1152,1536]{1,0:T(8,128)(2,1)}, f32[1152,1536]{1,0:T(8,128)}) fusion(f32[1536]{0:T(1024)S(1)} %copy-done.12, bf16[1152,3072]{1,0:T(8,128)(2,1)} %constant_dynamic-update-slice_fusion.16, bf16[3072,1536]{1,0:T(8,128)(2,1)} %all-gather.6.cloned.1.call-done), kind=kOutput, calls=%fused_computation.9 | convolution fusion | flops 10882252800 | bytes 27138048 | tf_op jit(solution)/shard_map/dot_general | solution.py:173
  206.7 89.9 %all-gather.8.cloned.1.call-done = bf16[1536,2048]{1,0:T(8,128)(2,1)} async-done(((bf16[1536,512]{1,0:T(8,128)(2,1)}), bf16[1536,2048]{1,0:T(8,128)(2,1)}) %all-gather.8.cloned.1.call-update) | async-done | bytes 6291472 | tf_op jit(solution)/shard_map/all_gather | solution.py:143
  296.6 3.4 convolution_convert_fusion.6
  300.2 2.4 convolution_convert_fusion.5
  307.1 1.5 collective-permute-start.25
  309.7 1.5 collective-permute-start.27
  313.0 11.1 %fusion.96 = f32[1152,1536]{1,0:T(8,128)} fusion(bf16[1152,2048]{1,0:T(8,128)(2,1)} %constant_dynamic-update-slice_fusion.8, bf16[1536,2048]{1,0:T(8,128)(2,1)S(1)} %bitcast.66), kind=kOutput, calls=%fused_computation.145 | convolution fusion | flops 7247757312 | bytes 18087936 | tf_op jit(solution)/shard_map/dot_general | solution.py:137
  325.2 12.2 %collective-permute-done.27 = bf16[1152,256]{1,0:T(8,128)(2,1)S(1)} collective-permute-done((bf16[1152,256]{1,0:T(8,128)(2,1)S(1)}, bf16[1152,256]{1,0:T(8,128)(2,1)S(1)}, u32[]{:S(2)}, u32[]{:S(2)}) %collective-permute-start.27) | collective-permute-done | bytes 589856 | tf_op jit(solution)/shard_map/ppermute | solution.py:81
  337.5 1.5 convert_add_fusion.1
  338.9 21.5 %all-gather.4.cloned.1.call-done = bf16[1536,1024]{1,0:T(8,128)(2,1)} async-done(((bf16[1536,256]{1,0:T(8,128)(2,1)}), bf16[1536,1024]{1,0:T(8,128)(2,1)}) %all-gather.4.cloned.1.call-update) | async-done | bytes 3145744 | tf_op jit(solution)/shard_map/all_gather | solution.py:146
  360.4 11.4 %fusion.1 = bf16[1152,1536]{1,0:T(8,128)(2,1)S(1)} fusion(f32[1152,1536]{1,0:T(8,128)} %fusion.96, bf16[1152,1024]{1,0:T(8,128)(2,1)} %constant_dynamic-update-slice_fusion, bf16[1536,1024]{1,0:T(8,128)(2,1)} %all-gather.4.cloned.1.call-done, f32[1152,1536]{1,0:T(8,128)} %get-tuple-element.46), kind=kOutput, calls=%fused_computation.4 | convolution fusion | flops 3643342848 | bytes 23199744 | tf_op jit(solution)/shard_map/dot_general | solution.py:137
  371.9 3.5 convolution_convert_fusion
  375.4 3.4 convolution_convert_fusion.1
  379.3 2.0 convolution_convert_fusion.2
  381.5 2.0 convolution_convert_fusion.3
  384.0 2.0 convert_add_fusion
  386.1 2.1 add_convert_fusion
  388.2 2.1 add_convert_fusion.1
  390.3 2.3 add_convert_fusion.2
  396.5 1.6 collective-permute-start.41
  398.1 1.5 collective-permute-start.42
  405.2 1.5 collective-permute-start.36
  407.8 11.2 %collective-permute-done.41 = bf16[1152,384]{1,0:T(8,128)(2,1)S(1)} collective-permute-done((bf16[1152,384]{1,0:T(8,128)(2,1)S(1)}, bf16[1152,384]{1,0:T(8,128)(2,1)S(1)}, u32[]{:S(2)}, u32[]{:S(2)}) %collective-permute-start.41) | collective-permute-done | bytes 884768 | tf_op jit(solution)/shard_map/ppermute | solution.py:81
  419.1 1.5 collective-permute-start.38
  420.5 17.9 %collective-permute-done.42 = bf16[1152,384]{1,0:T(8,128)(2,1)S(1)} collective-permute-done((bf16[1152,384]{1,0:T(8,128)(2,1)S(1)}, bf16[1152,384]{1,0:T(8,128)(2,1)S(1)}, u32[]{:S(2)}, u32[]{:S(2)}) %collective-permute-start.42) | collective-permute-done | bytes 884768 | tf_op jit(solution)/shard_map/ppermute | solution.py:81
  439.4 1.2 fusion.91
  440.7 3.0 collective-permute-start.45
  445.0 5.5 %collective-permute-done.38 = bf16[1152,128]{1,0:T(8,128)(2,1)S(1)} collective-permute-done((bf16[1152,128]{1,0:T(8,128)(2,1)S(1)}, bf16[1152,128]{1,0:T(8,128)(2,1)S(1)}, u32[]{:S(2)}, u32[]{:S(2)}) %collective-permute-start.38) | collective-permute-done | bytes 294944 | tf_op jit(solution)/shard_map/ppermute | solution.py:81
  450.5 2.0 collective-permute-start.47
  453.1 1.8 collective-permute-start.50
  455.6 1.6 collective-permute-done.49
  458.3 1.3 collective-permute-start.51
  459.6 1.3 collective-permute-start.52
  460.9 1.2 fusion.8
  462.9 4.1 collective-permute-done.52.bottom_ref
  467.0 10.1 %depthwise_flipped.1 = bf16[24,48,384]{2,1,0:T(8,128)(2,1)} custom-call(bf16[24,48,384]{2,1,0:T(8,128)(2,1)S(1)} %bitcast.52, bf16[3,48,384]{2,1,0:T(8,128)(2,1)S(1)} %collective-permute-done.51.top_ref, bf16[3,48,384]{2,1,0:T(8,128)(2,1)S(1)} %collective-permute-done.52.bottom_ref, f32[7,7,384]{2,1,0:T(8,128)S(1)} %copy-done.2, ...), custom_call_target="tpu_custom_call" | custom-call | flops 43352064 | bytes 2654208 | tf_op jit(solution)/shard_map/depthwise_flipped/pallas_call | solution.py:53
  (172 shorter events, 50.6 us)
Async XLA Ops:
  7.2 172.0 %all-gather.6.cloned.1.call-start = ((), (), s32[]{:S(2)}) async-start(), calls=%async_computation.1 | async-start | bytes 11796480 | tf_op jit(solution)/shard_map/all_gather | solution.py:142
  7.9 288.7 %all-gather.8.cloned.1.call-start = ((), (), s32[]{:S(2)}) async-start(), calls=%async_computation.2 | async-start | bytes 7864320 | tf_op jit(solution)/shard_map/all_gather | solution.py:143
  16.7 343.8 %all-gather.4.cloned.1.call-start = ((), (), s32[]{:S(2)}) async-start(), calls=%async_computation | async-start | bytes 3932160 | tf_op jit(solution)/shard_map/all_gather | solution.py:146
  16.9 8.6 %copy-start = (bf16[24,48,384]{2,1,0:T(8,128)(2,1)S(1)}, bf16[24,48,384]{2,1,0:T(8,128)(2,1)}, u32[]{:S(2)}) copy-start(bf16[24,48,384]{2,1,0:T(8,128)(2,1)} %x_ref.1) | copy-start | bytes 2654212
  16.9 14.2 %slice-start.1 = ((bf16[1536,2,384]{2,1,0:T(2,128)(2,1)}), bf16[1536,2,128]{2,1,0:T(2,128)(2,1)S(1)}, s32[]{:S(2)}) async-start(bf16[1536,2,384]{2,1,0:T(2,128)(2,1)} %reshape.56), calls=%async_computation.4 | async-start | bytes 1572864 | tf_op jit(solution)/shard_map/slice | solution.py:147
  20.9 70.7 %collective-permute-start.9 = (bf16[1152,256]{1,0:T(8,128)(2,1)}, bf16[1152,256]{1,0:T(8,128)(2,1)}, u32[]{:S(2)}, u32[]{:S(2)}) collective-permute-start(bf16[1152,256]{1,0:T(8,128)(2,1)} %get-tuple-element.37), channel_id=1, source_target_pairs={{0,1},{1,0},{2,3},{3,2},{4,5},{5,4},{6,7},{7,6},{8,9},{9,8},{10,11... | collective-permute-start | bytes 1769480 | tf_op jit(solution)/shard_map/ppermute | solution.py:81
  21.4 72.1 %collective-permute-start.10 = (bf16[1152,256]{1,0:T(8,128)(2,1)}, bf16[1152,256]{1,0:T(8,128)(2,1)}, u32[]{:S(2)}, u32[]{:S(2)}) collective-permute-start(bf16[1152,256]{1,0:T(8,128)(2,1)} %get-tuple-element.37), channel_id=1, source_target_pairs={{0,2},{1,3},{2,0},{3,1},{4,6},{5,7},{6,4},{7,5},{8,10},{9,11},{10,... | collective-permute-start | bytes 1769480 | tf_op jit(solution)/shard_map/ppermute | solution.py:81
  24.0 94.0 %collective-permute-start.12 = (bf16[1152,256]{1,0:T(8,128)(2,1)}, bf16[1152,256]{1,0:T(8,128)(2,1)S(1)}, u32[]{:S(2)}, u32[]{:S(2)}) collective-permute-start(bf16[1152,256]{1,0:T(8,128)(2,1)} %get-tuple-element.37), channel_id=1, source_target_pairs={{0,4},{1,5},{2,6},{3,7},{4,0},{5,1},{6,2},{7,3},{8,12},{9,13},{10,... | collective-permute-start | bytes 1769480 | tf_op jit(solution)/shard_map/ppermute | solution.py:81
  26.2 10.7 %collective-permute-start = (bf16[3,48,384]{2,1,0:T(8,128)(2,1)}, bf16[3,48,384]{2,1,0:T(8,128)(2,1)S(1)}, u32[]{:S(2)}, u32[]{:S(2)}) collective-permute-start(bf16[3,48,384]{2,1,0:T(8,128)(2,1)} %get-tuple-element.40), channel_id=1, source_target_pairs={{0,8},{16,24},{1,9},{17,25},{2,10},{18,26},{3,11},{19,27},{4,12},{... | collective-permute-start | bytes 331784 | tf_op jit(solution)/shard_map/ppermute | solution.py:76
  29.7 18.3 %copy-start.2 = (f32[7,7,384]{2,1,0:T(8,128)S(1)}, f32[7,7,384]{2,1,0:T(8,128)}, u32[]{:S(2)}) copy-start(f32[7,7,384]{2,1,0:T(8,128)} %k_ref.3) | copy-start | bytes 225796
  29.7 16.8 %collective-permute-start.1 = (bf16[3,48,384]{2,1,0:T(8,128)(2,1)}, bf16[3,48,384]{2,1,0:T(8,128)(2,1)S(1)}, u32[]{:S(2)}, u32[]{:S(2)}) collective-permute-start(bf16[3,48,384]{2,1,0:T(8,128)(2,1)} %get-tuple-element.39), channel_id=1, source_target_pairs={{8,0},{24,16},{9,1},{25,17},{10,2},{26,18},{11,3},{27,19},{12,4},{... | collective-permute-start | bytes 331784 | tf_op jit(solution)/shard_map/ppermute | solution.py:76
  36.9 50.5 %collective-permute-start.16 = (bf16[1152,128]{1,0:T(8,128)(2,1)}, bf16[1152,128]{1,0:T(8,128)(2,1)}, u32[]{:S(2)}, u32[]{:S(2)}) collective-permute-start(bf16[1152,128]{1,0:T(8,128)(2,1)} %get-tuple-element.35), channel_id=1, source_target_pairs={{0,1},{1,0},{2,3},{3,2},{4,5},{5,4},{6,7},{7,6},{8,9},{9,8},{10,11... | collective-permute-start | bytes 884744 | tf_op jit(solution)/shard_map/ppermute | solution.py:81
  46.5 43.3 %collective-permute-start.17 = (bf16[1152,128]{1,0:T(8,128)(2,1)}, bf16[1152,128]{1,0:T(8,128)(2,1)}, u32[]{:S(2)}, u32[]{:S(2)}) collective-permute-start(bf16[1152,128]{1,0:T(8,128)(2,1)} %get-tuple-element.35), channel_id=1, source_target_pairs={{0,2},{1,3},{2,0},{3,1},{4,6},{5,7},{6,4},{7,5},{8,10},{9,11},{10,... | collective-permute-start | bytes 884744 | tf_op jit(solution)/shard_map/ppermute | solution.py:81
  87.4 24.9 %collective-permute-start.19 = (bf16[1152,128]{1,0:T(8,128)(2,1)S(1)}, bf16[1152,128]{1,0:T(8,128)(2,1)S(1)}, u32[]{:S(2)}, u32[]{:S(2)}) collective-permute-start(bf16[1152,128]{1,0:T(8,128)(2,1)S(1)} %copy-done.6), channel_id=1, source_target_pairs={{0,4},{1,5},{2,6},{3,7},{4,0},{5,1},{6,2},{7,3},{8,12},{9,13},{10,... | collective-permute-start | bytes 884744 | tf_op jit(solution)/shard_map/ppermute | solution.py:81
  89.8 22.5 %collective-permute-start.21 = (bf16[1152,128]{1,0:T(8,128)(2,1)S(1)}, bf16[1152,128]{1,0:T(8,128)(2,1)S(1)}, u32[]{:S(2)}, u32[]{:S(2)}) collective-permute-start(bf16[1152,128]{1,0:T(8,128)(2,1)S(1)} %copy-done.6), channel_id=1, source_target_pairs={{0,6},{1,7},{2,4},{3,5},{4,2},{5,3},{6,0},{7,1},{8,14},{9,15},{10,... | collective-permute-start | bytes 884744 | tf_op jit(solution)/shard_map/ppermute | solution.py:81
  91.6 21.3 %collective-permute-start.18 = (bf16[1152,128]{1,0:T(8,128)(2,1)}, bf16[1152,128]{1,0:T(8,128)(2,1)S(1)}, u32[]{:S(2)}, u32[]{:S(2)}) collective-permute-start(bf16[1152,128]{1,0:T(8,128)(2,1)} %collective-permute-done.17), channel_id=1, source_target_pairs={{0,1},{1,0},{2,3},{3,2},{4,5},{5,4},{6,7},{7,6},{8,9},{9,8},{10,11... | collective-permute-start | bytes 884744 | tf_op jit(solution)/shard_map/ppermute | solution.py:81
  93.5 28.7 %collective-permute-start.14 = (bf16[1152,256]{1,0:T(8,128)(2,1)}, bf16[1152,256]{1,0:T(8,128)(2,1)S(1)}, u32[]{:S(2)}, u32[]{:S(2)}) collective-permute-start(bf16[1152,256]{1,0:T(8,128)(2,1)} %get-tuple-element.37), channel_id=1, source_target_pairs={{0,6},{1,7},{2,4},{3,5},{4,2},{5,3},{6,0},{7,1},{8,14},{9,15},{10,... | collective-permute-start | bytes 1769480 | tf_op jit(solution)/shard_map/ppermute | solution.py:81
  112.3 7.9 %collective-permute-start.2 = (bf16[1152,384]{1,0:T(8,128)(2,1)S(1)}, bf16[1152,384]{1,0:T(8,128)(2,1)S(1)}, u32[]{:S(2)}, u32[]{:S(2)}) collective-permute-start(bf16[1152,384]{1,0:T(8,128)(2,1)S(1)} %get-tuple-element.44), channel_id=1, source_target_pairs={{0,1},{1,0},{2,3},{3,2},{4,5},{5,4},{6,7},{7,6},{8,9},{9,8},{10,11... | collective-permute-start | bytes 2654216 | tf_op jit(solution)/shard_map/ppermute | solution.py:81
  112.3 2.8 collective-permute-start.20
  112.8 6.5 %collective-permute-start.22 = (bf16[1152,128]{1,0:T(8,128)(2,1)S(1)}, bf16[1152,128]{1,0:T(8,128)(2,1)S(1)}, u32[]{:S(2)}, u32[]{:S(2)}) collective-permute-start(bf16[1152,128]{1,0:T(8,128)(2,1)S(1)} %collective-permute-done.21), channel_id=1, source_target_pairs={{0,1},{1,0},{2,3},{3,2},{4,5},{5,4},{6,7},{7,6},{8,9},{9,8},{10,11... | collective-permute-start | bytes 884744 | tf_op jit(solution)/shard_map/ppermute | solution.py:81
  115.2 22.5 %collective-permute-start.3 = (bf16[1152,384]{1,0:T(8,128)(2,1)S(1)}, bf16[1152,384]{1,0:T(8,128)(2,1)S(1)}, u32[]{:S(2)}, u32[]{:S(2)}) collective-permute-start(bf16[1152,384]{1,0:T(8,128)(2,1)S(1)} %get-tuple-element.44), channel_id=1, source_target_pairs={{0,2},{1,3},{2,0},{3,1},{4,6},{5,7},{6,4},{7,5},{8,10},{9,11},{10,... | collective-permute-start | bytes 2654216 | tf_op jit(solution)/shard_map/ppermute | solution.py:81
  117.9 40.3 %collective-permute-start.5 = (bf16[1152,384]{1,0:T(8,128)(2,1)S(1)}, bf16[1152,384]{1,0:T(8,128)(2,1)S(1)}, u32[]{:S(2)}, u32[]{:S(2)}) collective-permute-start(bf16[1152,384]{1,0:T(8,128)(2,1)S(1)} %get-tuple-element.44), channel_id=1, source_target_pairs={{0,4},{1,5},{2,6},{3,7},{4,0},{5,1},{6,2},{7,3},{8,12},{9,13},{10,... | collective-permute-start | bytes 2654216 | tf_op jit(solution)/shard_map/ppermute | solution.py:81
  119.3 39.0 %collective-permute-start.7 = (bf16[1152,384]{1,0:T(8,128)(2,1)S(1)}, bf16[1152,384]{1,0:T(8,128)(2,1)S(1)}, u32[]{:S(2)}, u32[]{:S(2)}) collective-permute-start(bf16[1152,384]{1,0:T(8,128)(2,1)S(1)} %get-tuple-element.44), channel_id=1, source_target_pairs={{0,6},{1,7},{2,4},{3,5},{4,2},{5,3},{6,0},{7,1},{8,14},{9,15},{10,... | collective-permute-start | bytes 2654216 | tf_op jit(solution)/shard_map/ppermute | solution.py:81
  120.2 38.5 %collective-permute-start.11 = (bf16[1152,256]{1,0:T(8,128)(2,1)}, bf16[1152,256]{1,0:T(8,128)(2,1)S(1)}, u32[]{:S(2)}, u32[]{:S(2)}) collective-permute-start(bf16[1152,256]{1,0:T(8,128)(2,1)} %collective-permute-done.10), channel_id=1, source_target_pairs={{0,1},{1,0},{2,3},{3,2},{4,5},{5,4},{6,7},{7,6},{8,9},{9,8},{10,11... | collective-permute-start | bytes 1769480 | tf_op jit(solution)/shard_map/ppermute | solution.py:81
  122.3 38.5 %collective-permute-start.13 = (bf16[1152,256]{1,0:T(8,128)(2,1)S(1)}, bf16[1152,256]{1,0:T(8,128)(2,1)S(1)}, u32[]{:S(2)}, u32[]{:S(2)}) collective-permute-start(bf16[1152,256]{1,0:T(8,128)(2,1)S(1)} %collective-permute-done.12), channel_id=1, source_target_pairs={{0,1},{1,0},{2,3},{3,2},{4,5},{5,4},{6,7},{7,6},{8,9},{9,8},{10,11... | collective-permute-start | bytes 1769480 | tf_op jit(solution)/shard_map/ppermute | solution.py:81
  137.6 24.9 %collective-permute-start.15 = (bf16[1152,256]{1,0:T(8,128)(2,1)S(1)}, bf16[1152,256]{1,0:T(8,128)(2,1)S(1)}, u32[]{:S(2)}, u32[]{:S(2)}) collective-permute-start(bf16[1152,256]{1,0:T(8,128)(2,1)S(1)} %collective-permute-done.14), channel_id=1, source_target_pairs={{0,1},{1,0},{2,3},{3,2},{4,5},{5,4},{6,7},{7,6},{8,9},{9,8},{10,11... | collective-permute-start | bytes 1769480 | tf_op jit(solution)/shard_map/ppermute | solution.py:81
  158.3 5.3 %collective-permute-start.4 = (bf16[1152,384]{1,0:T(8,128)(2,1)S(1)}, bf16[1152,384]{1,0:T(8,128)(2,1)S(1)}, u32[]{:S(2)}, u32[]{:S(2)}) collective-permute-start(bf16[1152,384]{1,0:T(8,128)(2,1)S(1)} %collective-permute-done.3), channel_id=1, source_target_pairs={{0,1},{1,0},{2,3},{3,2},{4,5},{5,4},{6,7},{7,6},{8,9},{9,8},{10,11... | collective-permute-start | bytes 2654216 | tf_op jit(solution)/shard_map/ppermute | solution.py:81
  158.3 7.4 %collective-permute-start.6 = (bf16[1152,384]{1,0:T(8,128)(2,1)S(1)}, bf16[1152,384]{1,0:T(8,128)(2,1)S(1)}, u32[]{:S(2)}, u32[]{:S(2)}) collective-permute-start(bf16[1152,384]{1,0:T(8,128)(2,1)S(1)} %collective-permute-done.5), channel_id=1, source_target_pairs={{0,1},{1,0},{2,3},{3,2},{4,5},{5,4},{6,7},{7,6},{8,9},{9,8},{10,11... | collective-permute-start | bytes 2654216 | tf_op jit(solution)/shard_map/ppermute | solution.py:81
  158.8 9.1 %collective-permute-start.8 = (bf16[1152,384]{1,0:T(8,128)(2,1)S(1)}, bf16[1152,384]{1,0:T(8,128)(2,1)S(1)}, u32[]{:S(2)}, u32[]{:S(2)}) collective-permute-start(bf16[1152,384]{1,0:T(8,128)(2,1)S(1)} %collective-permute-done.7), channel_id=1, source_target_pairs={{0,1},{1,0},{2,3},{3,2},{4,5},{5,4},{6,7},{7,6},{8,9},{9,8},{10,11... | collective-permute-start | bytes 2654216 | tf_op jit(solution)/shard_map/ppermute | solution.py:81
  164.6 14.5 %copy-start.12 = (f32[1536]{0:T(1024)S(1)}, f32[1536]{0:T(1024)}, u32[]{:S(2)}) copy-start(f32[1536]{0:T(1024)} %param.16) | copy-start | bytes 18436
  300.1 5.9 %collective-permute-start.24 = (bf16[1152,256]{1,0:T(8,128)(2,1)S(1)}, bf16[1152,256]{1,0:T(8,128)(2,1)S(1)}, u32[]{:S(2)}, u32[]{:S(2)}) collective-permute-start(bf16[1152,256]{1,0:T(8,128)(2,1)S(1)} %convolution_convert_fusion.6), channel_id=1, source_target_pairs={{0,1},{1,0},{2,3},{3,2},{4,5},{5,4},{6,7},{7,6},{8,9},{9,8},{10,11... | collective-permute-start | bytes 1769480 | tf_op jit(solution)/shard_map/ppermute | solution.py:81
  302.6 6.0 %collective-permute-start.26 = (bf16[1152,256]{1,0:T(8,128)(2,1)S(1)}, bf16[1152,256]{1,0:T(8,128)(2,1)S(1)}, u32[]{:S(2)}, u32[]{:S(2)}) collective-permute-start(bf16[1152,256]{1,0:T(8,128)(2,1)S(1)} %convolution_convert_fusion.5), channel_id=1, source_target_pairs={{0,1},{1,0},{2,3},{3,2},{4,5},{5,4},{6,7},{7,6},{8,9},{9,8},{10,11... | collective-permute-start | bytes 1769480 | tf_op jit(solution)/shard_map/ppermute | solution.py:81
  304.2 21.0 %collective-permute-start.23 = (bf16[1152,256]{1,0:T(8,128)(2,1)S(1)}, bf16[1152,256]{1,0:T(8,128)(2,1)S(1)}, u32[]{:S(2)}, u32[]{:S(2)}) collective-permute-start(bf16[1152,256]{1,0:T(8,128)(2,1)S(1)} %convolution_convert_fusion.7), channel_id=1, source_target_pairs={{0,1},{1,0},{2,3},{3,2},{4,5},{5,4},{6,7},{7,6},{8,9},{9,8},{10,11... | collective-permute-start | bytes 1769480 | tf_op jit(solution)/shard_map/ppermute | solution.py:81
  305.4 5.8 %collective-permute-start.28 = (bf16[1152,256]{1,0:T(8,128)(2,1)S(1)}, bf16[1152,256]{1,0:T(8,128)(2,1)S(1)}, u32[]{:S(2)}, u32[]{:S(2)}) collective-permute-start(bf16[1152,256]{1,0:T(8,128)(2,1)S(1)} %convolution_convert_fusion.4), channel_id=1, source_target_pairs={{0,1},{1,0},{2,3},{3,2},{4,5},{5,4},{6,7},{7,6},{8,9},{9,8},{10,11... | collective-permute-start | bytes 1769480 | tf_op jit(solution)/shard_map/ppermute | solution.py:81
  307.1 18.2 %collective-permute-start.25 = (bf16[1152,256]{1,0:T(8,128)(2,1)S(1)}, bf16[1152,256]{1,0:T(8,128)(2,1)S(1)}, u32[]{:S(2)}, u32[]{:S(2)}) collective-permute-start(bf16[1152,256]{1,0:T(8,128)(2,1)S(1)} %add_convert_fusion.6), channel_id=1, source_target_pairs={{0,2},{1,3},{2,0},{3,1},{4,6},{5,7},{6,4},{7,5},{8,10},{9,11},{10,... | collective-permute-start | bytes 1769480 | tf_op jit(solution)/shard_map/ppermute | solution.py:81
  309.7 27.7 %collective-permute-start.27 = (bf16[1152,256]{1,0:T(8,128)(2,1)S(1)}, bf16[1152,256]{1,0:T(8,128)(2,1)S(1)}, u32[]{:S(2)}, u32[]{:S(2)}) collective-permute-start(bf16[1152,256]{1,0:T(8,128)(2,1)S(1)} %add_convert_fusion.5), channel_id=1, source_target_pairs={{0,4},{1,5},{2,6},{3,7},{4,0},{5,1},{6,2},{7,3},{8,12},{9,13},{10,... | collective-permute-start | bytes 1769480 | tf_op jit(solution)/shard_map/ppermute | solution.py:81
  312.4 25.1 %collective-permute-start.29 = (bf16[1152,256]{1,0:T(8,128)(2,1)S(1)}, bf16[1152,256]{1,0:T(8,128)(2,1)S(1)}, u32[]{:S(2)}, u32[]{:S(2)}) collective-permute-start(bf16[1152,256]{1,0:T(8,128)(2,1)S(1)} %add_convert_fusion.4), channel_id=1, source_target_pairs={{0,6},{1,7},{2,4},{3,5},{4,2},{5,3},{6,0},{7,1},{8,14},{9,15},{10,... | collective-permute-start | bytes 1769480 | tf_op jit(solution)/shard_map/ppermute | solution.py:81
  371.9 7.5 %slice-start.2 = ((s8[9437184]{0:T(1024)(128)(4,1)}), s8[4194304]{0:T(1024)(128)(4,1)S(1)}, s32[]{:S(2)}) async-start(s8[9437184]{0:T(1024)(128)(4,1)} %bitcast.63), calls=%async_computation.5 | async-start | bytes 8388608
  375.4 8.7 %collective-permute-start.33 = (bf16[1152,384]{1,0:T(8,128)(2,1)S(1)}, bf16[1152,384]{1,0:T(8,128)(2,1)S(1)}, u32[]{:S(2)}, u32[]{:S(2)}) collective-permute-start(bf16[1152,384]{1,0:T(8,128)(2,1)S(1)} %convolution_convert_fusion), channel_id=1, source_target_pairs={{0,1},{1,0},{2,3},{3,2},{4,5},{5,4},{6,7},{7,6},{8,9},{9,8},{10,11... | collective-permute-start | bytes 2654216 | tf_op jit(solution)/shard_map/ppermute | solution.py:81
  378.8 7.3 %collective-permute-start.32 = (bf16[1152,384]{1,0:T(8,128)(2,1)S(1)}, bf16[1152,384]{1,0:T(8,128)(2,1)S(1)}, u32[]{:S(2)}, u32[]{:S(2)}) collective-permute-start(bf16[1152,384]{1,0:T(8,128)(2,1)S(1)} %convolution_convert_fusion.1), channel_id=1, source_target_pairs={{0,1},{1,0},{2,3},{3,2},{4,5},{5,4},{6,7},{7,6},{8,9},{9,8},{10,11... | collective-permute-start | bytes 2654216 | tf_op jit(solution)/shard_map/ppermute | solution.py:81
  381.4 6.8 %collective-permute-start.31 = (bf16[1152,384]{1,0:T(8,128)(2,1)S(1)}, bf16[1152,384]{1,0:T(8,128)(2,1)S(1)}, u32[]{:S(2)}, u32[]{:S(2)}) collective-permute-start(bf16[1152,384]{1,0:T(8,128)(2,1)S(1)} %convolution_convert_fusion.2), channel_id=1, source_target_pairs={{0,1},{1,0},{2,3},{3,2},{4,5},{5,4},{6,7},{7,6},{8,9},{9,8},{10,11... | collective-permute-start | bytes 2654216 | tf_op jit(solution)/shard_map/ppermute | solution.py:81
  383.6 6.7 %collective-permute-start.30 = (bf16[1152,384]{1,0:T(8,128)(2,1)S(1)}, bf16[1152,384]{1,0:T(8,128)(2,1)S(1)}, u32[]{:S(2)}, u32[]{:S(2)}) collective-permute-start(bf16[1152,384]{1,0:T(8,128)(2,1)S(1)} %convolution_convert_fusion.3), channel_id=1, source_target_pairs={{0,1},{1,0},{2,3},{3,2},{4,5},{5,4},{6,7},{7,6},{8,9},{9,8},{10,11... | collective-permute-start | bytes 2654216 | tf_op jit(solution)/shard_map/ppermute | solution.py:81
  396.5 22.6 %collective-permute-start.41 = (bf16[1152,384]{1,0:T(8,128)(2,1)S(1)}, bf16[1152,384]{1,0:T(8,128)(2,1)S(1)}, u32[]{:S(2)}, u32[]{:S(2)}) collective-permute-start(bf16[1152,384]{1,0:T(8,128)(2,1)S(1)} %add_convert_fusion.2), channel_id=1, source_target_pairs={{0,2},{1,3},{2,0},{3,1},{4,6},{5,7},{6,4},{7,5},{8,10},{9,11},{10,... | collective-permute-start | bytes 2654216 | tf_op jit(solution)/shard_map/ppermute | solution.py:81
  398.1 40.4 %collective-permute-start.42 = (bf16[1152,384]{1,0:T(8,128)(2,1)S(1)}, bf16[1152,384]{1,0:T(8,128)(2,1)S(1)}, u32[]{:S(2)}, u32[]{:S(2)}) collective-permute-start(bf16[1152,384]{1,0:T(8,128)(2,1)S(1)} %add_convert_fusion.1), channel_id=1, source_target_pairs={{0,4},{1,5},{2,6},{3,7},{4,0},{5,1},{6,2},{7,3},{8,12},{9,13},{10,... | collective-permute-start | bytes 2654216 | tf_op jit(solution)/shard_map/ppermute | solution.py:81
  399.5 39.9 %collective-permute-start.43 = (bf16[1152,384]{1,0:T(8,128)(2,1)S(1)}, bf16[1152,384]{1,0:T(8,128)(2,1)S(1)}, u32[]{:S(2)}, u32[]{:S(2)}) collective-permute-start(bf16[1152,384]{1,0:T(8,128)(2,1)S(1)} %add_convert_fusion), channel_id=1, source_target_pairs={{0,6},{1,7},{2,4},{3,5},{4,2},{5,3},{6,0},{7,1},{8,14},{9,15},{10,... | collective-permute-start | bytes 2654216 | tf_op jit(solution)/shard_map/ppermute | solution.py:81
  400.1 40.7 %collective-permute-start.34 = (bf16[1152,128]{1,0:T(8,128)(2,1)S(1)}, bf16[1152,128]{1,0:T(8,128)(2,1)S(1)}, u32[]{:S(2)}, u32[]{:S(2)}) collective-permute-start(bf16[1152,128]{1,0:T(8,128)(2,1)S(1)} %convolution_convert_fusion.11), channel_id=1, source_target_pairs={{0,1},{1,0},{2,3},{3,2},{4,5},{5,4},{6,7},{7,6},{8,9},{9,8},{10,11... | collective-permute-start | bytes 884744 | tf_op jit(solution)/shard_map/ppermute | solution.py:81
  400.1 2.0 collective-permute-start.35
  402.1 1.6 collective-permute-start.37
  403.6 1.6 collective-permute-start.39
  405.2 39.6 %collective-permute-start.36 = (bf16[1152,128]{1,0:T(8,128)(2,1)S(1)}, bf16[1152,128]{1,0:T(8,128)(2,1)S(1)}, u32[]{:S(2)}, u32[]{:S(2)}) collective-permute-start(bf16[1152,128]{1,0:T(8,128)(2,1)S(1)} %add_convert_fusion.9), channel_id=1, source_target_pairs={{0,2},{1,3},{2,0},{3,1},{4,6},{5,7},{6,4},{7,5},{8,10},{9,11},{10,... | collective-permute-start | bytes 884744 | tf_op jit(solution)/shard_map/ppermute | solution.py:81
  419.1 31.4 %collective-permute-start.38 = (bf16[1152,128]{1,0:T(8,128)(2,1)S(1)}, bf16[1152,128]{1,0:T(8,128)(2,1)S(1)}, u32[]{:S(2)}, u32[]{:S(2)}) collective-permute-start(bf16[1152,128]{1,0:T(8,128)(2,1)S(1)} %add_convert_fusion.8), channel_id=1, source_target_pairs={{0,4},{1,5},{2,6},{3,7},{4,0},{5,1},{6,2},{7,3},{8,12},{9,13},{10,... | collective-permute-start | bytes 884744 | tf_op jit(solution)/shard_map/ppermute | solution.py:81
  438.4 14.1 %collective-permute-start.40 = (bf16[1152,128]{1,0:T(8,128)(2,1)S(1)}, bf16[1152,128]{1,0:T(8,128)(2,1)S(1)}, u32[]{:S(2)}, u32[]{:S(2)}) collective-permute-start(bf16[1152,128]{1,0:T(8,128)(2,1)S(1)} %add_convert_fusion.7), channel_id=1, source_target_pairs={{0,6},{1,7},{2,4},{3,5},{4,2},{5,3},{6,0},{7,1},{8,14},{9,15},{10,... | collective-permute-start | bytes 884744 | tf_op jit(solution)/shard_map/ppermute | solution.py:81
  440.7 11.9 %collective-permute-start.44 = (f32[2,1152]{1,0:T(2,128)S(1)}, f32[2,1152]{1,0:T(2,128)S(1)}, u32[]{:S(2)}, u32[]{:S(2)}) collective-permute-start(f32[2,1152]{1,0:T(2,128)S(1)} %pad_maximum_fusion), channel_id=1, source_target_pairs={{0,1},{1,0},{2,3},{3,2},{4,5},{5,4},{6,7},{7,6},{8,9},{9,8},{10,11... | collective-permute-start | bytes 27656 | tf_op jit(solution)/shard_map/ppermute | solution.py:81
  440.7 12.4 %collective-permute-start.45 = (f32[2,1152]{1,0:T(2,128)S(1)}, f32[2,1152]{1,0:T(2,128)S(1)}, u32[]{:S(2)}, u32[]{:S(2)}) collective-permute-start(f32[2,1152]{1,0:T(2,128)S(1)} %pad_maximum_fusion), channel_id=1, source_target_pairs={{0,2},{1,3},{2,0},{3,1},{4,6},{5,7},{6,4},{7,5},{8,10},{9,11},{10,... | collective-permute-start | bytes 27656 | tf_op jit(solution)/shard_map/ppermute | solution.py:81
  444.8 16.1 %copy-start.3 = (f32[1152,256]{1,0:T(8,128)S(1)}, f32[1152,256]{1,0:T(8,128)}, u32[]{:S(2)}) copy-start(f32[1152,256]{1,0:T(8,128)} %convert_add_fusion.1) | copy-start | bytes 3538948
  444.8 16.1 %copy-start.9 = (f32[384]{0:T(512)S(1)}, f32[384]{0:T(512)}, u32[]{:S(2)}) copy-start(f32[384]{0:T(512)} %param.19) | copy-start | bytes 4612
  444.9 16.1 %copy-start.11 = (f32[384]{0:T(512)S(1)}, f32[384]{0:T(512)}, u32[]{:S(2)}) copy-start(f32[384]{0:T(512)} %param.18) | copy-start | bytes 4612
  444.9 10.2 %collective-permute-start.46 = (f32[2,1152]{1,0:T(2,128)S(1)}, f32[2,1152]{1,0:T(2,128)S(1)}, u32[]{:S(2)}, u32[]{:S(2)}) collective-permute-start(f32[2,1152]{1,0:T(2,128)S(1)} %pad_maximum_fusion), channel_id=1, source_target_pairs={{0,3},{1,2},{2,1},{3,0},{4,7},{5,6},{6,5},{7,4},{8,11},{9,10},{10,... | collective-permute-start | bytes 27656 | tf_op jit(solution)/shard_map/ppermute | solution.py:81
  450.5 4.6 collective-permute-start.47
  452.5 3.1 collective-permute-start.48
  452.5 4.7 collective-permute-start.49
  453.1 4.1 collective-permute-start.50
  458.3 4.6 collective-permute-start.51
  459.6 7.4 %collective-permute-start.52 = (bf16[3,48,384]{2,1,0:T(8,128)(2,1)S(1)}, bf16[3,48,384]{2,1,0:T(8,128)(2,1)S(1)}, u32[]{:S(2)}, u32[]{:S(2)}) collective-permute-start(bf16[3,48,384]{2,1,0:T(8,128)(2,1)S(1)} %bitcast.61), channel_id=1, source_target_pairs={{8,0},{24,16},{9,1},{25,17},{10,2},{26,18},{11,3},{27,19},{12,4},{... | collective-permute-start | bytes 331784 | tf_op jit(solution)/shard_map/ppermute | solution.py:76
  (12 other events, 46.1 us)
Sparse Core Ops, SparseCore 0:
  9.6 169.5 all-gather.5
  180.7 115.8 all-gather.7
  298.8 61.6 all-gather.3

commit v3 on v2

--- a/solution.py
+++ b/solution.py
@@ -81,6 +81,18 @@
     return lax.ppermute(value, "col", [(i, i ^ distance) for i in range(count)])
 
 
+def gather_rows(piece):
+    count = lax.axis_size("row")
+    me = lax.axis_index("row")
+    depth, wide = piece.shape
+    out = jnp.zeros((depth, wide * count), piece.dtype)
+    for distance in range(count - 1, -1, -1):
+        pairs = [(i, i ^ distance) for i in range(count)]
+        arrived = lax.ppermute(piece, "row", pairs) if distance else piece
+        out = lax.dynamic_update_slice(out, arrived, (0, (me ^ distance) * wide))
+    return out
+
+
 def gather_columns(piece):
     count = lax.axis_size("col")
     me = lax.axis_index("col")
@@ -97,7 +109,7 @@
 def pair_sums(part):
     count = lax.axis_size("col")
     me = lax.axis_index("col")
-    order = list(range(2, count, 2)) + [0]
+    order = list(range(count - 2, -1, -2))
     arrived = {d: swap(part(me ^ d ^ 1).astype(jnp.bfloat16), 1) for d in order}
     pairs = []
     for d in order:
@@ -108,7 +120,7 @@
 
 def sum_pairs(pairs):
     total = pairs[-1]
-    for index, pair in enumerate(pairs[:-1]):
+    for index, pair in enumerate(reversed(pairs[:-1])):
         total = total + swap(pair, 2 * index + 2).astype(jnp.float32)
     return total
 
@@ -130,7 +142,7 @@
     col_start = lax.axis_index("col") * narrow
     tokens = row_count * grid_width
     units = w_expand.shape[1]
-    cut = narrow * 2 // 3
+    cut = narrow // 3
     dot = functools.partial(jnp.dot, preferred_element_type=jnp.float32)
 
     def turned(left, right):
@@ -140,9 +152,7 @@
 
     owners = w_reduce.reshape(units, -1, narrow)
     expand_full = lax.all_gather(w_expand, "row", axis=0, tiled=True)
-    reduce_first = lax.all_gather(
-        owners[:, :, :cut].reshape(units, -1), "row", axis=1, tiled=True
-    )
+    reduce_first = gather_rows(owners[:, :, :cut].reshape(units, -1))
     reduce_last = lax.all_gather(
         owners[:, :, cut:].reshape(units, -1), "row", axis=1, tiled=True
     )
@@ -166,8 +176,8 @@
     grad_branch = (layer_scale * cot_f).reshape(tokens, narrow).astype(jnp.bfloat16)
     grad_first = gather_columns(grad_branch[:, :cut])
     grad_last = gather_columns(grad_branch[:, cut:])
-    expand_full, grad_first, grad_last = lax.optimization_barrier(
-        (expand_full, grad_first, grad_last)
+    expand_full, reduce_first, grad_first, grad_last = lax.optimization_barrier(
+        (expand_full, reduce_first, grad_first, grad_last)
     )
 
     preact = dot(normed_full, expand_full) + b_expand
@@ -182,10 +192,15 @@
 
     branch_first = sum_pairs(pair_sums(branch_part(reduce_first, hidden)))
     grad_hidden = turned(grad_first, reduce_first)
-    reduce_last, branch_first, grad_hidden = lax.optimization_barrier(
-        (reduce_last, branch_first, grad_hidden)
-    )
     slope = cumulative + preact * jnp.exp(-0.5 * preact * preact) * density_scale
+    vectors = jnp.stack([ln_gain, ln_bias])
+    gain_unit, bias_unit = jnp.dot(
+        vectors, expand_full.astype(jnp.float32), precision=lax.Precision.HIGHEST
+    )
+    scaled = preact - (b_expand + bias_unit)
+    reduce_last, branch_first, grad_hidden, slope, gain_unit, scaled = lax.optimization_barrier(
+        (reduce_last, branch_first, grad_hidden, slope, gain_unit, scaled)
+    )
     grad_hidden = grad_hidden + turned(grad_last, reduce_last)
     grad_preact = (grad_hidden * slope).astype(jnp.bfloat16)
 
@@ -195,16 +210,20 @@
         )
 
     grad_pairs = pair_sums(grad_part)
-    *grad_pairs, hidden = lax.optimization_barrier((*grad_pairs, hidden))
+    grad_float = grad_preact.astype(jnp.float32)
+    grad_sums = jnp.stack(
+        [jnp.sum(grad_float * gain_unit, 1), jnp.sum(grad_float * scaled, 1)]
+    )
+    distance = 1
+    while distance < lax.axis_size("col"):
+        grad_sums = grad_sums + swap(grad_sums, distance)
+        distance *= 2
+    grad_total, grad_cross = grad_sums[0], grad_sums[1]
+    hidden = lax.optimization_barrier((hidden, *grad_pairs))[0]
     grad_gain = sum_pairs(grad_pairs) * local_gain
     branch_last = sum_pairs(pair_sums(branch_part(reduce_last, hidden)))
     branch_out = jnp.concatenate([branch_first, branch_last], 1) + b_reduce
 
-    grad_sums = jnp.stack([jnp.sum(grad_gain, 1), jnp.sum(grad_gain * normal_local, 1)])
-    every_sum = grad_sums
-    for distance in range(1, lax.axis_size("col")):
-        every_sum = every_sum + swap(grad_sums, distance)
-    grad_total, grad_cross = every_sum[0], every_sum[1]
     grad_mixed = inv_std * (
         grad_gain - grad_total[:, None] / channels - normal_local * grad_cross[:, None] / channels
     )

time: 492 us -> 484 us (0.984)
  matrix products: 90.7 us -> 82.5 us
    all_gather x1 -> x0, waiting for transfers between devices: 89.9 us -> none  [body(): lax.all_gather(owners[:, :, :cut].reshape(units, -1), 'row', axis=1, tile...]
    ppermute x2, waiting for transfers between devices: 0.71 us -> 62.4 us  [halo(): lax.ppermute(field[-3:], 'row', down)]
    ppermute x0 -> x3, waiting for transfers between devices: none -> 49.6 us  [gather_rows(): arrived = lax.ppermute(piece, 'row', pairs) if distance else piece]
    all_gather x1, waiting for transfers between devices: 21.5 us -> 37.1 us  [body(): lax.all_gather(owners[:, :, cut:].reshape(units, -1), 'row', axis=1, tile...]
    ppermute x49 -> x45, waiting for transfers between devices: 99.3 us -> 85.5 us  [swap(): return lax.ppermute(value, 'col', [(i, i ^ distance) for i in range(count)])]
    all_gather x1, waiting for transfers between devices: 10.1 us -> 0.01 us  [body(): expand_full = lax.all_gather(w_expand, 'row', axis=0, tiled=True)]
    dot_general x1, matrix products: 27.6 us -> 17.7 us  [body(): preact = dot(normed_full, expand_full) + b_expand]
    ppermute x2, waiting for transfers between devices: 13.7 us -> 4.24 us  [halo(): lax.ppermute(field[:3], 'row', up)]
  transfers between devices with their start and end apart: 56 -> 54, of which waited for: 19 -> 15; matrix products, arithmetic and copies ran while one was open for 25% -> 22% of each run, Pallas kernels for 2% -> 4%
where the time goes in v3:
time: 484 us; the launch traced here: 480 us
  waiting for transfers between devices  240 us (50%)
  matrix products  82.5 us (17%)
  starting transfers between devices  44.6 us (9%)
  local copies, waits for them, and re-layouts  43.3 us (9%)
  blocking collectives  25.9 us (5%)
  Pallas kernels  19 us (4%)
  between operations  15.1 us (3%)
  other arithmetic  9.65 us (2%)
    ppermute x45, waiting for transfers between devices, swap(): return lax.ppermute(value, 'col', [(i, i ^ distance) for i in range(count)])  85.5 us
    ppermute x2, waiting for transfers between devices, halo(): lax.ppermute(field[-3:], 'row', down)  62.4 us
    ppermute x3, waiting for transfers between devices, gather_rows(): arrived = lax.ppermute(piece, 'row', pairs) if distance else piece  49.6 us
    dot_general x10, matrix products, turned(): lax.dot_general(left, right, (((1,), (1,)), ((), ())), preferred_element_...  38.4 us
    all_gather x1, waiting for transfers between devices, body(): lax.all_gather(owners[:, :, cut:].reshape(units, -1), 'row', axis=1, tile...  37.1 us
    ppermute x45, starting transfers between devices, swap(): return lax.ppermute(value, 'col', [(i, i ^ distance) for i in range(count)])  31.4 us
    psum x1, blocking collectives, body(): lax.psum((jnp.sum(local_mixed, 1), jnp.sum(local_mixed * local_mixed, 1))...  25.9 us
    dot_general x16, matrix products, branch_part(): dot(activated, lax.dynamic_slice_in_dim(weights, owner * width, width, 1))  19.1 us
  transfers between devices with their start and end apart: 54, of which 15 were waited for; matrix products, arithmetic and copies ran while one was open for 22% of the time, Pallas kernels for 4%

profile of v3, /device:TPU:0, one launch (start us, length us, event | category | flops | bytes accessed | tf_op | source)
XLA Modules:
  0.0 479.6 jit_solution(9455971537768460767)
XLA Ops:
  8.0 5.9 %reshape.58 = bf16[1536,2,384]{2,1,0:T(2,128)(2,1)} reshape(bf16[1536,768]{1,0:T(8,128)(2,1)} %param.17) | data formatting | bytes 4718592 | tf_op jit(solution)/shard_map/reshape | solution.py:153
  13.8 1.6 slice.49
  17.3 5.0 %collective-permute-start.9 = (bf16[1536,256]{1,0:T(8,128)(2,1)}, bf16[1536,256]{1,0:T(8,128)(2,1)}, u32[]{:S(2)}, u32[]{:S(2)}) collective-permute-start(bf16[1536,256]{1,0:T(8,128)(2,1)} %bitcast.54), channel_id=1, source_target_pairs={{0,24},{8,16},{16,8},{24,0},{1,25},{9,17},{17,9},{25,1},{2,26},{10... | collective-permute-start | bytes 2359304 | tf_op jit(solution)/shard_map/ppermute | solution.py:91
  23.6 2.5 collective-permute-start
  26.1 1.3 collective-permute-start.1
  27.4 1.5 copy.12
  28.9 2.8 broadcast_in_dim.11
  31.7 1.2 fusion.102
  32.9 1.4 dynamic_slice.79
  35.0 60.0 %collective-permute-done.top_ref = bf16[3,48,384]{2,1,0:T(8,128)(2,1)S(1)} collective-permute-done((bf16[3,48,384]{2,1,0:T(8,128)(2,1)S(1)}, bf16[3,48,384]{2,1,0:T(8,128)(2,1)S(1)}, u32[]{:S(2)}, u32[]{:S(2)}) %collective-permute-start) | collective-permute-done | bytes 110624 | tf_op jit(solution)/shard_map/ppermute | solution.py:76
  95.1 1.2 collective-permute-start.13
  96.3 9.0 %depthwise.1 = bf16[24,48,384]{2,1,0:T(8,128)(2,1)S(1)} custom-call(bf16[24,48,384]{2,1,0:T(8,128)(2,1)S(1)} %copy-done, bf16[3,48,384]{2,1,0:T(8,128)(2,1)S(1)} %collective-permute-done.top_ref, bf16[3,48,384]{2,1,0:T(8,128)(2,1)S(1)} %collective-permute-done.1.bottom_ref, f32[7,7,384]{2,1,0:T(8,128)S(1)} %copy-done.2), custom_call_target="tpu_custom_call" | custom-call | flops 43352064 | bytes 2654208 | tf_op jit(solution)/shard_map/depthwise/pallas_call | solution.py:53
  105.9 25.9 %all-reduce = (f32[1152]{0:T(1024)S(1)}, f32[1152]{0:T(1024)S(1)}) all-reduce(f32[1152]{0:T(1024)S(1)} %reduce_sum.43, f32[1152]{0:T(1024)S(1)} %reduce_sum.41), channel_id=1, replica_groups=mesh['row'=4,'col'=8] {'col'}, use_global_device_ids=true, to_apply=%region_3.0 | all-reduce | flops 2304 | bytes 18432 | tf_op jit(solution)/shard_map/psum | solution.py:163
  131.9 3.8 broadcast_in_dim.8
  135.7 1.5 constant_dynamic-update-slice_fusion.27
  141.1 8.7 %collective-permute-done.20 = bf16[1152,256]{1,0:T(8,128)(2,1)S(1)} collective-permute-done((bf16[1152,256]{1,0:T(8,128)(2,1)S(1)}, bf16[1152,256]{1,0:T(8,128)(2,1)S(1)}, u32[]{:S(2)}, u32[]{:S(2)}) %collective-permute-start.20) | collective-permute-done | bytes 589856 | tf_op jit(solution)/shard_map/ppermute | solution.py:81
  149.9 1.7 collective-permute-start.11
  152.5 2.4 collective-permute-start.17
  155.0 5.8 %collective-permute-done.17 = bf16[1152,128]{1,0:T(8,128)(2,1)S(1)} collective-permute-done((bf16[1152,128]{1,0:T(8,128)(2,1)}, bf16[1152,128]{1,0:T(8,128)(2,1)S(1)}, u32[]{:S(2)}, u32[]{:S(2)}) %collective-permute-start.17) | collective-permute-done | bytes 294944 | tf_op jit(solution)/shard_map/ppermute | solution.py:81
  161.7 1.4 collective-permute-done.18
  163.4 2.3 collective-permute-start.24
  166.0 1.2 constant_dynamic-update-slice_fusion.19
  167.3 7.0 %collective-permute-done.10 = bf16[1536,256]{1,0:T(8,128)(2,1)} collective-permute-done((bf16[1536,256]{1,0:T(8,128)(2,1)}, bf16[1536,256]{1,0:T(8,128)(2,1)}, u32[]{:S(2)}, u32[]{:S(2)}) %collective-permute-start.10) | collective-permute-done | bytes 786464 | tf_op jit(solution)/shard_map/ppermute | solution.py:91
  174.2 1.5 collective-permute-start.3
  175.7 1.2 constant_dynamic-update-slice_fusion.18
  177.0 42.7 %collective-permute-done.11 = bf16[1536,256]{1,0:T(8,128)(2,1)S(1)} collective-permute-done((bf16[1536,256]{1,0:T(8,128)(2,1)}, bf16[1536,256]{1,0:T(8,128)(2,1)S(1)}, u32[]{:S(2)}, u32[]{:S(2)}) %collective-permute-start.11) | collective-permute-done | bytes 786464 | tf_op jit(solution)/shard_map/ppermute | solution.py:91
  219.7 1.5 collective-permute-start.5
  221.3 1.5 collective-permute-start.7
  223.0 1.1 constant_dynamic-update-slice_fusion.26
  225.9 33.9 %collective-permute-done.5 = bf16[1152,384]{1,0:T(8,128)(2,1)S(1)} collective-permute-done((bf16[1152,384]{1,0:T(8,128)(2,1)S(1)}, bf16[1152,384]{1,0:T(8,128)(2,1)S(1)}, u32[]{:S(2)}, u32[]{:S(2)}) %collective-permute-start.5) | collective-permute-done | bytes 884768 | tf_op jit(solution)/shard_map/ppermute | solution.py:81
  268.2 1.1 constant_dynamic-update-slice_fusion.21
  270.5 7.3 %fusion.70 = f32[2,1536]{1,0:T(2,128)S(1)} fusion(bf16[3072,1536]{1,0:T(8,128)(2,1)} %all-gather.5.cloned.1.call-done, f32[1,3072]{1,0:T(1,128)S(1)} %bitcast.68, f32[1,3072]{1,0:T(1,128)S(1)} %bitcast.69), kind=kOutput, calls=%fused_computation.88 | convolution fusion | flops 113252352 | bytes 9474048 | tf_op jit(solution)/shard_map/dot_general | solution.py:197
  277.9 17.7 %broadcast_subtract_fusion = (f32[1152,1536]{1,0:T(8,128)}, bf16[1152,1536]{1,0:T(8,128)(2,1)S(1)}, f32[1152,1536]{1,0:T(8,128)}) fusion(f32[1536]{0:T(1024)S(1)} %add.280, f32[1536]{0:T(1024)S(1)} %copy-done.21, bf16[1152,3072]{1,0:T(8,128)(2,1)} %constant_dynamic-update-slice_fusion.20, bf16[3072,1536]{1,0:T(8,128)(2,1)S(1)} %copy-done.3), kind=kOutput, calls=%fused_computation.15 | convolution fusion | flops 10892869632 | bytes 34222080 | tf_op jit(solution)/shard_map/dot_general | solution.py:183
  295.6 2.6 convolution_convert_fusion.8
  304.4 2.7 collective-permute-start.32
  310.3 5.9 %fusion.105 = f32[1152,1536]{1,0:T(8,128)} fusion(bf16[1152,1024]{1,0:T(8,128)(2,1)S(1)} %copy-done.13, bf16[1536,1024]{1,0:T(8,128)(2,1)S(1)} %copy-done.9), kind=kOutput, calls=%fused_computation.158 | convolution fusion | flops 3623878656 | bytes 12582912 | tf_op jit(solution)/shard_map/dot_general | solution.py:149
  316.3 4.5 collective-permute-done.30
  322.0 37.1 %all-gather.3.cloned.1.call-done = bf16[1536,2048]{1,0:T(8,128)(2,1)} async-done(((bf16[1536,512]{1,0:T(8,128)(2,1)}), bf16[1536,2048]{1,0:T(8,128)(2,1)}) %all-gather.3.cloned.1.call-update) | async-done | bytes 6291472 | tf_op jit(solution)/shard_map/all_gather | solution.py:156
  359.0 14.6 %fusion.1 = bf16[1152,1536]{1,0:T(8,128)(2,1)S(1)} fusion(f32[1152,1536]{1,0:T(8,128)} %get-tuple-element.20, f32[1152,1536]{1,0:T(8,128)} %fusion.105, bf16[1152,2048]{1,0:T(8,128)(2,1)} %constant_dynamic-update-slice_fusion, bf16[1536,2048]{1,0:T(8,128)(2,1)} %all-gather.3.cloned.1.call-done), kind=kOutput, calls=%fused_computation.6 | convolution fusion | flops 7253065728 | bytes 28704768 | tf_op jit(solution)/shard_map/dot_general | solution.py:149
  373.7 3.4 convolution_convert_fusion.3
  377.1 4.7 fusion.2
  382.0 2.0 convolution_convert_fusion.2
  384.0 1.5 collective-permute-start.48
  385.6 2.0 convolution_convert_fusion.1
  388.2 1.6 collective-permute-start.49
  389.7 2.0 convolution_convert_fusion
  392.4 2.0 add_convert_fusion.2
  394.5 2.1 add_convert_fusion.1
  396.6 2.2 add_convert_fusion
  398.8 2.0 convert_add_fusion
  400.9 1.2 slice-done.5
  403.2 1.1 convolution_convert_fusion.5
  404.3 1.6 collective-permute-start.46
  413.5 1.6 collective-permute-start.43
  416.2 11.6 %collective-permute-done.46 = bf16[1152,384]{1,0:T(8,128)(2,1)S(1)} collective-permute-done((bf16[1152,384]{1,0:T(8,128)(2,1)S(1)}, bf16[1152,384]{1,0:T(8,128)(2,1)S(1)}, u32[]{:S(2)}, u32[]{:S(2)}) %collective-permute-start.46) | collective-permute-done | bytes 884768 | tf_op jit(solution)/shard_map/ppermute | solution.py:81
  428.9 17.9 %collective-permute-done.45 = bf16[1152,384]{1,0:T(8,128)(2,1)S(1)} collective-permute-done((bf16[1152,384]{1,0:T(8,128)(2,1)S(1)}, bf16[1152,384]{1,0:T(8,128)(2,1)S(1)}, u32[]{:S(2)}, u32[]{:S(2)}) %collective-permute-start.45) | collective-permute-done | bytes 884768 | tf_op jit(solution)/shard_map/ppermute | solution.py:81
  447.9 1.2 multiply_convert_fusion.1
  449.1 1.3 collective-permute-start.50
  450.4 2.3 collective-permute-done.50.top_ref
  452.8 1.3 collective-permute-start.51
  455.1 4.2 collective-permute-done.51.bottom_ref
  459.4 10.1 %depthwise_flipped.1 = bf16[24,48,384]{2,1,0:T(8,128)(2,1)} custom-call(bf16[24,48,384]{2,1,0:T(8,128)(2,1)S(1)} %bitcast.55, bf16[3,48,384]{2,1,0:T(8,128)(2,1)S(1)} %collective-permute-done.50.top_ref, bf16[3,48,384]{2,1,0:T(8,128)(2,1)S(1)} %collective-permute-done.51.bottom_ref, f32[7,7,384]{2,1,0:T(8,128)S(1)} %copy-done.2, ...), custom_call_target="tpu_custom_call" | custom-call | flops 43352064 | bytes 2654208 | tf_op jit(solution)/shard_map/depthwise_flipped/pallas_call | solution.py:53
  469.5 1.5 collective-permute-done.41
  471.3 1.2 fusion.10
  (201 shorter events, 48.8 us)
Async XLA Ops:
  7.2 263.3 %all-gather.5.cloned.1.call-start = ((), (), s32[]{:S(2)}) async-start(), calls=%async_computation.1 | async-start | bytes 11796480 | tf_op jit(solution)/shard_map/all_gather | solution.py:154
  7.9 14.4 %copy-start.1 = (bf16[24,48,384]{2,1,0:T(8,128)(2,1)S(1)}, bf16[24,48,384]{2,1,0:T(8,128)(2,1)}, u32[]{:S(2)}) copy-start(bf16[24,48,384]{2,1,0:T(8,128)(2,1)} %rest_0_.1) | copy-start | bytes 2654212
  7.9 14.4 %copy-start.22 = (f32[384]{0:T(512)S(1)}, f32[384]{0:T(512)}, u32[]{:S(2)}) copy-start(f32[384]{0:T(512)} %param.19) | copy-start | bytes 4612
  7.9 351.1 %all-gather.3.cloned.1.call-start = ((), (), s32[]{:S(2)}) async-start(), calls=%async_computation | async-start | bytes 7864320 | tf_op jit(solution)/shard_map/all_gather | solution.py:156
  17.3 146.1 %collective-permute-start.9 = (bf16[1536,256]{1,0:T(8,128)(2,1)}, bf16[1536,256]{1,0:T(8,128)(2,1)}, u32[]{:S(2)}, u32[]{:S(2)}) collective-permute-start(bf16[1536,256]{1,0:T(8,128)(2,1)} %bitcast.54), channel_id=1, source_target_pairs={{0,24},{8,16},{16,8},{24,0},{1,25},{9,17},{17,9},{25,1},{2,26},{10... | collective-permute-start | bytes 2359304 | tf_op jit(solution)/shard_map/ppermute | solution.py:91
  22.3 151.9 %collective-permute-start.10 = (bf16[1536,256]{1,0:T(8,128)(2,1)}, bf16[1536,256]{1,0:T(8,128)(2,1)}, u32[]{:S(2)}, u32[]{:S(2)}) collective-permute-start(bf16[1536,256]{1,0:T(8,128)(2,1)} %bitcast.54), channel_id=1, source_target_pairs={{0,16},{8,24},{16,0},{24,8},{1,17},{9,25},{17,1},{25,9},{2,18},{10... | collective-permute-start | bytes 2359304 | tf_op jit(solution)/shard_map/ppermute | solution.py:91
  23.6 113.7 %collective-permute-start.12 = (bf16[1152,128]{1,0:T(8,128)(2,1)}, bf16[1152,128]{1,0:T(8,128)(2,1)}, u32[]{:S(2)}, u32[]{:S(2)}) collective-permute-start(bf16[1152,128]{1,0:T(8,128)(2,1)} %get-tuple-element.41), channel_id=1, source_target_pairs={{0,1},{1,0},{2,3},{3,2},{4,5},{5,4},{6,7},{7,6},{8,9},{9,8},{10,11... | collective-permute-start | bytes 884744 | tf_op jit(solution)/shard_map/ppermute | solution.py:81
  23.6 71.5 %collective-permute-start = (bf16[3,48,384]{2,1,0:T(8,128)(2,1)S(1)}, bf16[3,48,384]{2,1,0:T(8,128)(2,1)S(1)}, u32[]{:S(2)}, u32[]{:S(2)}) collective-permute-start(bf16[3,48,384]{2,1,0:T(8,128)(2,1)S(1)} %get-tuple-element.44), channel_id=1, source_target_pairs={{0,8},{16,24},{1,9},{17,25},{2,10},{18,26},{3,11},{19,27},{4,12},{... | collective-permute-start | bytes 331784 | tf_op jit(solution)/shard_map/ppermute | solution.py:76
  26.1 70.2 %collective-permute-start.1 = (bf16[3,48,384]{2,1,0:T(8,128)(2,1)S(1)}, bf16[3,48,384]{2,1,0:T(8,128)(2,1)S(1)}, u32[]{:S(2)}, u32[]{:S(2)}) collective-permute-start(bf16[3,48,384]{2,1,0:T(8,128)(2,1)S(1)} %get-tuple-element.43), channel_id=1, source_target_pairs={{8,0},{24,16},{9,1},{25,17},{10,2},{26,18},{11,3},{27,19},{12,4},{... | collective-permute-start | bytes 331784 | tf_op jit(solution)/shard_map/ppermute | solution.py:76
  28.9 67.4 %copy-start.2 = (f32[7,7,384]{2,1,0:T(8,128)S(1)}, f32[7,7,384]{2,1,0:T(8,128)}, u32[]{:S(2)}) copy-start(f32[7,7,384]{2,1,0:T(8,128)} %k_ref.3) | copy-start | bytes 225796
  95.1 43.2 %collective-permute-start.13 = (bf16[1152,128]{1,0:T(8,128)(2,1)}, bf16[1152,128]{1,0:T(8,128)(2,1)}, u32[]{:S(2)}, u32[]{:S(2)}) collective-permute-start(bf16[1152,128]{1,0:T(8,128)(2,1)} %get-tuple-element.41), channel_id=1, source_target_pairs={{0,2},{1,3},{2,0},{3,1},{4,6},{5,7},{6,4},{7,5},{8,10},{9,11},{10,... | collective-permute-start | bytes 884744 | tf_op jit(solution)/shard_map/ppermute | solution.py:81
  96.3 43.8 %collective-permute-start.19 = (bf16[1152,256]{1,0:T(8,128)(2,1)}, bf16[1152,256]{1,0:T(8,128)(2,1)S(1)}, u32[]{:S(2)}, u32[]{:S(2)}) collective-permute-start(bf16[1152,256]{1,0:T(8,128)(2,1)} %get-tuple-element.39), channel_id=1, source_target_pairs={{0,1},{1,0},{2,3},{3,2},{4,5},{5,4},{6,7},{7,6},{8,9},{9,8},{10,11... | collective-permute-start | bytes 1769480 | tf_op jit(solution)/shard_map/ppermute | solution.py:81
  137.2 12.6 %collective-permute-start.20 = (bf16[1152,256]{1,0:T(8,128)(2,1)S(1)}, bf16[1152,256]{1,0:T(8,128)(2,1)S(1)}, u32[]{:S(2)}, u32[]{:S(2)}) collective-permute-start(bf16[1152,256]{1,0:T(8,128)(2,1)S(1)} %copy-done.14), channel_id=1, source_target_pairs={{0,2},{1,3},{2,0},{3,1},{4,6},{5,7},{6,4},{7,5},{8,10},{9,11},{10,... | collective-permute-start | bytes 1769480 | tf_op jit(solution)/shard_map/ppermute | solution.py:81
  138.3 14.1 %collective-permute-start.15 = (bf16[1152,128]{1,0:T(8,128)(2,1)}, bf16[1152,128]{1,0:T(8,128)(2,1)S(1)}, u32[]{:S(2)}, u32[]{:S(2)}) collective-permute-start(bf16[1152,128]{1,0:T(8,128)(2,1)} %get-tuple-element.41), channel_id=1, source_target_pairs={{0,4},{1,5},{2,6},{3,7},{4,0},{5,1},{6,2},{7,3},{8,12},{9,13},{10,... | collective-permute-start | bytes 884744 | tf_op jit(solution)/shard_map/ppermute | solution.py:81
  140.2 14.7 %collective-permute-start.14 = (bf16[1152,128]{1,0:T(8,128)(2,1)}, bf16[1152,128]{1,0:T(8,128)(2,1)S(1)}, u32[]{:S(2)}, u32[]{:S(2)}) collective-permute-start(bf16[1152,128]{1,0:T(8,128)(2,1)} %collective-permute-done.13), channel_id=1, source_target_pairs={{0,1},{1,0},{2,3},{3,2},{4,5},{5,4},{6,7},{7,6},{8,9},{9,8},{10,11... | collective-permute-start | bytes 884744 | tf_op jit(solution)/shard_map/ppermute | solution.py:81
  149.9 69.8 %collective-permute-start.11 = (bf16[1536,256]{1,0:T(8,128)(2,1)}, bf16[1536,256]{1,0:T(8,128)(2,1)S(1)}, u32[]{:S(2)}, u32[]{:S(2)}) collective-permute-start(bf16[1536,256]{1,0:T(8,128)(2,1)} %bitcast.54), channel_id=1, source_target_pairs={{0,8},{8,0},{16,24},{24,16},{1,9},{9,1},{17,25},{25,17},{2,10},{10... | collective-permute-start | bytes 2359304 | tf_op jit(solution)/shard_map/ppermute | solution.py:91
  152.5 8.4 %collective-permute-start.17 = (bf16[1152,128]{1,0:T(8,128)(2,1)}, bf16[1152,128]{1,0:T(8,128)(2,1)S(1)}, u32[]{:S(2)}, u32[]{:S(2)}) collective-permute-start(bf16[1152,128]{1,0:T(8,128)(2,1)} %get-tuple-element.41), channel_id=1, source_target_pairs={{0,6},{1,7},{2,4},{3,5},{4,2},{5,3},{6,0},{7,1},{8,14},{9,15},{10,... | collective-permute-start | bytes 884744 | tf_op jit(solution)/shard_map/ppermute | solution.py:81
  154.8 6.7 %collective-permute-start.16 = (bf16[1152,128]{1,0:T(8,128)(2,1)S(1)}, bf16[1152,128]{1,0:T(8,128)(2,1)S(1)}, u32[]{:S(2)}, u32[]{:S(2)}) collective-permute-start(bf16[1152,128]{1,0:T(8,128)(2,1)S(1)} %collective-permute-done.15), channel_id=1, source_target_pairs={{0,1},{1,0},{2,3},{3,2},{4,5},{5,4},{6,7},{7,6},{8,9},{9,8},{10,11... | collective-permute-start | bytes 884744 | tf_op jit(solution)/shard_map/ppermute | solution.py:81
  160.8 60.5 %collective-permute-start.22 = (bf16[1152,256]{1,0:T(8,128)(2,1)S(1)}, bf16[1152,256]{1,0:T(8,128)(2,1)S(1)}, u32[]{:S(2)}, u32[]{:S(2)}) collective-permute-start(bf16[1152,256]{1,0:T(8,128)(2,1)S(1)} %copy-done.14), channel_id=1, source_target_pairs={{0,4},{1,5},{2,6},{3,7},{4,0},{5,1},{6,2},{7,3},{8,12},{9,13},{10,... | collective-permute-start | bytes 1769480 | tf_op jit(solution)/shard_map/ppermute | solution.py:81
  161.5 1.6 collective-permute-start.18
  163.1 59.7 %collective-permute-start.2 = (bf16[1152,384]{1,0:T(8,128)(2,1)S(1)}, bf16[1152,384]{1,0:T(8,128)(2,1)S(1)}, u32[]{:S(2)}, u32[]{:S(2)}) collective-permute-start(bf16[1152,384]{1,0:T(8,128)(2,1)S(1)} %get-tuple-element.48), channel_id=1, source_target_pairs={{0,1},{1,0},{2,3},{3,2},{4,5},{5,4},{6,7},{7,6},{8,9},{9,8},{10,11... | collective-permute-start | bytes 2654216 | tf_op jit(solution)/shard_map/ppermute | solution.py:81
  163.3 58.0 %copy-start.12 = (bf16[1152,1024]{1,0:T(8,128)(2,1)}, bf16[1152,1024]{1,0:T(8,128)(2,1)S(1)}, u32[]{:S(2)}) copy-start(bf16[1152,1024]{1,0:T(8,128)(2,1)S(1)} %constant_dynamic-update-slice_fusion.8) | copy-start | bytes 7077892
  163.3 59.5 %copy-start.5 = (bf16[1536,2,128]{2,1,0:T(2,128)(2,1)S(1)}, bf16[1536,2,128]{2,1,0:T(2,128)(2,1)}, u32[]{:S(2)}) copy-start(bf16[1536,2,128]{2,1,0:T(2,128)(2,1)} %copy-done.4) | copy-start | bytes 2359300
  163.4 60.8 %collective-permute-start.24 = (bf16[1152,256]{1,0:T(8,128)(2,1)S(1)}, bf16[1152,256]{1,0:T(8,128)(2,1)S(1)}, u32[]{:S(2)}, u32[]{:S(2)}) collective-permute-start(bf16[1152,256]{1,0:T(8,128)(2,1)S(1)} %copy-done.14), channel_id=1, source_target_pairs={{0,6},{1,7},{2,4},{3,5},{4,2},{5,3},{6,0},{7,1},{8,14},{9,15},{10,... | collective-permute-start | bytes 1769480 | tf_op jit(solution)/shard_map/ppermute | solution.py:81
  174.2 50.5 %collective-permute-start.3 = (bf16[1152,384]{1,0:T(8,128)(2,1)S(1)}, bf16[1152,384]{1,0:T(8,128)(2,1)S(1)}, u32[]{:S(2)}, u32[]{:S(2)}) collective-permute-start(bf16[1152,384]{1,0:T(8,128)(2,1)S(1)} %get-tuple-element.48), channel_id=1, source_target_pairs={{0,2},{1,3},{2,0},{3,1},{4,6},{5,7},{6,4},{7,5},{8,10},{9,11},{10,... | collective-permute-start | bytes 2654216 | tf_op jit(solution)/shard_map/ppermute | solution.py:81
  219.7 40.1 %collective-permute-start.5 = (bf16[1152,384]{1,0:T(8,128)(2,1)S(1)}, bf16[1152,384]{1,0:T(8,128)(2,1)S(1)}, u32[]{:S(2)}, u32[]{:S(2)}) collective-permute-start(bf16[1152,384]{1,0:T(8,128)(2,1)S(1)} %get-tuple-element.48), channel_id=1, source_target_pairs={{0,4},{1,5},{2,6},{3,7},{4,0},{5,1},{6,2},{7,3},{8,12},{9,13},{10,... | collective-permute-start | bytes 2654216 | tf_op jit(solution)/shard_map/ppermute | solution.py:81
  221.3 38.5 %collective-permute-start.7 = (bf16[1152,384]{1,0:T(8,128)(2,1)S(1)}, bf16[1152,384]{1,0:T(8,128)(2,1)S(1)}, u32[]{:S(2)}, u32[]{:S(2)}) collective-permute-start(bf16[1152,384]{1,0:T(8,128)(2,1)S(1)} %get-tuple-element.48), channel_id=1, source_target_pairs={{0,6},{1,7},{2,4},{3,5},{4,2},{5,3},{6,0},{7,1},{8,14},{9,15},{10,... | collective-permute-start | bytes 2654216 | tf_op jit(solution)/shard_map/ppermute | solution.py:81
  222.8 37.5 %collective-permute-start.21 = (bf16[1152,256]{1,0:T(8,128)(2,1)S(1)}, bf16[1152,256]{1,0:T(8,128)(2,1)S(1)}, u32[]{:S(2)}, u32[]{:S(2)}) collective-permute-start(bf16[1152,256]{1,0:T(8,128)(2,1)S(1)} %collective-permute-done.20), channel_id=1, source_target_pairs={{0,1},{1,0},{2,3},{3,2},{4,5},{5,4},{6,7},{7,6},{8,9},{9,8},{10,11... | collective-permute-start | bytes 1769480 | tf_op jit(solution)/shard_map/ppermute | solution.py:81
  223.0 40.2 %copy-start.8 = (bf16[1536,1024]{1,0:T(8,128)(2,1)}, bf16[1536,1024]{1,0:T(8,128)(2,1)S(1)}, u32[]{:S(2)}) copy-start(bf16[1536,1024]{1,0:T(8,128)(2,1)S(1)} %constant_dynamic-update-slice_fusion.16) | copy-start | bytes 9437188
  224.1 38.1 %collective-permute-start.23 = (bf16[1152,256]{1,0:T(8,128)(2,1)S(1)}, bf16[1152,256]{1,0:T(8,128)(2,1)S(1)}, u32[]{:S(2)}, u32[]{:S(2)}) collective-permute-start(bf16[1152,256]{1,0:T(8,128)(2,1)S(1)} %collective-permute-done.22), channel_id=1, source_target_pairs={{0,1},{1,0},{2,3},{3,2},{4,5},{5,4},{6,7},{7,6},{8,9},{9,8},{10,11... | collective-permute-start | bytes 1769480 | tf_op jit(solution)/shard_map/ppermute | solution.py:81
  224.7 39.3 %collective-permute-start.25 = (bf16[1152,256]{1,0:T(8,128)(2,1)S(1)}, bf16[1152,256]{1,0:T(8,128)(2,1)S(1)}, u32[]{:S(2)}, u32[]{:S(2)}) collective-permute-start(bf16[1152,256]{1,0:T(8,128)(2,1)S(1)} %collective-permute-done.24), channel_id=1, source_target_pairs={{0,1},{1,0},{2,3},{3,2},{4,5},{5,4},{6,7},{7,6},{8,9},{9,8},{10,11... | collective-permute-start | bytes 1769480 | tf_op jit(solution)/shard_map/ppermute | solution.py:81
  259.8 5.2 %collective-permute-start.4 = (bf16[1152,384]{1,0:T(8,128)(2,1)S(1)}, bf16[1152,384]{1,0:T(8,128)(2,1)S(1)}, u32[]{:S(2)}, u32[]{:S(2)}) collective-permute-start(bf16[1152,384]{1,0:T(8,128)(2,1)S(1)} %collective-permute-done.3), channel_id=1, source_target_pairs={{0,1},{1,0},{2,3},{3,2},{4,5},{5,4},{6,7},{7,6},{8,9},{9,8},{10,11... | collective-permute-start | bytes 2654216 | tf_op jit(solution)/shard_map/ppermute | solution.py:81
  259.8 7.3 %collective-permute-start.6 = (bf16[1152,384]{1,0:T(8,128)(2,1)S(1)}, bf16[1152,384]{1,0:T(8,128)(2,1)S(1)}, u32[]{:S(2)}, u32[]{:S(2)}) collective-permute-start(bf16[1152,384]{1,0:T(8,128)(2,1)S(1)} %collective-permute-done.5), channel_id=1, source_target_pairs={{0,1},{1,0},{2,3},{3,2},{4,5},{5,4},{6,7},{7,6},{8,9},{9,8},{10,11... | collective-permute-start | bytes 2654216 | tf_op jit(solution)/shard_map/ppermute | solution.py:81
  260.3 9.1 %collective-permute-start.8 = (bf16[1152,384]{1,0:T(8,128)(2,1)S(1)}, bf16[1152,384]{1,0:T(8,128)(2,1)S(1)}, u32[]{:S(2)}, u32[]{:S(2)}) collective-permute-start(bf16[1152,384]{1,0:T(8,128)(2,1)S(1)} %collective-permute-done.7), channel_id=1, source_target_pairs={{0,1},{1,0},{2,3},{3,2},{4,5},{5,4},{6,7},{7,6},{8,9},{9,8},{10,11... | collective-permute-start | bytes 2654216 | tf_op jit(solution)/shard_map/ppermute | solution.py:81
  295.5 25.3 %copy-start.6 = (bf16[1152,1536]{1,0:T(8,128)(2,1)}, bf16[1152,1536]{1,0:T(8,128)(2,1)S(1)}, u32[]{:S(2)}) copy-start(bf16[1152,1536]{1,0:T(8,128)(2,1)S(1)} %get-tuple-element.21) | copy-start | bytes 10616836
  298.1 5.2 %collective-permute-start.31 = (bf16[1152,128]{1,0:T(8,128)(2,1)S(1)}, bf16[1152,128]{1,0:T(8,128)(2,1)S(1)}, u32[]{:S(2)}, u32[]{:S(2)}) collective-permute-start(bf16[1152,128]{1,0:T(8,128)(2,1)S(1)} %convolution_convert_fusion.8), channel_id=1, source_target_pairs={{0,1},{1,0},{2,3},{3,2},{4,5},{5,4},{6,7},{7,6},{8,9},{9,8},{10,11... | collective-permute-start | bytes 884744 | tf_op jit(solution)/shard_map/ppermute | solution.py:81
  300.0 7.1 %collective-permute-start.29 = (bf16[1152,128]{1,0:T(8,128)(2,1)S(1)}, bf16[1152,128]{1,0:T(8,128)(2,1)S(1)}, u32[]{:S(2)}, u32[]{:S(2)}) collective-permute-start(bf16[1152,128]{1,0:T(8,128)(2,1)S(1)} %convolution_convert_fusion.9), channel_id=1, source_target_pairs={{0,1},{1,0},{2,3},{3,2},{4,5},{5,4},{6,7},{7,6},{8,9},{9,8},{10,11... | collective-permute-start | bytes 884744 | tf_op jit(solution)/shard_map/ppermute | solution.py:81
  301.5 7.3 %collective-permute-start.27 = (bf16[1152,128]{1,0:T(8,128)(2,1)S(1)}, bf16[1152,128]{1,0:T(8,128)(2,1)S(1)}, u32[]{:S(2)}, u32[]{:S(2)}) collective-permute-start(bf16[1152,128]{1,0:T(8,128)(2,1)S(1)} %convolution_convert_fusion.10), channel_id=1, source_target_pairs={{0,1},{1,0},{2,3},{3,2},{4,5},{5,4},{6,7},{7,6},{8,9},{9,8},{10,11... | collective-permute-start | bytes 884744 | tf_op jit(solution)/shard_map/ppermute | solution.py:81
  302.8 13.5 %collective-permute-start.26 = (bf16[1152,128]{1,0:T(8,128)(2,1)S(1)}, bf16[1152,128]{1,0:T(8,128)(2,1)S(1)}, u32[]{:S(2)}, u32[]{:S(2)}) collective-permute-start(bf16[1152,128]{1,0:T(8,128)(2,1)S(1)} %convolution_convert_fusion.11), channel_id=1, source_target_pairs={{0,1},{1,0},{2,3},{3,2},{4,5},{5,4},{6,7},{7,6},{8,9},{9,8},{10,11... | collective-permute-start | bytes 884744 | tf_op jit(solution)/shard_map/ppermute | solution.py:81
  304.4 11.9 %collective-permute-start.32 = (bf16[1152,128]{1,0:T(8,128)(2,1)S(1)}, bf16[1152,128]{1,0:T(8,128)(2,1)S(1)}, u32[]{:S(2)}, u32[]{:S(2)}) collective-permute-start(bf16[1152,128]{1,0:T(8,128)(2,1)S(1)} %add_convert_fusion.7), channel_id=1, source_target_pairs={{0,6},{1,7},{2,4},{3,5},{4,2},{5,3},{6,0},{7,1},{8,14},{9,15},{10,... | collective-permute-start | bytes 884744 | tf_op jit(solution)/shard_map/ppermute | solution.py:81
  308.2 12.5 %collective-permute-start.30 = (bf16[1152,128]{1,0:T(8,128)(2,1)S(1)}, bf16[1152,128]{1,0:T(8,128)(2,1)S(1)}, u32[]{:S(2)}, u32[]{:S(2)}) collective-permute-start(bf16[1152,128]{1,0:T(8,128)(2,1)S(1)} %add_convert_fusion.8), channel_id=1, source_target_pairs={{0,4},{1,5},{2,6},{3,7},{4,0},{5,1},{6,2},{7,3},{8,12},{9,13},{10,... | collective-permute-start | bytes 884744 | tf_op jit(solution)/shard_map/ppermute | solution.py:81
  309.9 11.0 %collective-permute-start.28 = (bf16[1152,128]{1,0:T(8,128)(2,1)S(1)}, bf16[1152,128]{1,0:T(8,128)(2,1)S(1)}, u32[]{:S(2)}, u32[]{:S(2)}) collective-permute-start(bf16[1152,128]{1,0:T(8,128)(2,1)S(1)} %add_convert_fusion.9), channel_id=1, source_target_pairs={{0,2},{1,3},{2,0},{3,1},{4,6},{5,7},{6,4},{7,5},{8,10},{9,11},{10,... | collective-permute-start | bytes 884744 | tf_op jit(solution)/shard_map/ppermute | solution.py:81
  381.8 2.2 collective-permute-start.47
  384.0 4.1 collective-permute-start.48
  387.6 4.8 %collective-permute-start.33 = (bf16[1152,384]{1,0:T(8,128)(2,1)S(1)}, bf16[1152,384]{1,0:T(8,128)(2,1)S(1)}, u32[]{:S(2)}, u32[]{:S(2)}) collective-permute-start(bf16[1152,384]{1,0:T(8,128)(2,1)S(1)} %convolution_convert_fusion.3), channel_id=1, source_target_pairs={{0,1},{1,0},{2,3},{3,2},{4,5},{5,4},{6,7},{7,6},{8,9},{9,8},{10,11... | collective-permute-start | bytes 2654216 | tf_op jit(solution)/shard_map/ppermute | solution.py:81
  387.8 6.6 %collective-permute-start.34 = (bf16[1152,384]{1,0:T(8,128)(2,1)S(1)}, bf16[1152,384]{1,0:T(8,128)(2,1)S(1)}, u32[]{:S(2)}, u32[]{:S(2)}) collective-permute-start(bf16[1152,384]{1,0:T(8,128)(2,1)S(1)} %convolution_convert_fusion.2), channel_id=1, source_target_pairs={{0,1},{1,0},{2,3},{3,2},{4,5},{5,4},{6,7},{7,6},{8,9},{9,8},{10,11... | collective-permute-start | bytes 2654216 | tf_op jit(solution)/shard_map/ppermute | solution.py:81
  388.2 4.2 collective-permute-start.49
  391.8 4.8 collective-permute-start.35
  391.8 7.0 %collective-permute-start.36 = (bf16[1152,384]{1,0:T(8,128)(2,1)S(1)}, bf16[1152,384]{1,0:T(8,128)(2,1)S(1)}, u32[]{:S(2)}, u32[]{:S(2)}) collective-permute-start(bf16[1152,384]{1,0:T(8,128)(2,1)S(1)} %convolution_convert_fusion), channel_id=1, source_target_pairs={{0,1},{1,0},{2,3},{3,2},{4,5},{5,4},{6,7},{7,6},{8,9},{9,8},{10,11... | collective-permute-start | bytes 2654216 | tf_op jit(solution)/shard_map/ppermute | solution.py:81
  404.3 23.5 %collective-permute-start.46 = (bf16[1152,384]{1,0:T(8,128)(2,1)S(1)}, bf16[1152,384]{1,0:T(8,128)(2,1)S(1)}, u32[]{:S(2)}, u32[]{:S(2)}) collective-permute-start(bf16[1152,384]{1,0:T(8,128)(2,1)S(1)} %add_convert_fusion.2), channel_id=1, source_target_pairs={{0,6},{1,7},{2,4},{3,5},{4,2},{5,3},{6,0},{7,1},{8,14},{9,15},{10,... | collective-permute-start | bytes 2654216 | tf_op jit(solution)/shard_map/ppermute | solution.py:81
  405.9 40.9 %collective-permute-start.45 = (bf16[1152,384]{1,0:T(8,128)(2,1)S(1)}, bf16[1152,384]{1,0:T(8,128)(2,1)S(1)}, u32[]{:S(2)}, u32[]{:S(2)}) collective-permute-start(bf16[1152,384]{1,0:T(8,128)(2,1)S(1)} %add_convert_fusion.1), channel_id=1, source_target_pairs={{0,4},{1,5},{2,6},{3,7},{4,0},{5,1},{6,2},{7,3},{8,12},{9,13},{10,... | collective-permute-start | bytes 2654216 | tf_op jit(solution)/shard_map/ppermute | solution.py:81
  406.9 41.0 %collective-permute-start.44 = (bf16[1152,384]{1,0:T(8,128)(2,1)S(1)}, bf16[1152,384]{1,0:T(8,128)(2,1)S(1)}, u32[]{:S(2)}, u32[]{:S(2)}) collective-permute-start(bf16[1152,384]{1,0:T(8,128)(2,1)S(1)} %add_convert_fusion), channel_id=1, source_target_pairs={{0,2},{1,3},{2,0},{3,1},{4,6},{5,7},{6,4},{7,5},{8,10},{9,11},{10,... | collective-permute-start | bytes 2654216 | tf_op jit(solution)/shard_map/ppermute | solution.py:81
  407.9 2.7 collective-permute-start.42
  407.9 4.0 collective-permute-start.40
  410.6 2.9 collective-permute-start.38
  411.8 57.6 %collective-permute-start.37 = (bf16[1152,256]{1,0:T(8,128)(2,1)S(1)}, bf16[1152,256]{1,0:T(8,128)(2,1)S(1)}, u32[]{:S(2)}, u32[]{:S(2)}) collective-permute-start(bf16[1152,256]{1,0:T(8,128)(2,1)S(1)} %convolution_convert_fusion.7), channel_id=1, source_target_pairs={{0,1},{1,0},{2,3},{3,2},{4,5},{5,4},{6,7},{7,6},{8,9},{9,8},{10,11... | collective-permute-start | bytes 1769480 | tf_op jit(solution)/shard_map/ppermute | solution.py:81
  413.5 34.4 %copy-start.16 = (f32[1152]{0:T(1024)S(1)}, f32[1152]{0:T(1024)}, u32[]{:S(2)}) copy-start(f32[1152]{0:T(1024)} %copy-done.15) | copy-start | bytes 13828
  413.5 34.4 %copy-start.18 = (f32[1152]{0:T(1024)S(1)}, f32[1152]{0:T(1024)}, u32[]{:S(2)}) copy-start(f32[1152]{0:T(1024)} %copy-done.17) | copy-start | bytes 13828
  413.5 55.9 %collective-permute-start.43 = (bf16[1152,256]{1,0:T(8,128)(2,1)S(1)}, bf16[1152,256]{1,0:T(8,128)(2,1)S(1)}, u32[]{:S(2)}, u32[]{:S(2)}) collective-permute-start(bf16[1152,256]{1,0:T(8,128)(2,1)S(1)} %add_convert_fusion.4), channel_id=1, source_target_pairs={{0,6},{1,7},{2,4},{3,5},{4,2},{5,3},{6,0},{7,1},{8,14},{9,15},{10,... | collective-permute-start | bytes 1769480 | tf_op jit(solution)/shard_map/ppermute | solution.py:81
  427.8 43.1 %collective-permute-start.41 = (bf16[1152,256]{1,0:T(8,128)(2,1)S(1)}, bf16[1152,256]{1,0:T(8,128)(2,1)S(1)}, u32[]{:S(2)}, u32[]{:S(2)}) collective-permute-start(bf16[1152,256]{1,0:T(8,128)(2,1)S(1)} %add_convert_fusion.5), channel_id=1, source_target_pairs={{0,4},{1,5},{2,6},{3,7},{4,0},{5,1},{6,2},{7,3},{8,12},{9,13},{10,... | collective-permute-start | bytes 1769480 | tf_op jit(solution)/shard_map/ppermute | solution.py:81
  446.8 24.1 %collective-permute-start.39 = (bf16[1152,256]{1,0:T(8,128)(2,1)S(1)}, bf16[1152,256]{1,0:T(8,128)(2,1)S(1)}, u32[]{:S(2)}, u32[]{:S(2)}) collective-permute-start(bf16[1152,256]{1,0:T(8,128)(2,1)S(1)} %add_convert_fusion.6), channel_id=1, source_target_pairs={{0,2},{1,3},{2,0},{3,1},{4,6},{5,7},{6,4},{7,5},{8,10},{9,11},{10,... | collective-permute-start | bytes 1769480 | tf_op jit(solution)/shard_map/ppermute | solution.py:81
  449.1 3.6 collective-permute-start.50
  452.8 6.6 %collective-permute-start.51 = (bf16[3,48,384]{2,1,0:T(8,128)(2,1)S(1)}, bf16[3,48,384]{2,1,0:T(8,128)(2,1)S(1)}, u32[]{:S(2)}, u32[]{:S(2)}) collective-permute-start(bf16[3,48,384]{2,1,0:T(8,128)(2,1)S(1)} %bitcast.66), channel_id=1, source_target_pairs={{8,0},{24,16},{9,1},{25,17},{10,2},{26,18},{11,3},{27,19},{12,4},{... | collective-permute-start | bytes 331784 | tf_op jit(solution)/shard_map/ppermute | solution.py:76
  459.4 12.0 %copy-start.25 = (f32[384]{0:T(512)S(1)}, f32[384]{0:T(512)}, u32[]{:S(2)}) copy-start(f32[384]{0:T(512)} %param.18) | copy-start | bytes 4612
  (22 other events, 113.6 us)
Sparse Core Ops, SparseCore 0:
  9.6 232.3 all-gather.4
  243.6 115.4 all-gather.2

commit v4 on v3

--- a/solution.py
+++ b/solution.py
@@ -81,18 +81,6 @@
     return lax.ppermute(value, "col", [(i, i ^ distance) for i in range(count)])
 
 
-def gather_rows(piece):
-    count = lax.axis_size("row")
-    me = lax.axis_index("row")
-    depth, wide = piece.shape
-    out = jnp.zeros((depth, wide * count), piece.dtype)
-    for distance in range(count - 1, -1, -1):
-        pairs = [(i, i ^ distance) for i in range(count)]
-        arrived = lax.ppermute(piece, "row", pairs) if distance else piece
-        out = lax.dynamic_update_slice(out, arrived, (0, (me ^ distance) * wide))
-    return out
-
-
 def gather_columns(piece):
     count = lax.axis_size("col")
     me = lax.axis_index("col")
@@ -106,22 +94,46 @@
     return out
 
 
-def pair_sums(part):
+def pair_sums(part, operand):
     count = lax.axis_size("col")
     me = lax.axis_index("col")
     order = list(range(count - 2, -1, -2))
-    arrived = {d: swap(part(me ^ d ^ 1).astype(jnp.bfloat16), 1) for d in order}
+    arrived = {}
     pairs = []
-    for d in order:
-        pair = part(me ^ d) + arrived[d].astype(jnp.float32)
-        pairs.append(pair.astype(jnp.bfloat16) if d else pair)
-    return pairs
-
-
-def sum_pairs(pairs):
+
+    def send(d):
+        nonlocal operand
+        term = part(operand, me ^ d ^ 1).astype(jnp.bfloat16)
+        operand, term = lax.optimization_barrier((operand, term))
+        arrived[d] = swap(term, 1)
+
+    def add(d):
+        nonlocal operand
+        pair = part(operand, me ^ d) + arrived[d].astype(jnp.float32)
+        pair = pair.astype(jnp.bfloat16) if d else pair
+        operand, pair = lax.optimization_barrier((operand, pair))
+        pairs.append(pair)
+
+    ahead = min(3, len(order))
+    for d in order[:ahead]:
+        send(d)
+    for index, d in enumerate(order):
+        add(d)
+        if index >= 1 and index + ahead - 1 < len(order):
+            send(order[index + ahead - 1])
+    return pairs, operand
+
+
+def exchange(pairs):
+    count = lax.axis_size("col")
+    return [swap(pair, count - 2 - 2 * i) for i, pair in enumerate(pairs[:-1])]
+
+
+def sum_pairs(pairs, received=None):
+    received = exchange(pairs) if received is None else received
     total = pairs[-1]
-    for index, pair in enumerate(reversed(pairs[:-1])):
-        total = total + swap(pair, 2 * index + 2).astype(jnp.float32)
+    for piece in received:
+        total = total + piece.astype(jnp.float32)
     return total
 
 
@@ -142,7 +154,7 @@
     col_start = lax.axis_index("col") * narrow
     tokens = row_count * grid_width
     units = w_expand.shape[1]
-    cut = narrow // 3
+    cut = narrow * 2 // 3
     dot = functools.partial(jnp.dot, preferred_element_type=jnp.float32)
 
     def turned(left, right):
@@ -152,7 +164,9 @@
 
     owners = w_reduce.reshape(units, -1, narrow)
     expand_full = lax.all_gather(w_expand, "row", axis=0, tiled=True)
-    reduce_first = gather_rows(owners[:, :, :cut].reshape(units, -1))
+    reduce_first = lax.all_gather(
+        owners[:, :, :cut].reshape(units, -1), "row", axis=1, tiled=True
+    )
     reduce_last = lax.all_gather(
         owners[:, :, cut:].reshape(units, -1), "row", axis=1, tiled=True
     )
@@ -176,8 +190,8 @@
     grad_branch = (layer_scale * cot_f).reshape(tokens, narrow).astype(jnp.bfloat16)
     grad_first = gather_columns(grad_branch[:, :cut])
     grad_last = gather_columns(grad_branch[:, cut:])
-    expand_full, reduce_first, grad_first, grad_last = lax.optimization_barrier(
-        (expand_full, reduce_first, grad_first, grad_last)
+    expand_full, grad_first, grad_last = lax.optimization_barrier(
+        (expand_full, grad_first, grad_last)
     )
 
     preact = dot(normed_full, expand_full) + b_expand
@@ -186,11 +200,14 @@
 
     def branch_part(weights, activated):
         width = weights.shape[1] // lax.axis_size("col")
-        return lambda owner: dot(
-            activated, lax.dynamic_slice_in_dim(weights, owner * width, width, 1)
-        )
-
-    branch_first = sum_pairs(pair_sums(branch_part(reduce_first, hidden)))
+        return pair_sums(
+            lambda operand, owner: dot(
+                operand, lax.dynamic_slice_in_dim(weights, owner * width, width, 1)
+            ),
+            activated,
+        )[0]
+
+    branch_first = sum_pairs(branch_part(reduce_first, hidden))
     grad_hidden = turned(grad_first, reduce_first)
     slope = cumulative + preact * jnp.exp(-0.5 * preact * preact) * density_scale
     vectors = jnp.stack([ln_gain, ln_bias])
@@ -204,12 +221,10 @@
     grad_hidden = grad_hidden + turned(grad_last, reduce_last)
     grad_preact = (grad_hidden * slope).astype(jnp.bfloat16)
 
-    def grad_part(owner):
-        return turned(
-            grad_preact, lax.dynamic_slice_in_dim(expand_full, owner * narrow, narrow, 0)
-        )
-
-    grad_pairs = pair_sums(grad_part)
+    def grad_part(operand, owner):
+        return turned(operand, lax.dynamic_slice_in_dim(expand_full, owner * narrow, narrow, 0))
+
+    grad_pairs, grad_preact = pair_sums(grad_part, grad_preact)
     grad_float = grad_preact.astype(jnp.float32)
     grad_sums = jnp.stack(
         [jnp.sum(grad_float * gain_unit, 1), jnp.sum(grad_float * scaled, 1)]
@@ -219,9 +234,10 @@
         grad_sums = grad_sums + swap(grad_sums, distance)
         distance *= 2
     grad_total, grad_cross = grad_sums[0], grad_sums[1]
-    hidden = lax.optimization_barrier((hidden, *grad_pairs))[0]
-    grad_gain = sum_pairs(grad_pairs) * local_gain
-    branch_last = sum_pairs(pair_sums(branch_part(reduce_last, hidden)))
+    received = exchange(grad_pairs)
+    hidden = lax.optimization_barrier((hidden, *received[:-1], grad_pairs[-1]))[0]
+    grad_gain = sum_pairs(grad_pairs, received) * local_gain
+    branch_last = sum_pairs(branch_part(reduce_last, hidden))
     branch_out = jnp.concatenate([branch_first, branch_last], 1) + b_reduce
 
     grad_mixed = inv_std * (

time: 484 us -> 491 us (1.014)
  waiting for transfers between devices: 240 us -> 256 us
  starting transfers between devices: 44.6 us -> 36.2 us
  matrix products: 82.5 us -> 89.6 us
    all_gather x0 -> x1, waiting for transfers between devices: none -> 90.2 us  [body(): lax.all_gather(owners[:, :, :cut].reshape(units, -1), 'row', axis=1, tile...]
    ppermute x2, waiting for transfers between devices: 62.4 us -> 0.01 us  [halo(): lax.ppermute(field[-3:], 'row', down)]
    ppermute x3 -> x0, waiting for transfers between devices: 49.6 us -> none  [gather_rows(): arrived = lax.ppermute(piece, 'row', pairs) if distance else piece]
    ppermute x45, waiting for transfers between devices: 85.5 us -> 112 us  [swap(): return lax.ppermute(value, 'col', [(i, i ^ distance) for i in range(count)])]
    all_gather x1, waiting for transfers between devices: 0.01 us -> 18.3 us  [body(): expand_full = lax.all_gather(w_expand, 'row', axis=0, tiled=True)]
    all_gather x1, waiting for transfers between devices: 37.1 us -> 20.5 us  [body(): lax.all_gather(owners[:, :, cut:].reshape(units, -1), 'row', axis=1, tile...]
    ppermute x2, waiting for transfers between devices: 4.24 us -> 13.3 us  [halo(): lax.ppermute(field[:3], 'row', up)]
    ppermute x3 -> x0, starting transfers between devices: 6.74 us -> none  [gather_rows(): arrived = lax.ppermute(piece, 'row', pairs) if distance else piece]
  transfers between devices with their start and end apart: 54 -> 52, of which waited for: 15 -> 19; matrix products, arithmetic and copies ran while one was open for 22% -> 25% of each run, Pallas kernels for 4% -> 4%
where the time goes in v4:
time: 491 us; the launch traced here: 487 us
  waiting for transfers between devices  256 us (52%)
  matrix products  89.6 us (18%)
  local copies, waits for them, and re-layouts  39.5 us (8%)
  starting transfers between devices  36.2 us (7%)
  blocking collectives  24.8 us (5%)
  Pallas kernels  18.5 us (4%)
  between operations  14.8 us (3%)
  other arithmetic  7.57 us (2%)
    ppermute x45, waiting for transfers between devices, swap(): return lax.ppermute(value, 'col', [(i, i ^ distance) for i in range(count)])  112 us
    all_gather x1, waiting for transfers between devices, body(): lax.all_gather(owners[:, :, :cut].reshape(units, -1), 'row', axis=1, tile...  90.2 us
    dot_general x10, matrix products, turned(): lax.dot_general(left, right, (((1,), (1,)), ((), ())), preferred_element_...  41.2 us
    ppermute x45, starting transfers between devices, swap(): return lax.ppermute(value, 'col', [(i, i ^ distance) for i in range(count)])  28.7 us
    psum x1, blocking collectives, body(): lax.psum((jnp.sum(local_mixed, 1), jnp.sum(local_mixed * local_mixed, 1))...  24.8 us
    dot_general x16, matrix products, branch_part(): dot(operand, lax.dynamic_slice_in_dim(weights, owner * width, width, 1))  21.2 us
    all_gather x1, waiting for transfers between devices, body(): lax.all_gather(owners[:, :, cut:].reshape(units, -1), 'row', axis=1, tile...  20.5 us
    dot_general x1, matrix products, body(): preact = dot(normed_full, expand_full) + b_expand  19.9 us
  transfers between devices with their start and end apart: 52, of which 19 were waited for; matrix products, arithmetic and copies ran while one was open for 25% of the time, Pallas kernels for 4%

profile of v4, /device:TPU:0, one launch (start us, length us, event | category | flops | bytes accessed | tf_op | source)
XLA Modules:
  0.0 486.5 jit_solution(11151925300130951206)
XLA Ops:
  7.9 5.8 %reshape.58 = bf16[1536,2,384]{2,1,0:T(2,128)(2,1)} reshape(bf16[1536,768]{1,0:T(8,128)(2,1)} %param.17) | data formatting | bytes 4718592 | tf_op jit(solution)/shard_map/reshape | solution.py:165
  13.7 1.4 slice-done.3
  15.1 1.5 copy.13
  18.4 2.5 collective-permute-start.17
  20.9 1.5 collective-permute-start.19
  22.5 3.5 collective-permute-start
  26.0 1.3 collective-permute-start.1
  28.3 2.7 broadcast_in_dim.7
  31.0 1.2 fusion.105
  33.0 1.4 dynamic_slice.79
  34.8 9.6 %collective-permute-done.1.bottom_ref = bf16[3,48,384]{2,1,0:T(8,128)(2,1)S(1)} collective-permute-done((bf16[3,48,384]{2,1,0:T(8,128)(2,1)S(1)}, bf16[3,48,384]{2,1,0:T(8,128)(2,1)S(1)}, u32[]{:S(2)}, u32[]{:S(2)}) %collective-permute-start.1) | collective-permute-done | bytes 110624 | tf_op jit(solution)/shard_map/ppermute | solution.py:76
  44.4 8.6 %depthwise.1 = bf16[24,48,384]{2,1,0:T(8,128)(2,1)S(1)} custom-call(bf16[24,48,384]{2,1,0:T(8,128)(2,1)S(1)} %copy-done, bf16[3,48,384]{2,1,0:T(8,128)(2,1)S(1)} %collective-permute-done.top_ref, bf16[3,48,384]{2,1,0:T(8,128)(2,1)S(1)} %collective-permute-done.1.bottom_ref, f32[7,7,384]{2,1,0:T(8,128)S(1)} %copy-done.2), custom_call_target="tpu_custom_call" | custom-call | flops 43352064 | bytes 2654208 | tf_op jit(solution)/shard_map/depthwise/pallas_call | solution.py:53
  53.6 24.8 %all-reduce = (f32[1152]{0:T(1024)S(1)}, f32[1152]{0:T(1024)S(1)}) all-reduce(f32[1152]{0:T(1024)S(1)} %reduce_sum.43, f32[1152]{0:T(1024)S(1)} %reduce_sum.41), channel_id=1, replica_groups=mesh['row'=4,'col'=8] {'col'}, use_global_device_ids=true, to_apply=%region_3.0 | all-reduce | flops 2304 | bytes 18432 | tf_op jit(solution)/shard_map/psum | solution.py:177
  78.4 3.8 broadcast_in_dim.6
  82.2 1.4 constant_dynamic-update-slice_fusion.23
  84.7 1.6 collective-permute-start.12
  88.5 8.6 %collective-permute-done.10 = bf16[1152,256]{1,0:T(8,128)(2,1)S(1)} collective-permute-done((bf16[1152,256]{1,0:T(8,128)(2,1)S(1)}, bf16[1152,256]{1,0:T(8,128)(2,1)S(1)}, u32[]{:S(2)}, u32[]{:S(2)}) %collective-permute-start.10) | collective-permute-done | bytes 589856 | tf_op jit(solution)/shard_map/ppermute | solution.py:81
  97.1 1.8 collective-permute-start.14
  101.6 1.2 collective-permute-done.20
  103.3 1.4 collective-permute-start.5
  104.7 6.9 %collective-permute-done.12 = bf16[1152,256]{1,0:T(8,128)(2,1)S(1)} collective-permute-done((bf16[1152,256]{1,0:T(8,128)(2,1)S(1)}, bf16[1152,256]{1,0:T(8,128)(2,1)S(1)}, u32[]{:S(2)}, u32[]{:S(2)}) %collective-permute-start.12) | collective-permute-done | bytes 589856 | tf_op jit(solution)/shard_map/ppermute | solution.py:81
  112.9 1.2 constant_dynamic-update-slice_fusion.22
  114.6 17.8 %collective-permute-done.3 = bf16[1152,384]{1,0:T(8,128)(2,1)S(1)} collective-permute-done((bf16[1152,384]{1,0:T(8,128)(2,1)S(1)}, bf16[1152,384]{1,0:T(8,128)(2,1)S(1)}, u32[]{:S(2)}, u32[]{:S(2)}) %collective-permute-start.3) | collective-permute-done | bytes 884768 | tf_op jit(solution)/shard_map/ppermute | solution.py:81
  133.5 16.8 %collective-permute-done.5 = bf16[1152,384]{1,0:T(8,128)(2,1)S(1)} collective-permute-done((bf16[1152,384]{1,0:T(8,128)(2,1)S(1)}, bf16[1152,384]{1,0:T(8,128)(2,1)S(1)}, u32[]{:S(2)}, u32[]{:S(2)}) %collective-permute-start.5) | collective-permute-done | bytes 884768 | tf_op jit(solution)/shard_map/ppermute | solution.py:81
  159.6 1.2 constant_dynamic-update-slice_fusion.16
  160.8 18.3 %all-gather.6.cloned.1.call-done = bf16[3072,1536]{1,0:T(8,128)(2,1)} async-done(((bf16[768,1536]{1,0:T(8,128)(2,1)}), bf16[3072,1536]{1,0:T(8,128)(2,1)}) %all-gather.6.cloned.1.call-update) | async-done | bytes 9437200 | tf_op jit(solution)/shard_map/all_gather | solution.py:166
  179.1 7.3 %fusion.72 = f32[2,1536]{1,0:T(2,128)S(1)} fusion(bf16[3072,1536]{1,0:T(8,128)(2,1)} %all-gather.6.cloned.1.call-done, f32[1,3072]{1,0:T(1,128)S(1)} %bitcast.68, f32[1,3072]{1,0:T(1,128)S(1)} %bitcast.69), kind=kOutput, calls=%fused_computation.90 | convolution fusion | flops 113252352 | bytes 9474048 | tf_op jit(solution)/shard_map/dot_general | solution.py:214
  186.5 19.9 %broadcast_subtract_fusion = (f32[1152,1536]{1,0:T(8,128)}, bf16[1152,1536]{1,0:T(8,128)(2,1)}, f32[1152,1536]{1,0:T(8,128)}) fusion(f32[1536]{0:T(1024)S(1)} %add.264, f32[1536]{0:T(1024)S(1)} %copy-done.16, bf16[1152,3072]{1,0:T(8,128)(2,1)} %constant_dynamic-update-slice_fusion.16, bf16[3072,1536]{1,0:T(8,128)(2,1)S(1)} %copy-done.3), kind=kOutput, calls=%fused_computation.15 | convolution fusion | flops 10892869632 | bytes 34222080 | tf_op jit(solution)/shard_map/dot_general | solution.py:197
  206.4 90.2 %all-gather.8.cloned.1.call-done = bf16[1536,2048]{1,0:T(8,128)(2,1)} async-done(((bf16[1536,512]{1,0:T(8,128)(2,1)}), bf16[1536,2048]{1,0:T(8,128)(2,1)}) %all-gather.8.cloned.1.call-update) | async-done | bytes 6291472 | tf_op jit(solution)/shard_map/all_gather | solution.py:167
  296.6 3.4 convolution_convert_fusion.7
  300.2 2.4 convolution_convert_fusion.6
  305.5 1.1 add_convert_fusion.5
  306.6 1.1 convolution_convert_fusion.4
  309.4 1.5 collective-permute-start.29
  310.9 1.5 collective-permute-start.28
  312.9 11.4 %fusion.107 = f32[1152,1536]{1,0:T(8,128)} fusion(bf16[1152,2048]{1,0:T(8,128)(2,1)} %constant_dynamic-update-slice_fusion.8, bf16[1536,2048]{1,0:T(8,128)(2,1)S(1)} %bitcast.71), kind=kOutput, calls=%fused_computation.156 | convolution fusion | flops 7247757312 | bytes 18087936 | tf_op jit(solution)/shard_map/dot_general | solution.py:161
  325.6 12.9 %collective-permute-done.28 = bf16[1152,256]{1,0:T(8,128)(2,1)S(1)} collective-permute-done((bf16[1152,256]{1,0:T(8,128)(2,1)S(1)}, bf16[1152,256]{1,0:T(8,128)(2,1)S(1)}, u32[]{:S(2)}, u32[]{:S(2)}) %collective-permute-start.28) | collective-permute-done | bytes 589856 | tf_op jit(solution)/shard_map/ppermute | solution.py:81
  338.5 1.3 convert_add_fusion.1
  339.9 20.5 %all-gather.4.cloned.1.call-done = bf16[1536,1024]{1,0:T(8,128)(2,1)} async-done(((bf16[1536,256]{1,0:T(8,128)(2,1)}), bf16[1536,1024]{1,0:T(8,128)(2,1)}) %all-gather.4.cloned.1.call-update) | async-done | bytes 3145744 | tf_op jit(solution)/shard_map/all_gather | solution.py:170
  360.4 10.6 %fusion.1 = bf16[1152,1536]{1,0:T(8,128)(2,1)S(1)} fusion(f32[1152,1536]{1,0:T(8,128)} %get-tuple-element.79, f32[1152,1536]{1,0:T(8,128)} %fusion.107, bf16[1152,1024]{1,0:T(8,128)(2,1)} %copy-done.11, bf16[1536,1024]{1,0:T(8,128)(2,1)} %all-gather.4.cloned.1.call-done), kind=kOutput, calls=%fused_computation.6 | convolution fusion | flops 3629187072 | bytes 23199744 | tf_op jit(solution)/shard_map/dot_general | solution.py:161
  371.0 3.4 convolution_convert_fusion.3
  374.6 3.4 convolution_convert_fusion.2
  378.4 2.0 convolution_convert_fusion.1
  380.6 2.0 add_convert_fusion.2
  382.7 2.0 add_convert_fusion.1
  384.7 2.2 convolution_convert_fusion
  387.4 2.0 add_convert_fusion
  389.5 1.5 collective-permute-start.33
  391.0 1.5 collective-permute-start.31
  392.5 2.0 convert_add_fusion
  394.6 1.6 fusion.2
  396.9 33.2 %collective-permute-done.33 = bf16[1152,384]{1,0:T(8,128)(2,1)S(1)} collective-permute-done((bf16[1152,384]{1,0:T(8,128)(2,1)S(1)}, bf16[1152,384]{1,0:T(8,128)(2,1)S(1)}, u32[]{:S(2)}, u32[]{:S(2)}) %collective-permute-start.33) | collective-permute-done | bytes 884768 | tf_op jit(solution)/shard_map/ppermute | solution.py:81
  430.2 1.6 collective-permute-start.45
  433.9 1.6 collective-permute-start.46
  437.7 1.2 multiply_convert_fusion.1
  438.9 1.3 collective-permute-start.47
  440.2 1.3 collective-permute-start.48
  443.2 3.7 collective-permute-done.48.bottom_ref
  446.9 9.9 %depthwise_flipped.1 = bf16[24,48,384]{2,1,0:T(8,128)(2,1)} custom-call(bf16[24,48,384]{2,1,0:T(8,128)(2,1)S(1)} %bitcast.53, bf16[3,48,384]{2,1,0:T(8,128)(2,1)S(1)} %collective-permute-done.47.top_ref, bf16[3,48,384]{2,1,0:T(8,128)(2,1)S(1)} %collective-permute-done.48.bottom_ref, f32[7,7,384]{2,1,0:T(8,128)S(1)} %copy-done.2, ...), custom_call_target="tpu_custom_call" | custom-call | flops 43352064 | bytes 2654208 | tf_op jit(solution)/shard_map/depthwise_flipped/pallas_call | solution.py:53
  461.4 1.5 collective-permute-start.42
  462.9 1.5 collective-permute-start.41
  466.0 5.2 %collective-permute-done.42 = bf16[1152,128]{1,0:T(8,128)(2,1)S(1)} collective-permute-done((bf16[1152,128]{1,0:T(8,128)(2,1)S(1)}, bf16[1152,128]{1,0:T(8,128)(2,1)S(1)}, u32[]{:S(2)}, u32[]{:S(2)}) %collective-permute-start.42) | collective-permute-done | bytes 294944 | tf_op jit(solution)/shard_map/ppermute | solution.py:81
  471.2 7.1 %collective-permute-done.41 = bf16[1152,128]{1,0:T(8,128)(2,1)S(1)} collective-permute-done((bf16[1152,128]{1,0:T(8,128)(2,1)S(1)}, bf16[1152,128]{1,0:T(8,128)(2,1)S(1)}, u32[]{:S(2)}, u32[]{:S(2)}) %collective-permute-start.41) | collective-permute-done | bytes 294944 | tf_op jit(solution)/shard_map/ppermute | solution.py:81
  478.5 1.2 fusion.10
  (190 shorter events, 44.6 us)
Async XLA Ops:
  7.2 172.0 %all-gather.6.cloned.1.call-start = ((), (), s32[]{:S(2)}) async-start(), calls=%async_computation.1 | async-start | bytes 11796480 | tf_op jit(solution)/shard_map/all_gather | solution.py:166
  7.9 288.7 %all-gather.8.cloned.1.call-start = ((), (), s32[]{:S(2)}) async-start(), calls=%async_computation.2 | async-start | bytes 7864320 | tf_op jit(solution)/shard_map/all_gather | solution.py:167
  16.6 10.6 %slice-start.4 = ((bf16[1536,2,384]{2,1,0:T(2,128)(2,1)}), bf16[1536,2,128]{2,1,0:T(2,128)(2,1)S(1)}, s32[]{:S(2)}) async-start(bf16[1536,2,384]{2,1,0:T(2,128)(2,1)} %reshape.58), calls=%async_computation.7 | async-start | bytes 1572864 | tf_op jit(solution)/shard_map/slice | solution.py:171
  16.7 343.8 %all-gather.4.cloned.1.call-start = ((), (), s32[]{:S(2)}) async-start(), calls=%async_computation | async-start | bytes 3932160 | tf_op jit(solution)/shard_map/all_gather | solution.py:170
  16.9 11.3 %copy-start.7 = (bf16[24,48,384]{2,1,0:T(8,128)(2,1)}, bf16[24,48,384]{2,1,0:T(8,128)(2,1)S(1)}, u32[]{:S(2)}) copy-start(bf16[24,48,384]{2,1,0:T(8,128)(2,1)S(1)} %multiply_convert_fusion.2) | copy-start | bytes 2654212
  18.0 10.3 %copy-start.9 = (bf16[1152,1024]{1,0:T(8,128)(2,1)}, bf16[1152,1024]{1,0:T(8,128)(2,1)S(1)}, u32[]{:S(2)}) copy-start(bf16[1152,1024]{1,0:T(8,128)(2,1)S(1)} %get-tuple-element.130) | copy-start | bytes 7077892
  18.0 65.7 %collective-permute-start.16 = (bf16[1152,128]{1,0:T(8,128)(2,1)}, bf16[1152,128]{1,0:T(8,128)(2,1)}, u32[]{:S(2)}, u32[]{:S(2)}) collective-permute-start(bf16[1152,128]{1,0:T(8,128)(2,1)} %get-tuple-element.129), channel_id=1, source_target_pairs={{0,1},{1,0},{2,3},{3,2},{4,5},{5,4},{6,7},{7,6},{8,9},{9,8},{10,11... | collective-permute-start | bytes 884744 | tf_op jit(solution)/shard_map/ppermute | solution.py:81
  18.4 66.3 %collective-permute-start.17 = (bf16[1152,128]{1,0:T(8,128)(2,1)}, bf16[1152,128]{1,0:T(8,128)(2,1)}, u32[]{:S(2)}, u32[]{:S(2)}) collective-permute-start(bf16[1152,128]{1,0:T(8,128)(2,1)} %get-tuple-element.129), channel_id=1, source_target_pairs={{0,2},{1,3},{2,0},{3,1},{4,6},{5,7},{6,4},{7,5},{8,10},{9,11},{10,... | collective-permute-start | bytes 884744 | tf_op jit(solution)/shard_map/ppermute | solution.py:81
  20.9 78.9 %collective-permute-start.19 = (bf16[1152,128]{1,0:T(8,128)(2,1)}, bf16[1152,128]{1,0:T(8,128)(2,1)}, u32[]{:S(2)}, u32[]{:S(2)}) collective-permute-start(bf16[1152,128]{1,0:T(8,128)(2,1)} %get-tuple-element.129), channel_id=1, source_target_pairs={{0,4},{1,5},{2,6},{3,7},{4,0},{5,1},{6,2},{7,3},{8,12},{9,13},{10,... | collective-permute-start | bytes 884744 | tf_op jit(solution)/shard_map/ppermute | solution.py:81
  22.5 11.9 %collective-permute-start = (bf16[3,48,384]{2,1,0:T(8,128)(2,1)S(1)}, bf16[3,48,384]{2,1,0:T(8,128)(2,1)S(1)}, u32[]{:S(2)}, u32[]{:S(2)}) collective-permute-start(bf16[3,48,384]{2,1,0:T(8,128)(2,1)S(1)} %get-tuple-element.134), channel_id=1, source_target_pairs={{0,8},{16,24},{1,9},{17,25},{2,10},{18,26},{3,11},{19,27},{4,12},{... | collective-permute-start | bytes 331784 | tf_op jit(solution)/shard_map/ppermute | solution.py:76
  26.0 18.5 %collective-permute-start.1 = (bf16[3,48,384]{2,1,0:T(8,128)(2,1)S(1)}, bf16[3,48,384]{2,1,0:T(8,128)(2,1)S(1)}, u32[]{:S(2)}, u32[]{:S(2)}) collective-permute-start(bf16[3,48,384]{2,1,0:T(8,128)(2,1)S(1)} %get-tuple-element.133), channel_id=1, source_target_pairs={{8,0},{24,16},{9,1},{25,17},{10,2},{26,18},{11,3},{27,19},{12,4},{... | collective-permute-start | bytes 331784 | tf_op jit(solution)/shard_map/ppermute | solution.py:76
  28.3 16.1 %copy-start.2 = (f32[7,7,384]{2,1,0:T(8,128)S(1)}, f32[7,7,384]{2,1,0:T(8,128)}, u32[]{:S(2)}) copy-start(f32[7,7,384]{2,1,0:T(8,128)} %k_ref.3) | copy-start | bytes 225796
  34.4 65.5 %collective-permute-start.21 = (bf16[1152,128]{1,0:T(8,128)(2,1)}, bf16[1152,128]{1,0:T(8,128)(2,1)}, u32[]{:S(2)}, u32[]{:S(2)}) collective-permute-start(bf16[1152,128]{1,0:T(8,128)(2,1)} %get-tuple-element.129), channel_id=1, source_target_pairs={{0,6},{1,7},{2,4},{3,5},{4,2},{5,3},{6,0},{7,1},{8,14},{9,15},{10,... | collective-permute-start | bytes 884744 | tf_op jit(solution)/shard_map/ppermute | solution.py:81
  44.4 43.0 %collective-permute-start.9 = (bf16[1152,256]{1,0:T(8,128)(2,1)}, bf16[1152,256]{1,0:T(8,128)(2,1)S(1)}, u32[]{:S(2)}, u32[]{:S(2)}) collective-permute-start(bf16[1152,256]{1,0:T(8,128)(2,1)} %get-tuple-element.131), channel_id=1, source_target_pairs={{0,1},{1,0},{2,3},{3,2},{4,5},{5,4},{6,7},{7,6},{8,9},{9,8},{10,11... | collective-permute-start | bytes 1769480 | tf_op jit(solution)/shard_map/ppermute | solution.py:81
  83.6 13.4 %collective-permute-start.10 = (bf16[1152,256]{1,0:T(8,128)(2,1)S(1)}, bf16[1152,256]{1,0:T(8,128)(2,1)S(1)}, u32[]{:S(2)}, u32[]{:S(2)}) collective-permute-start(bf16[1152,256]{1,0:T(8,128)(2,1)S(1)} %copy-done.12), channel_id=1, source_target_pairs={{0,2},{1,3},{2,0},{3,1},{4,6},{5,7},{6,4},{7,5},{8,10},{9,11},{10,... | collective-permute-start | bytes 1769480 | tf_op jit(solution)/shard_map/ppermute | solution.py:81
  84.7 26.9 %collective-permute-start.12 = (bf16[1152,256]{1,0:T(8,128)(2,1)S(1)}, bf16[1152,256]{1,0:T(8,128)(2,1)S(1)}, u32[]{:S(2)}, u32[]{:S(2)}) collective-permute-start(bf16[1152,256]{1,0:T(8,128)(2,1)S(1)} %copy-done.12), channel_id=1, source_target_pairs={{0,4},{1,5},{2,6},{3,7},{4,0},{5,1},{6,2},{7,3},{8,12},{9,13},{10,... | collective-permute-start | bytes 1769480 | tf_op jit(solution)/shard_map/ppermute | solution.py:81
  87.5 12.8 %collective-permute-start.18 = (bf16[1152,128]{1,0:T(8,128)(2,1)}, bf16[1152,128]{1,0:T(8,128)(2,1)S(1)}, u32[]{:S(2)}, u32[]{:S(2)}) collective-permute-start(bf16[1152,128]{1,0:T(8,128)(2,1)} %collective-permute-done.17), channel_id=1, source_target_pairs={{0,1},{1,0},{2,3},{3,2},{4,5},{5,4},{6,7},{7,6},{8,9},{9,8},{10,11... | collective-permute-start | bytes 884744 | tf_op jit(solution)/shard_map/ppermute | solution.py:81
  97.1 17.2 %collective-permute-start.14 = (bf16[1152,256]{1,0:T(8,128)(2,1)S(1)}, bf16[1152,256]{1,0:T(8,128)(2,1)S(1)}, u32[]{:S(2)}, u32[]{:S(2)}) collective-permute-start(bf16[1152,256]{1,0:T(8,128)(2,1)S(1)} %copy-done.12), channel_id=1, source_target_pairs={{0,6},{1,7},{2,4},{3,5},{4,2},{5,3},{6,0},{7,1},{8,14},{9,15},{10,... | collective-permute-start | bytes 1769480 | tf_op jit(solution)/shard_map/ppermute | solution.py:81
  99.8 12.9 %collective-permute-start.2 = (bf16[1152,384]{1,0:T(8,128)(2,1)S(1)}, bf16[1152,384]{1,0:T(8,128)(2,1)S(1)}, u32[]{:S(2)}, u32[]{:S(2)}) collective-permute-start(bf16[1152,384]{1,0:T(8,128)(2,1)S(1)} %get-tuple-element.138), channel_id=1, source_target_pairs={{0,1},{1,0},{2,3},{3,2},{4,5},{5,4},{6,7},{7,6},{8,9},{9,8},{10,11... | collective-permute-start | bytes 2654216 | tf_op jit(solution)/shard_map/ppermute | solution.py:81
  99.8 2.9 collective-permute-start.20
  100.3 3.0 collective-permute-start.22
  102.8 29.6 %collective-permute-start.3 = (bf16[1152,384]{1,0:T(8,128)(2,1)S(1)}, bf16[1152,384]{1,0:T(8,128)(2,1)S(1)}, u32[]{:S(2)}, u32[]{:S(2)}) collective-permute-start(bf16[1152,384]{1,0:T(8,128)(2,1)S(1)} %get-tuple-element.138), channel_id=1, source_target_pairs={{0,2},{1,3},{2,0},{3,1},{4,6},{5,7},{6,4},{7,5},{8,10},{9,11},{10,... | collective-permute-start | bytes 2654216 | tf_op jit(solution)/shard_map/ppermute | solution.py:81
  103.3 47.0 %collective-permute-start.5 = (bf16[1152,384]{1,0:T(8,128)(2,1)S(1)}, bf16[1152,384]{1,0:T(8,128)(2,1)S(1)}, u32[]{:S(2)}, u32[]{:S(2)}) collective-permute-start(bf16[1152,384]{1,0:T(8,128)(2,1)S(1)} %get-tuple-element.138), channel_id=1, source_target_pairs={{0,4},{1,5},{2,6},{3,7},{4,0},{5,1},{6,2},{7,3},{8,12},{9,13},{10,... | collective-permute-start | bytes 2654216 | tf_op jit(solution)/shard_map/ppermute | solution.py:81
  111.6 38.7 %collective-permute-start.7 = (bf16[1152,384]{1,0:T(8,128)(2,1)S(1)}, bf16[1152,384]{1,0:T(8,128)(2,1)S(1)}, u32[]{:S(2)}, u32[]{:S(2)}) collective-permute-start(bf16[1152,384]{1,0:T(8,128)(2,1)S(1)} %get-tuple-element.138), channel_id=1, source_target_pairs={{0,6},{1,7},{2,4},{3,5},{4,2},{5,3},{6,0},{7,1},{8,14},{9,15},{10,... | collective-permute-start | bytes 2654216 | tf_op jit(solution)/shard_map/ppermute | solution.py:81
  112.7 38.1 %collective-permute-start.11 = (bf16[1152,256]{1,0:T(8,128)(2,1)S(1)}, bf16[1152,256]{1,0:T(8,128)(2,1)S(1)}, u32[]{:S(2)}, u32[]{:S(2)}) collective-permute-start(bf16[1152,256]{1,0:T(8,128)(2,1)S(1)} %collective-permute-done.10), channel_id=1, source_target_pairs={{0,1},{1,0},{2,3},{3,2},{4,5},{5,4},{6,7},{7,6},{8,9},{9,8},{10,11... | collective-permute-start | bytes 1769480 | tf_op jit(solution)/shard_map/ppermute | solution.py:81
  112.9 40.6 %copy-start.11 = (bf16[1152,1024]{1,0:T(8,128)(2,1)}, bf16[1152,1024]{1,0:T(8,128)(2,1)S(1)}, u32[]{:S(2)}) copy-start(bf16[1152,1024]{1,0:T(8,128)(2,1)S(1)} %constant_dynamic-update-slice_fusion) | copy-start | bytes 7077892
  114.3 38.4 %collective-permute-start.13 = (bf16[1152,256]{1,0:T(8,128)(2,1)S(1)}, bf16[1152,256]{1,0:T(8,128)(2,1)S(1)}, u32[]{:S(2)}, u32[]{:S(2)}) collective-permute-start(bf16[1152,256]{1,0:T(8,128)(2,1)S(1)} %collective-permute-done.12), channel_id=1, source_target_pairs={{0,1},{1,0},{2,3},{3,2},{4,5},{5,4},{6,7},{7,6},{8,9},{9,8},{10,11... | collective-permute-start | bytes 1769480 | tf_op jit(solution)/shard_map/ppermute | solution.py:81
  132.4 22.1 %collective-permute-start.15 = (bf16[1152,256]{1,0:T(8,128)(2,1)S(1)}, bf16[1152,256]{1,0:T(8,128)(2,1)S(1)}, u32[]{:S(2)}, u32[]{:S(2)}) collective-permute-start(bf16[1152,256]{1,0:T(8,128)(2,1)S(1)} %collective-permute-done.14), channel_id=1, source_target_pairs={{0,1},{1,0},{2,3},{3,2},{4,5},{5,4},{6,7},{7,6},{8,9},{9,8},{10,11... | collective-permute-start | bytes 1769480 | tf_op jit(solution)/shard_map/ppermute | solution.py:81
  150.3 5.1 %collective-permute-start.4 = (bf16[1152,384]{1,0:T(8,128)(2,1)S(1)}, bf16[1152,384]{1,0:T(8,128)(2,1)S(1)}, u32[]{:S(2)}, u32[]{:S(2)}) collective-permute-start(bf16[1152,384]{1,0:T(8,128)(2,1)S(1)} %collective-permute-done.3), channel_id=1, source_target_pairs={{0,1},{1,0},{2,3},{3,2},{4,5},{5,4},{6,7},{7,6},{8,9},{9,8},{10,11... | collective-permute-start | bytes 2654216 | tf_op jit(solution)/shard_map/ppermute | solution.py:81
  150.3 7.2 %collective-permute-start.6 = (bf16[1152,384]{1,0:T(8,128)(2,1)S(1)}, bf16[1152,384]{1,0:T(8,128)(2,1)S(1)}, u32[]{:S(2)}, u32[]{:S(2)}) collective-permute-start(bf16[1152,384]{1,0:T(8,128)(2,1)S(1)} %collective-permute-done.5), channel_id=1, source_target_pairs={{0,1},{1,0},{2,3},{3,2},{4,5},{5,4},{6,7},{7,6},{8,9},{9,8},{10,11... | collective-permute-start | bytes 2654216 | tf_op jit(solution)/shard_map/ppermute | solution.py:81
  150.8 8.8 %collective-permute-start.8 = (bf16[1152,384]{1,0:T(8,128)(2,1)S(1)}, bf16[1152,384]{1,0:T(8,128)(2,1)S(1)}, u32[]{:S(2)}, u32[]{:S(2)}) collective-permute-start(bf16[1152,384]{1,0:T(8,128)(2,1)S(1)} %collective-permute-done.7), channel_id=1, source_target_pairs={{0,1},{1,0},{2,3},{3,2},{4,5},{5,4},{6,7},{7,6},{8,9},{9,8},{10,11... | collective-permute-start | bytes 2654216 | tf_op jit(solution)/shard_map/ppermute | solution.py:81
  156.4 22.7 %copy-start.14 = (f32[3072]{0:T(1024)S(1)}, f32[3072]{0:T(1024)}, u32[]{:S(2)}) copy-start(f32[3072]{0:T(1024)} %param.14) | copy-start | bytes 36868
  156.4 22.7 %copy-start.15 = (f32[3072]{0:T(1024)S(1)}, f32[3072]{0:T(1024)}, u32[]{:S(2)}) copy-start(f32[3072]{0:T(1024)} %param.13) | copy-start | bytes 36868
  300.1 4.3 collective-permute-start.23
  302.6 2.9 collective-permute-start.24
  304.3 3.4 collective-permute-start.25
  308.8 15.5 %collective-permute-start.26 = (bf16[1152,256]{1,0:T(8,128)(2,1)S(1)}, bf16[1152,256]{1,0:T(8,128)(2,1)S(1)}, u32[]{:S(2)}, u32[]{:S(2)}) collective-permute-start(bf16[1152,256]{1,0:T(8,128)(2,1)S(1)} %convolution_convert_fusion.4), channel_id=1, source_target_pairs={{0,1},{1,0},{2,3},{3,2},{4,5},{5,4},{6,7},{7,6},{8,9},{9,8},{10,11... | collective-permute-start | bytes 1769480 | tf_op jit(solution)/shard_map/ppermute | solution.py:81
  309.4 16.2 %collective-permute-start.29 = (bf16[1152,256]{1,0:T(8,128)(2,1)S(1)}, bf16[1152,256]{1,0:T(8,128)(2,1)S(1)}, u32[]{:S(2)}, u32[]{:S(2)}) collective-permute-start(bf16[1152,256]{1,0:T(8,128)(2,1)S(1)} %add_convert_fusion.4), channel_id=1, source_target_pairs={{0,2},{1,3},{2,0},{3,1},{4,6},{5,7},{6,4},{7,5},{8,10},{9,11},{10,... | collective-permute-start | bytes 1769480 | tf_op jit(solution)/shard_map/ppermute | solution.py:81
  310.9 27.7 %collective-permute-start.28 = (bf16[1152,256]{1,0:T(8,128)(2,1)S(1)}, bf16[1152,256]{1,0:T(8,128)(2,1)S(1)}, u32[]{:S(2)}, u32[]{:S(2)}) collective-permute-start(bf16[1152,256]{1,0:T(8,128)(2,1)S(1)} %add_convert_fusion.5), channel_id=1, source_target_pairs={{0,4},{1,5},{2,6},{3,7},{4,0},{5,1},{6,2},{7,3},{8,12},{9,13},{10,... | collective-permute-start | bytes 1769480 | tf_op jit(solution)/shard_map/ppermute | solution.py:81
  312.3 26.2 %collective-permute-start.27 = (bf16[1152,256]{1,0:T(8,128)(2,1)S(1)}, bf16[1152,256]{1,0:T(8,128)(2,1)S(1)}, u32[]{:S(2)}, u32[]{:S(2)}) collective-permute-start(bf16[1152,256]{1,0:T(8,128)(2,1)S(1)} %add_convert_fusion.6), channel_id=1, source_target_pairs={{0,6},{1,7},{2,4},{3,5},{4,2},{5,3},{6,0},{7,1},{8,14},{9,15},{10,... | collective-permute-start | bytes 1769480 | tf_op jit(solution)/shard_map/ppermute | solution.py:81
  374.5 6.1 %collective-permute-start.30 = (bf16[1152,384]{1,0:T(8,128)(2,1)S(1)}, bf16[1152,384]{1,0:T(8,128)(2,1)S(1)}, u32[]{:S(2)}, u32[]{:S(2)}) collective-permute-start(bf16[1152,384]{1,0:T(8,128)(2,1)S(1)} %convolution_convert_fusion.3), channel_id=1, source_target_pairs={{0,1},{1,0},{2,3},{3,2},{4,5},{5,4},{6,7},{7,6},{8,9},{9,8},{10,11... | collective-permute-start | bytes 2654216 | tf_op jit(solution)/shard_map/ppermute | solution.py:81
  377.9 4.7 collective-permute-start.32
  380.5 7.0 %collective-permute-start.34 = (bf16[1152,384]{1,0:T(8,128)(2,1)S(1)}, bf16[1152,384]{1,0:T(8,128)(2,1)S(1)}, u32[]{:S(2)}, u32[]{:S(2)}) collective-permute-start(bf16[1152,384]{1,0:T(8,128)(2,1)S(1)} %convolution_convert_fusion.1), channel_id=1, source_target_pairs={{0,1},{1,0},{2,3},{3,2},{4,5},{5,4},{6,7},{7,6},{8,9},{9,8},{10,11... | collective-permute-start | bytes 2654216 | tf_op jit(solution)/shard_map/ppermute | solution.py:81
  386.9 5.5 %collective-permute-start.35 = (bf16[1152,384]{1,0:T(8,128)(2,1)S(1)}, bf16[1152,384]{1,0:T(8,128)(2,1)S(1)}, u32[]{:S(2)}, u32[]{:S(2)}) collective-permute-start(bf16[1152,384]{1,0:T(8,128)(2,1)S(1)} %convolution_convert_fusion), channel_id=1, source_target_pairs={{0,1},{1,0},{2,3},{3,2},{4,5},{5,4},{6,7},{7,6},{8,9},{9,8},{10,11... | collective-permute-start | bytes 2654216 | tf_op jit(solution)/shard_map/ppermute | solution.py:81
  389.5 40.7 %collective-permute-start.33 = (bf16[1152,384]{1,0:T(8,128)(2,1)S(1)}, bf16[1152,384]{1,0:T(8,128)(2,1)S(1)}, u32[]{:S(2)}, u32[]{:S(2)}) collective-permute-start(bf16[1152,384]{1,0:T(8,128)(2,1)S(1)} %add_convert_fusion.1), channel_id=1, source_target_pairs={{0,4},{1,5},{2,6},{3,7},{4,0},{5,1},{6,2},{7,3},{8,12},{9,13},{10,... | collective-permute-start | bytes 2654216 | tf_op jit(solution)/shard_map/ppermute | solution.py:81
  391.0 39.1 %collective-permute-start.31 = (bf16[1152,384]{1,0:T(8,128)(2,1)S(1)}, bf16[1152,384]{1,0:T(8,128)(2,1)S(1)}, u32[]{:S(2)}, u32[]{:S(2)}) collective-permute-start(bf16[1152,384]{1,0:T(8,128)(2,1)S(1)} %add_convert_fusion.2), channel_id=1, source_target_pairs={{0,6},{1,7},{2,4},{3,5},{4,2},{5,3},{6,0},{7,1},{8,14},{9,15},{10,... | collective-permute-start | bytes 2654216 | tf_op jit(solution)/shard_map/ppermute | solution.py:81
  394.5 37.2 %copy-start.6 = (bf16[1152,1536]{1,0:T(8,128)(2,1)S(1)}, bf16[1152,1536]{1,0:T(8,128)(2,1)}, u32[]{:S(2)}) copy-start(bf16[1152,1536]{1,0:T(8,128)(2,1)} %get-tuple-element.104) | copy-start | bytes 10616836
  394.6 37.2 %copy-start.13 = (bf16[1536,1024]{1,0:T(8,128)(2,1)S(1)}, bf16[1536,1024]{1,0:T(8,128)(2,1)}, u32[]{:S(2)}) copy-start(bf16[1536,1024]{1,0:T(8,128)(2,1)} %all-gather.4.cloned.1.call-done) | copy-start | bytes 9437188
  396.2 34.0 %collective-permute-start.44 = (f32[2,1152]{1,0:T(2,128)S(1)}, f32[2,1152]{1,0:T(2,128)S(1)}, u32[]{:S(2)}, u32[]{:S(2)}) collective-permute-start(f32[2,1152]{1,0:T(2,128)S(1)} %pad_maximum_fusion), channel_id=1, source_target_pairs={{0,1},{1,0},{2,3},{3,2},{4,5},{5,4},{6,7},{7,6},{8,9},{9,8},{10,11... | collective-permute-start | bytes 27656 | tf_op jit(solution)/shard_map/ppermute | solution.py:81
  396.3 41.4 %collective-permute-start.43 = (bf16[1152,384]{1,0:T(8,128)(2,1)S(1)}, bf16[1152,384]{1,0:T(8,128)(2,1)S(1)}, u32[]{:S(2)}, u32[]{:S(2)}) collective-permute-start(bf16[1152,384]{1,0:T(8,128)(2,1)S(1)} %add_convert_fusion), channel_id=1, source_target_pairs={{0,2},{1,3},{2,0},{3,1},{4,6},{5,7},{6,4},{7,5},{8,10},{9,11},{10,... | collective-permute-start | bytes 2654216 | tf_op jit(solution)/shard_map/ppermute | solution.py:81
  430.2 3.7 collective-permute-start.45
  433.9 3.7 collective-permute-start.46
  436.6 20.2 %collective-permute-start.36 = (bf16[1152,128]{1,0:T(8,128)(2,1)S(1)}, bf16[1152,128]{1,0:T(8,128)(2,1)S(1)}, u32[]{:S(2)}, u32[]{:S(2)}) collective-permute-start(bf16[1152,128]{1,0:T(8,128)(2,1)S(1)} %convolution_convert_fusion.11), channel_id=1, source_target_pairs={{0,1},{1,0},{2,3},{3,2},{4,5},{5,4},{6,7},{7,6},{8,9},{9,8},{10,11... | collective-permute-start | bytes 884744 | tf_op jit(solution)/shard_map/ppermute | solution.py:81
  438.9 4.3 collective-permute-start.47
  440.2 6.6 %collective-permute-start.48 = (bf16[3,48,384]{2,1,0:T(8,128)(2,1)S(1)}, bf16[3,48,384]{2,1,0:T(8,128)(2,1)S(1)}, u32[]{:S(2)}, u32[]{:S(2)}) collective-permute-start(bf16[3,48,384]{2,1,0:T(8,128)(2,1)S(1)} %bitcast.66), channel_id=1, source_target_pairs={{8,0},{24,16},{9,1},{25,17},{10,2},{26,18},{11,3},{27,19},{12,4},{... | collective-permute-start | bytes 331784 | tf_op jit(solution)/shard_map/ppermute | solution.py:76
  442.7 15.3 %collective-permute-start.37 = (bf16[1152,128]{1,0:T(8,128)(2,1)S(1)}, bf16[1152,128]{1,0:T(8,128)(2,1)S(1)}, u32[]{:S(2)}, u32[]{:S(2)}) collective-permute-start(bf16[1152,128]{1,0:T(8,128)(2,1)S(1)} %convolution_convert_fusion.10), channel_id=1, source_target_pairs={{0,1},{1,0},{2,3},{3,2},{4,5},{5,4},{6,7},{7,6},{8,9},{9,8},{10,11... | collective-permute-start | bytes 884744 | tf_op jit(solution)/shard_map/ppermute | solution.py:81
  442.7 17.5 %collective-permute-start.38 = (bf16[1152,128]{1,0:T(8,128)(2,1)S(1)}, bf16[1152,128]{1,0:T(8,128)(2,1)S(1)}, u32[]{:S(2)}, u32[]{:S(2)}) collective-permute-start(bf16[1152,128]{1,0:T(8,128)(2,1)S(1)} %convolution_convert_fusion.9), channel_id=1, source_target_pairs={{0,1},{1,0},{2,3},{3,2},{4,5},{5,4},{6,7},{7,6},{8,9},{9,8},{10,11... | collective-permute-start | bytes 884744 | tf_op jit(solution)/shard_map/ppermute | solution.py:81
  460.1 4.8 collective-permute-start.39
  461.3 17.1 %copy-start.4 = (f32[1152,256]{1,0:T(8,128)S(1)}, f32[1152,256]{1,0:T(8,128)}, u32[]{:S(2)}) copy-start(f32[1152,256]{1,0:T(8,128)} %convert_add_fusion.1) | copy-start | bytes 3538948
  461.3 17.1 %copy-start.18 = (f32[384]{0:T(512)S(1)}, f32[384]{0:T(512)}, u32[]{:S(2)}) copy-start(f32[384]{0:T(512)} %param.19) | copy-start | bytes 4612
  461.4 17.1 %copy-start.20 = (f32[384]{0:T(512)S(1)}, f32[384]{0:T(512)}, u32[]{:S(2)}) copy-start(f32[384]{0:T(512)} %param.18) | copy-start | bytes 4612
  461.4 9.9 %collective-permute-start.42 = (bf16[1152,128]{1,0:T(8,128)(2,1)S(1)}, bf16[1152,128]{1,0:T(8,128)(2,1)S(1)}, u32[]{:S(2)}, u32[]{:S(2)}) collective-permute-start(bf16[1152,128]{1,0:T(8,128)(2,1)S(1)} %add_convert_fusion.7), channel_id=1, source_target_pairs={{0,2},{1,3},{2,0},{3,1},{4,6},{5,7},{6,4},{7,5},{8,10},{9,11},{10,... | collective-permute-start | bytes 884744 | tf_op jit(solution)/shard_map/ppermute | solution.py:81
  462.9 15.4 %collective-permute-start.41 = (bf16[1152,128]{1,0:T(8,128)(2,1)S(1)}, bf16[1152,128]{1,0:T(8,128)(2,1)S(1)}, u32[]{:S(2)}, u32[]{:S(2)}) collective-permute-start(bf16[1152,128]{1,0:T(8,128)(2,1)S(1)} %add_convert_fusion.8), channel_id=1, source_target_pairs={{0,4},{1,5},{2,6},{3,7},{4,0},{5,1},{6,2},{7,3},{8,12},{9,13},{10,... | collective-permute-start | bytes 884744 | tf_op jit(solution)/shard_map/ppermute | solution.py:81
  464.4 14.0 %collective-permute-start.40 = (bf16[1152,128]{1,0:T(8,128)(2,1)S(1)}, bf16[1152,128]{1,0:T(8,128)(2,1)S(1)}, u32[]{:S(2)}, u32[]{:S(2)}) collective-permute-start(bf16[1152,128]{1,0:T(8,128)(2,1)S(1)} %add_convert_fusion.9), channel_id=1, source_target_pairs={{0,6},{1,7},{2,4},{3,5},{4,2},{5,3},{6,0},{7,1},{8,14},{9,15},{10,... | collective-permute-start | bytes 884744 | tf_op jit(solution)/shard_map/ppermute | solution.py:81
  (18 other events, 89.2 us)
Sparse Core Ops, SparseCore 0:
  9.6 169.5 all-gather.5
  180.7 115.8 all-gather.7
  298.8 61.5 all-gather.3
